TPU v7x, 128 devices: a whole 4x4x4 slice. The times are simulated.
128 devices in a mesh: dp: 32 (over x, z, core), mp: 4 (over y).
Axes of the slice: x: 4, y: 4, z: 4, core: 2. Of those that a mesh axis runs over, the one named last changes fastest.
Arguments:
- attn_out: bfloat16 [32768, 3072], P('dp', 'mp'), may hold values from -80 to 80
- cotangent: bfloat16 [32768, 6144], P('dp'), may hold values from -60 to 60
- master_weight: float32 [3072, 6144], P(('mp', 'dp')), may hold values from -0.1 to 0.1
- moment_weight: float32 [3072, 6144], P(('mp', 'dp')), may hold values from -0.1 to 0.1
- second_weight: float32 [3072, 6144], P(('mp', 'dp')), may hold values from 0.01 to 1
- teacher_weight: float32 [3072, 6144], P(('mp', 'dp')), may hold values from -0.1 to 0.1
- master_bias: float32 [6144], P('dp'), may hold values from -0.1 to 0.1
- moment_bias: float32 [6144], P('dp'), may hold values from -0.1 to 0.1
- second_bias: float32 [6144], P('dp'), may hold values from 0.01 to 1
- teacher_bias: float32 [6144], P('dp'), may hold values from -0.1 to 0.1
Outputs:
- new_master_weight: float32 [3072, 6144], P(('mp', 'dp'))
- new_moment_weight: float32 [3072, 6144], P(('mp', 'dp'))
- new_second_weight: float32 [3072, 6144], P(('mp', 'dp'))
- new_teacher_weight: float32 [3072, 6144], P(('mp', 'dp'))
- new_master_bias: float32 [6144], P('dp')
- new_moment_bias: float32 [6144], P('dp')
- new_second_bias: float32 [6144], P('dp')
- new_teacher_bias: float32 [6144], P('dp')
- teacher_weight_full: bfloat16 [3072, 6144], P('mp')
- teacher_bias_full: bfloat16 [6144], replicated
All inputs are finite; a program needn't handle non-finite values.
Results may differ from a plain program's by a relative error of at most 0.00045.
Values may be sent and summed in bfloat16 or wider, within the bound.
No kernel may reach another device: no remote copies, remote signals or barrier semaphores. Data moves between devices by JAX's collectives and lax.ppermute only.
A program may use at most 128 MiB of HBM per device.

v0:
```python
import jax
import jax.numpy as jnp
from jax import lax
from jax.sharding import PartitionSpec as P

beta_one = 0.9
beta_two = 0.95
adam_eps = 1e-08
learn_rate = 0.1
decay_rate = 0.05
ema_keep = 0.9


def adamw_update(gradient, master, moment, second, teacher, clip_factor, decay):
    clipped = clip_factor * gradient
    new_moment = beta_one * moment + (1.0 - beta_one) * clipped
    new_second = beta_two * second + (1.0 - beta_two) * clipped * clipped
    new_master = master - learn_rate * (
        new_moment / (jnp.sqrt(new_second) + adam_eps) + decay * master
    )
    new_teacher = ema_keep * teacher + (1.0 - ema_keep) * new_master
    return (new_master, new_moment, new_second, new_teacher)


def transposed_product(left, right):
    return lax.dot_general(
        left, right, (((0,), (0,)), ((), ())), preferred_element_type=jnp.float32
    )


def per_device(
    attn_out,
    cotangent,
    master_weight,
    moment_weight,
    second_weight,
    teacher_weight,
    master_bias,
    moment_bias,
    second_bias,
    teacher_bias,
):
    grad_term = transposed_product(attn_out, cotangent)
    weight_grad = lax.psum_scatter(grad_term, "dp", scatter_dimension=0, tiled=True)
    bias_term = jnp.sum(cotangent, axis=0, dtype=jnp.float32)
    bias_grad = lax.psum_scatter(bias_term, "dp", scatter_dimension=0, tiled=True)
    weight_squares = jnp.sum(weight_grad * weight_grad)
    bias_squares = jnp.sum(bias_grad * bias_grad)
    sq_norm = lax.psum(weight_squares, ("dp", "mp")) + lax.psum(bias_squares, "dp")
    total_count = weight_grad.shape[1] * (
        master_weight.shape[0] * lax.axis_size("dp") * lax.axis_size("mp") + 1
    )
    clip_factor = jnp.minimum(1.0, jnp.sqrt(jnp.float32(total_count)) / jnp.sqrt(sq_norm + 1e-06))
    master_w, moment_w, second_w, teacher_w = adamw_update(
        weight_grad,
        master_weight,
        moment_weight,
        second_weight,
        teacher_weight,
        clip_factor,
        decay_rate,
    )
    master_b, moment_b, second_b, teacher_b = adamw_update(
        bias_grad, master_bias, moment_bias, second_bias, teacher_bias, clip_factor, 0.0
    )
    full_weight, full_bias = (
        lax.all_gather(teacher_w.astype(jnp.bfloat16), "dp", axis=0, tiled=True),
        lax.all_gather(teacher_b.astype(jnp.bfloat16), "dp", axis=0, tiled=True),
    )
    return (
        master_w,
        moment_w,
        second_w,
        teacher_w,
        master_b,
        moment_b,
        second_b,
        teacher_b,
        full_weight,
        full_bias,
    )


def solution(mesh):
    placed = (
        P("dp", "mp"),
        P("dp", None),
        P(("mp", "dp"), None),
        P(("mp", "dp"), None),
        P(("mp", "dp"), None),
        P(("mp", "dp"), None),
        P("dp"),
        P("dp"),
        P("dp"),
        P("dp"),
    )
    return jax.shard_map(
        per_device,
        mesh=mesh,
        in_specs=placed,
        out_specs=(
            P(("mp", "dp"), None),
            P(("mp", "dp"), None),
            P(("mp", "dp"), None),
            P(("mp", "dp"), None),
            P("dp"),
            P("dp"),
            P("dp"),
            P("dp"),
            P("mp", None),
            P(),
        ),
        check_vma=False,
    )
```

profile of v0, /device:TPU:1, one launch (start us, length us, event | category | flops | bytes accessed | tf_op | source)
XLA Modules:
  0.0 439.0 jit_solution(12488702411490336077)
XLA Ops:
  7.2 0.0 copy-start
  7.2 0.0 reduce-scatter.2.cloned.1.call-start
  7.2 1.4 copy-done
  8.6 16.6 %fusion.7 = f32[768,6144]{1,0:T(8,128)} fusion(bf16[1024,768]{1,0:T(8,128)(2,1)S(1)} %copy-done, bf16[1024,6144]{1,0:T(8,128)(2,1)} %param.11), kind=kOutput, calls=%fused_computation.16 | convolution fusion | flops 9663676416 | bytes 33030144 | tf_op jit(solution)/shard_map/dot_general | solution.py:26
  25.2 0.0 copy-start.4
  25.2 0.0 copy-start.1
  25.2 0.0 copy-start.2
  25.2 0.0 copy-start.3
  25.2 0.0 reduce-scatter.2.cloned.1.call-update
  25.2 0.0 copy-start.5
  25.2 0.0 copy-start.6
  25.3 0.0 copy-start.7
  25.3 0.0 copy-start.8
  25.3 0.0 all-gather.2.cloned.1.call-start
  25.3 0.5 copy-done.4
  25.8 0.6 fusion.6
  27.1 6.4 %convert_reduce_fusion = f32[6144]{0:T(1024)S(1)} fusion(bf16[1024,6144]{1,0:T(8,128)(2,1)} %param.11), kind=kLoop, calls=%fused_computation | loop fusion | flops 12576768 | bytes 12607488 | tf_op jit(solution)/shard_map/reduce_sum | solution.py:45
  33.5 127.2 %all-reduce.1 = f32[6144]{0:T(1024)S(1)} all-reduce(f32[6144]{0:T(1024)S(1)} %convert_reduce_fusion), channel_id=3, replica_groups=mesh['dp'=32,'mp'=4] {'dp'}, use_global_device_ids=true, to_apply=%region_4.0.clone | all-reduce | flops 6144 | bytes 49152
  160.6 0.7 multiply_reduce_fusion.1
  161.3 0.0 reduce-scatter.2.cloned.1.call-done
  161.3 1.8 multiply_reduce_fusion
  163.1 68.3 %psum.15 = f32[]{:T(128)} all-reduce(f32[]{:T(128)} %multiply_reduce_fusion.1), channel_id=1, replica_groups=mesh['dp'=32,'mp'=4] {'dp'}, use_global_device_ids=true, to_apply=%region_6.0 | all-reduce | flops 1 | bytes 8 | tf_op jit(solution)/shard_map/psum | solution.py:49
  231.4 64.6 %psum.14 = f32[]{:T(128)} all-reduce(f32[]{:T(128)} %multiply_reduce_fusion), channel_id=1, replica_groups=mesh['dp'=32,'mp'=4] {'dp','mp'}, use_global_device_ids=true, to_apply=%region_2.0 | all-reduce | flops 1 | bytes 8 | tf_op jit(solution)/shard_map/psum | solution.py:49
  297.3 0.0 copy-done.1
  297.3 0.0 copy-done.2
  297.3 0.0 copy-done.3
  297.3 3.0 fusion.4
  300.3 0.0 all-gather.2.cloned.1.call-update
  301.0 0.0 copy-done.5
  301.0 0.0 copy-done.6
  301.0 0.0 copy-done.7
  301.1 0.0 copy-done.8
  301.1 0.7 fusion.2
  301.7 0.2 dynamic-update-slice
  302.0 121.6 %all-reduce = bf16[6144]{0:T(1024)(128)(2,1)} all-reduce(bf16[6144]{0:T(1024)(128)(2,1)S(1)} %dynamic-update-slice), channel_id=1, replica_groups=mesh['dp'=32,'mp'=4] {'dp'}, use_global_device_ids=true, to_apply=%add | all-reduce | flops 6144 | bytes 24576
  423.5 0.0 all-gather.2.cloned.1.call-done
  423.5 8.6 %copy.22 = bf16[768,6144]{1,0:T(8,128)(2,1)} copy(bf16[768,6144]{1,0:T(8,128)(2,1)} %all-gather.2.cloned.1.call-done) | data formatting | bytes 18874368
  (1 shorter events, 0.0 us)
Async XLA Ops:
  7.2 1.4 copy-start
  7.2 154.1 %reduce-scatter.2.cloned.1.call-start = ((), (), s32[]{:S(2)}) async-start(), calls=%async_computation.1 | async-start | bytes 19464192 | tf_op jit(solution)/shard_map/reduce_scatter | solution.py:44
  25.2 0.7 copy-start.4
  25.2 272.1 %copy-start.1 = (f32[24,6144]{1,0:T(8,128)S(1)}, f32[24,6144]{1,0:T(8,128)}, u32[]{:S(2)}) copy-start(f32[24,6144]{1,0:T(8,128)} %param.15) | copy-start | bytes 1769476
  25.2 272.1 %copy-start.2 = (f32[24,6144]{1,0:T(8,128)S(1)}, f32[24,6144]{1,0:T(8,128)}, u32[]{:S(2)}) copy-start(f32[24,6144]{1,0:T(8,128)} %param.12) | copy-start | bytes 1769476
  25.2 272.1 %copy-start.3 = (f32[24,6144]{1,0:T(8,128)S(1)}, f32[24,6144]{1,0:T(8,128)}, u32[]{:S(2)}) copy-start(f32[24,6144]{1,0:T(8,128)} %param.14) | copy-start | bytes 1769476
  25.2 275.8 %copy-start.5 = (f32[192]{0:T(256)S(1)}, f32[192]{0:T(256)}, u32[]{:S(2)}) copy-start(f32[192]{0:T(256)} %param.19) | copy-start | bytes 2308
  25.2 275.8 %copy-start.6 = (f32[192]{0:T(256)S(1)}, f32[192]{0:T(256)}, u32[]{:S(2)}) copy-start(f32[192]{0:T(256)} %param.16) | copy-start | bytes 2308
  25.3 275.8 %copy-start.7 = (f32[192]{0:T(256)S(1)}, f32[192]{0:T(256)}, u32[]{:S(2)}) copy-start(f32[192]{0:T(256)} %param.18) | copy-start | bytes 2308
  25.3 275.8 %copy-start.8 = (f32[192]{0:T(256)S(1)}, f32[192]{0:T(256)}, u32[]{:S(2)}) copy-start(f32[192]{0:T(256)} %param.17) | copy-start | bytes 2308
  25.3 398.3 %all-gather.2.cloned.1.call-start = ((), (), s32[]{:S(2)}) async-start(), calls=%async_computation.2 | async-start | bytes 9732096 | tf_op jit(solution)/shard_map/all_gather | solution.py:67
Sparse Core Ops, SparseCore 0:
  25.4 124.4 reduce-scatter.1
  300.5 52.7 all-gather.1
where the time goes:
time: 444 us; the launch traced here: 439 us
  blocking collectives  382 us (86%)
  between operations  16.8 us (4%)
  matrix products  16.6 us (4%)
  other arithmetic  12.6 us (3%)
  local copies, waits for them, and re-layouts  11.3 us (3%)
    unnamed x2, blocking collectives  249 us
    psum x1, blocking collectives, per_device(): lax.psum(bias_squares, 'dp')  68.3 us
    psum x1, blocking collectives, per_device(): lax.psum(weight_squares, ('dp', 'mp')) + lax.psum(bias_squares, 'dp')  64.6 us
    dot_general x1, matrix products, transposed_product(): lax.dot_general(left, right, (((0,), (0,)), ((), ())), preferred_element_...  16.6 us
    unnamed x22, local copies, waits for them, and re-layouts  11.3 us
  transfers between devices with their start and end apart: 2, of which 0 were waited for; matrix products, arithmetic and copies ran while one was open for 2% of the time, Pallas kernels for 0%

commit v1 on v0

--- a/solution.py
+++ b/solution.py
@@ -9,6 +9,7 @@
 learn_rate = 0.1
 decay_rate = 0.05
 ema_keep = 0.9
+X, Z, C, Y = 4, 4, 2, 4
 
 
 def adamw_update(gradient, master, moment, second, teacher, clip_factor, decay):
@@ -28,6 +29,72 @@
     )
 
 
+def place(x, z, c):
+    return (x % X) * (Z * C) + (z % Z) * C + c % C
+
+
+def shift(array, dx=0, dz=0, dc=0):
+    pairs = [
+        (place(x, z, c), place(x + dx, z + dz, c + dc))
+        for x in range(X)
+        for z in range(Z)
+        for c in range(C)
+    ]
+    return lax.ppermute(array, "dp", pairs)
+
+
+def shift_y(array, dy):
+    return lax.ppermute(array, "mp", [(y, (y + dy) % Y) for y in range(Y)])
+
+
+def along_x(array, d):
+    return shift(array, dx=d)
+
+
+def along_z(array, d):
+    return shift(array, dz=d)
+
+
+def all_sum(array, ways):
+    for way in ways:
+        if way == "core":
+            array = array + shift(array, dc=1)
+        else:
+            move = {"x": along_x, "z": along_z, "y": shift_y}[way]
+            array = array + move(array, 1) + move(array, 2) + move(array, 3)
+    return array
+
+
+def pick(array, axis, index):
+    return lax.dynamic_index_in_dim(array, index % array.shape[axis], axis, keepdims=False)
+
+
+def scatter_sum(blocks, axis, me, move):
+    total = pick(blocks, axis, me)
+    for d in (2, 1, 3):
+        total = total + move(pick(blocks, axis, me + d), d)
+    return total
+
+
+def reduce_x_first(product, x, z):
+    rows, cols = product.shape
+    blocks = product.reshape(X, Z, rows // (X * Z), cols)
+    part = scatter_sum(blocks, 0, x, along_x)
+    return scatter_sum(part, 0, z, along_z)
+
+
+def reduce_z_first(product, x, z):
+    rows, cols = product.shape
+    blocks = product.reshape(X, Z, rows // (X * Z), cols)
+    part = scatter_sum(blocks, 1, z, along_z)
+    return scatter_sum(part, 0, x, along_x)
+
+
+def squares(array):
+    rows, cols = array.shape
+    return jnp.sum((array * array).reshape(rows // 8, 8, cols // 128, 128), axis=(0, 2))
+
+
 def per_device(
     attn_out,
     cotangent,
@@ -40,16 +107,44 @@
     second_bias,
     teacher_bias,
 ):
-    grad_term = transposed_product(attn_out, cotangent)
-    weight_grad = lax.psum_scatter(grad_term, "dp", scatter_dimension=0, tiled=True)
+    index = lax.axis_index("dp")
+    x, z, c = index // (Z * C), (index // C) % Z, index % C
+    width = cotangent.shape[1]
+    half, quarter = width // 2, width // 4
+    tokens = cotangent.shape[0]
+    own_rows = master_weight.shape[0]
+
+    def columns(start):
+        return lax.dynamic_slice(cotangent, (0, start), (tokens, quarter))
+
+    attn_other = shift(attn_out, dc=1)
+    grads, sums = [], []
+    for which, reduce_in in ((0, reduce_x_first), (1, reduce_z_first)):
+        other = shift(columns((1 - c) * half + which * quarter), dc=1)
+        product = transposed_product(attn_out, columns(c * half + which * quarter))
+        product = product + transposed_product(attn_other, other)
+        grad = reduce_in(product, x, z)
+        grads.append(grad)
+        sums.append(squares(grad))
+    chip_grad = jnp.concatenate(grads, axis=1).reshape(C, own_rows, half)
+    own_half = pick(chip_grad, 0, c)
+    other_half = shift(pick(chip_grad, 0, 1 - c), dc=1)
+    first = jnp.where(c == 0, own_half, other_half)
+    last = jnp.where(c == 0, other_half, own_half)
+    weight_grad = jnp.concatenate([first, last], axis=1)
+
     bias_term = jnp.sum(cotangent, axis=0, dtype=jnp.float32)
-    bias_grad = lax.psum_scatter(bias_term, "dp", scatter_dimension=0, tiled=True)
-    weight_squares = jnp.sum(weight_grad * weight_grad)
-    bias_squares = jnp.sum(bias_grad * bias_grad)
-    sq_norm = lax.psum(weight_squares, ("dp", "mp")) + lax.psum(bias_squares, "dp")
-    total_count = weight_grad.shape[1] * (
-        master_weight.shape[0] * lax.axis_size("dp") * lax.axis_size("mp") + 1
+    state = jnp.stack([master_bias, moment_bias, second_bias, teacher_bias])
+    spread = lax.dynamic_update_slice(
+        jnp.zeros((4, width), jnp.float32), state, (0, index * master_bias.shape[0])
     )
+    packed = jnp.concatenate([bias_term.reshape(-1, 128), spread.reshape(-1, 128)], axis=0)
+    packed = all_sum(packed, ("core", "x", "z")).reshape(5, width)
+    bias_grad, bias_state = packed[0], packed[1:]
+
+    sq_norm = jnp.sum(all_sum(sums[0] + sums[1], ("core", "x", "z", "y")))
+    sq_norm = sq_norm + jnp.sum(bias_grad * bias_grad)
+    total_count = width * (own_rows * X * Z * C * Y + 1)
     clip_factor = jnp.minimum(1.0, jnp.sqrt(jnp.float32(total_count)) / jnp.sqrt(sq_norm + 1e-06))
     master_w, moment_w, second_w, teacher_w = adamw_update(
         weight_grad,
@@ -60,25 +155,12 @@
         clip_factor,
         decay_rate,
     )
-    master_b, moment_b, second_b, teacher_b = adamw_update(
-        bias_grad, master_bias, moment_bias, second_bias, teacher_bias, clip_factor, 0.0
-    )
-    full_weight, full_bias = (
-        lax.all_gather(teacher_w.astype(jnp.bfloat16), "dp", axis=0, tiled=True),
-        lax.all_gather(teacher_b.astype(jnp.bfloat16), "dp", axis=0, tiled=True),
-    )
-    return (
-        master_w,
-        moment_w,
-        second_w,
-        teacher_w,
-        master_b,
-        moment_b,
-        second_b,
-        teacher_b,
-        full_weight,
-        full_bias,
-    )
+    bias_new = adamw_update(bias_grad, *bias_state, clip_factor, 0.0)
+    count = master_bias.shape[0]
+    own_bias = [lax.dynamic_slice(b, (index * count,), (count,)) for b in bias_new]
+    full_bias = bias_new[3].astype(jnp.bfloat16)
+    full_weight = lax.all_gather(teacher_w.astype(jnp.bfloat16), "dp", axis=0, tiled=True)
+    return (master_w, moment_w, second_w, teacher_w, *own_bias, full_weight, full_bias)
 
 
 def solution(mesh):

time: 444 us -> 238 us (0.54); the launches traced: 439 us -> 238 us
  blocking collectives: 382 us -> 0 us
  waiting for transfers between devices: 0.04 us -> 113 us
  starting transfers between devices: 0.08 us -> 44.8 us
  local copies, waits for them, and re-layouts: 11.3 us -> 23.8 us
  matrix products: 16.6 us -> 23.6 us
    unnamed x2 -> x0, blocking collectives: 249 us -> none
    psum x2 -> x0, blocking collectives: 133 us -> none  [the longest x1 68.3 us: per_device(): lax.psum(bias_squares, 'dp')]
    ppermute x0 -> x33, waiting for transfers between devices: none -> 58.1 us  [the longest x30 55.7 us: shift(): return lax.ppermute(array, 'dp', pairs)]
    all_gather x1, waiting for transfers between devices: 0.01 us -> 54.8 us  [per_device(): lax.all_gather(teacher_w.astype(jnp.bfloat16), 'dp', axis=0, tiled=True)]
    ppermute x0 -> x33, starting transfers between devices: none -> 44.8 us  [the longest x30 41 us: shift(): return lax.ppermute(array, 'dp', pairs)]
    dynamic_slice x0 -> x5, local copies, waits for them, and re-layouts: none -> 7.48 us  [the longest x1 4.94 us: columns(): return lax.dynamic_slice(cotangent, (0, start), (tokens, quarter))]
    dot_general x1 -> x4, matrix products: 16.6 us -> 23.6 us  [transposed_product(): lax.dot_general(left, right, (((0,), (0,)), ((), ())), preferred_element_...]
    add x0 -> x9, other arithmetic: none -> 5.47 us  [the longest x2 4.41 us: scatter_sum(): total = total + move(pick(blocks, axis, me + d), d)]
  transfers between devices with their start and end apart: 2 -> 34, of which waited for: 0 -> 14; matrix products, arithmetic and copies ran while one was open for 2% -> 19% of each run, Pallas kernels for 0% -> 0%
where the time goes in v1:
time: 238 us
  waiting for transfers between devices  113 us (47%)
  starting transfers between devices  44.8 us (19%)
  local copies, waits for them, and re-layouts  23.8 us (10%)
  matrix products  23.6 us (10%)
  other arithmetic  16.9 us (7%)
  between operations  15.8 us (7%)
    ppermute x30, waiting for transfers between devices, shift(): return lax.ppermute(array, 'dp', pairs)  55.7 us
    all_gather x1, waiting for transfers between devices, per_device(): lax.all_gather(teacher_w.astype(jnp.bfloat16), 'dp', axis=0, tiled=True)  54.8 us
    ppermute x30, starting transfers between devices, shift(): return lax.ppermute(array, 'dp', pairs)  41 us
    dot_general x4, matrix products, transposed_product(): lax.dot_general(left, right, (((0,), (0,)), ((), ())), preferred_element_...  23.6 us
    unnamed x27, local copies, waits for them, and re-layouts  11.8 us
    reduce_sum x1, other arithmetic, per_device(): bias_term = jnp.sum(cotangent, axis=0, dtype=jnp.float32)  6.42 us
    dynamic_slice x1, local copies, waits for them, and re-layouts, columns(): return lax.dynamic_slice(cotangent, (0, start), (tokens, quarter))  4.94 us
  transfers between devices with their start and end apart: 34, of which 14 were waited for; matrix products, arithmetic and copies ran while one was open for 19% of the time, Pallas kernels for 0%

profile of v1, /device:TPU:1, one launch (start us, length us, event | category | flops | bytes accessed | tf_op | source)
XLA Modules:
  0.0 237.8 jit_solution(15882533086305783502)
XLA Ops:
  7.3 4.9 %constant_dynamic-slice_fusion.1 = (bf16[1024,1536]{1,0:T(8,128)(2,1)S(1)}, bf16[1024,1536]{1,0:T(8,128)(2,1)}) fusion(bf16[1024,6144]{1,0:T(8,128)(2,1)} %param.11, s32[]{:T(128)S(6)} %select_n.149, s32[]{:T(128)S(6)} %select_n.170), kind=kLoop, calls=%fused_computation.63 | loop fusion | bytes 12582920 | tf_op jit(solution)/shard_map/dynamic_slice | solution.py:118
  12.2 1.4 collective-permute-start.8
  14.6 6.4 %convert_reduce_fusion = f32[6144]{0:T(1024)S(1)} fusion(bf16[1024,6144]{1,0:T(8,128)(2,1)} %param.11), kind=kLoop, calls=%fused_computation | loop fusion | flops 12576768 | bytes 12607488 | tf_op jit(solution)/shard_map/reduce_sum | solution.py:136
  21.7 5.0 %fusion = f32[1536,768]{0,1:T(8,128)S(1)} fusion(bf16[1024,768]{1,0:T(8,128)(2,1)} %param.10, bf16[1024,6144]{1,0:T(8,128)(2,1)} %param.11, s32[]{:T(128)S(6)} %select_n.169), kind=kOutput, calls=%fused_computation.3 | convolution fusion | flops 2415919104 | bytes 9437188 | tf_op jit(solution)/shard_map/dot_general | solution.py:27
  26.7 5.0 %convolution_add_fusion = f32[1536,768]{0,1:T(8,128)S(1)} fusion(f32[1536,768]{0,1:T(8,128)S(1)} %fusion, bf16[1024,1536]{1,0:T(8,128)(2,1)} %collective-permute-done.8, bf16[1024,768]{1,0:T(8,128)(2,1)} %collective-permute-done.1), kind=kOutput, calls=%fused_computation.1 | convolution fusion | flops 2417098752 | bytes 14155776 | tf_op jit(solution)/shard_map/dot_general | solution.py:27
  31.7 2.0 dynamic-slice_bitcast_fusion.2
  33.7 1.3 copy-done
  35.0 3.7 %collective-permute-start.9 = (f32[4,48,1536]{2,1,0:T(8,128)}, f32[4,48,1536]{2,1,0:T(8,128)}, u32[]{:S(2)}, u32[]{:S(2)}) collective-permute-start(f32[4,48,1536]{2,1,0:T(8,128)} %get-tuple-element.29), channel_id=1, source_target_pairs={{0,16},{4,20},{8,24},{12,28},{16,0},{20,4},{24,8},{28,12},{32,48},... | collective-permute-start | bytes 3538952 | tf_op jit(solution)/shard_map/ppermute | solution.py:43
  38.7 7.2 %fusion.2 = f32[1536,768]{0,1:T(8,128)} fusion(bf16[1024,768]{1,0:T(8,128)(2,1)} %param.10, bf16[1024,6144]{1,0:T(8,128)(2,1)} %param.11, s32[]{:T(128)S(6)} %select_n.148), kind=kOutput, calls=%fused_computation.5 | convolution fusion | flops 2415919104 | bytes 9437188 | tf_op jit(solution)/shard_map/dot_general | solution.py:27
  46.3 1.0 collective-permute-start.10
  47.3 6.4 %convolution_add_fusion.1 = f32[1536,768]{0,1:T(8,128)S(1)} fusion(f32[1536,768]{0,1:T(8,128)} %fusion.2, bf16[1024,1536]{1,0:T(8,128)(2,1)} %collective-permute-done, bf16[1024,768]{1,0:T(8,128)(2,1)} %collective-permute-done.1), kind=kOutput, calls=%fused_computation.2 | convolution fusion | flops 2417098752 | bytes 14155776 | tf_op jit(solution)/shard_map/dot_general | solution.py:27
  53.7 2.0 dynamic-slice_bitcast_fusion.5
  55.7 1.3 copy-done.1
  57.0 2.7 %collective-permute-start.2 = (f32[4,48,1536]{2,1,0:T(8,128)}, f32[4,48,1536]{2,1,0:T(8,128)S(1)}, u32[]{:S(2)}, u32[]{:S(2)}) collective-permute-start(f32[4,48,1536]{2,1,0:T(8,128)} %get-tuple-element.26), channel_id=1, source_target_pairs={{0,64},{4,68},{8,72},{12,76},{16,80},{20,84},{24,88},{28,92},{32,9... | collective-permute-start | bytes 3538952 | tf_op jit(solution)/shard_map/ppermute | solution.py:43
  59.8 0.9 collective-permute-start.4
  60.7 4.2 %collective-permute-done.9 = f32[4,48,1536]{2,1,0:T(8,128)} collective-permute-done((f32[4,48,1536]{2,1,0:T(8,128)}, f32[4,48,1536]{2,1,0:T(8,128)}, u32[]{:S(2)}, u32[]{:S(2)}) %collective-permute-start.9) | collective-permute-done | bytes 1179680 | tf_op jit(solution)/shard_map/ppermute | solution.py:43
  64.9 1.2 collective-permute-start.3
  66.1 1.0 fusion.21
  67.1 23.5 %collective-permute-done.11 = f32[4,48,1536]{2,1,0:T(8,128)} collective-permute-done((f32[4,48,1536]{2,1,0:T(8,128)}, f32[4,48,1536]{2,1,0:T(8,128)}, u32[]{:S(2)}, u32[]{:S(2)}) %collective-permute-start.11) | collective-permute-done | bytes 1179680 | tf_op jit(solution)/shard_map/ppermute | solution.py:43
  90.6 2.4 %collective-permute-start.28 = (f32[240,128]{1,0:T(8,128)S(1)}, f32[240,128]{1,0:T(8,128)S(1)}, u32[]{:S(2)}, u32[]{:S(2)}) collective-permute-start(f32[240,128]{1,0:T(8,128)S(1)} %fusion.21), channel_id=1, source_target_pairs={{0,96},{4,100},{8,104},{12,108},{16,112},{20,116},{24,120},{28,124... | collective-permute-start | bytes 368648 | tf_op jit(solution)/shard_map/ppermute | solution.py:43
  93.6 2.7 %fusion.5 = f32[4,48,1536]{2,1,0:T(8,128)S(1)} fusion(f32[4,48,1536]{2,1,0:T(8,128)} %collective-permute-done.11, f32[4,48,1536]{2,1,0:T(8,128)} %collective-permute-done.10, f32[4,48,1536]{2,1,0:T(8,128)} %collective-permute-done.9, f32[4,4,48,1536]{3,2,1,0:T(8,128)} %bitcast.105, s32[]{:T(128)S(6)} %select_n.162), kind=kLoop, calls=%fused_computation.9 | loop fusion | flops 884736 | bytes 5898244 | tf_op jit(solution)/shard_map/add | solution.py:75
  96.4 0.7 collective-permute-start.26
  97.1 14.0 %collective-permute-done.4 = f32[4,48,1536]{2,1,0:T(8,128)S(1)} collective-permute-done((f32[4,48,1536]{2,1,0:T(8,128)}, f32[4,48,1536]{2,1,0:T(8,128)S(1)}, u32[]{:S(2)}, u32[]{:S(2)}) %collective-permute-start.4) | collective-permute-done | bytes 1179680 | tf_op jit(solution)/shard_map/ppermute | solution.py:43
  111.1 1.7 collective-permute-start.12
  113.2 2.3 collective-permute-start.14
  115.5 1.7 fusion.7
  117.4 1.1 collective-permute-start.5
  118.9 1.7 collective-permute-start.7
  120.6 1.2 collective-permute-done.12
  121.8 0.7 collective-permute-start.6
  122.6 6.4 %collective-permute-done.14 = f32[48,1536]{1,0:T(8,128)S(1)} collective-permute-done((f32[48,1536]{1,0:T(8,128)S(1)}, f32[48,1536]{1,0:T(8,128)S(1)}, u32[]{:S(2)}, u32[]{:S(2)}) %collective-permute-start.14) | collective-permute-done | bytes 294944 | tf_op jit(solution)/shard_map/ppermute | solution.py:43
  129.0 1.6 collective-permute-start.31
  130.6 0.8 collective-permute-start.30
  132.4 3.7 %collective-permute-start.15 = (f32[8,128]{1,0:T(8,128)S(1)}, f32[8,128]{1,0:T(8,128)S(1)}, u32[]{:S(2)}, u32[]{:S(2)}) collective-permute-start(f32[8,128]{1,0:T(8,128)S(1)} %add.332), channel_id=1, source_target_pairs={{0,4},{4,0},{8,12},{12,8},{16,20},{20,16},{24,28},{28,24},{32,36},... | collective-permute-start | bytes 12296 | tf_op jit(solution)/shard_map/ppermute | solution.py:43
  136.1 1.7 collective-permute-done.29
  137.9 5.3 %collective-permute-start.18 = (f32[8,128]{1,0:T(8,128)S(1)}, f32[8,128]{1,0:T(8,128)S(1)}, u32[]{:S(2)}, u32[]{:S(2)}) collective-permute-start(f32[8,128]{1,0:T(8,128)S(1)} %add.333), channel_id=1, source_target_pairs={{0,96},{4,100},{8,104},{12,108},{16,112},{20,116},{24,120},{28,124... | collective-permute-start | bytes 12296 | tf_op jit(solution)/shard_map/ppermute | solution.py:43
  143.9 3.2 %collective-permute-done.17 = f32[8,128]{1,0:T(8,128)S(1)} collective-permute-done((f32[8,128]{1,0:T(8,128)S(1)}, f32[8,128]{1,0:T(8,128)S(1)}, u32[]{:S(2)}, u32[]{:S(2)}) %collective-permute-start.17) | collective-permute-done | bytes 4128 | tf_op jit(solution)/shard_map/ppermute | solution.py:43
  147.3 1.0 collective-permute-start.20
  148.3 0.8 collective-permute-start.19
  149.1 3.6 %collective-permute-start.32 = (f32[24,3072]{1,0:T(8,128)S(1)}, f32[24,3072]{1,0:T(8,128)}, u32[]{:S(2)}, u32[]{:S(2)}) collective-permute-start(f32[24,3072]{1,0:T(8,128)S(1)} %dynamic-slice_bitcast_fusion.6), channel_id=1, source_target_pairs={{0,4},{4,0},{8,12},{12,8},{16,20},{20,16},{24,28},{28,24},{32,36},... | collective-permute-start | bytes 884744 | tf_op jit(solution)/shard_map/ppermute | solution.py:43
  152.7 2.8 %collective-permute-start.24 = (f32[8,128]{1,0:T(8,128)S(1)}, f32[8,128]{1,0:T(8,128)S(1)}, u32[]{:S(2)}, u32[]{:S(2)}) collective-permute-start(f32[8,128]{1,0:T(8,128)S(1)} %add_add_fusion.2), channel_id=1, source_target_pairs={{0,3},{1,0},{2,1},{3,2},{4,7},{5,4},{6,5},{7,6},{8,11},{9,8},{10,9... | collective-permute-start | bytes 12296 | tf_op jit(solution)/shard_map/ppermute | solution.py:47
  155.8 0.7 collective-permute-start.22
  157.1 2.3 collective-permute-done.23
  161.5 1.0 bitcast_select_fusion.1
  162.5 1.8 fusion.26
  164.4 0.6 fusion.22
  167.5 54.8 %all-gather.2.cloned.1.call-done = bf16[768,6144]{1,0:T(8,128)(2,1)} async-done(((bf16[24,6144]{1,0:T(8,128)(2,1)}), bf16[768,6144]{1,0:T(8,128)(2,1)}) %all-gather.2.cloned.1.call-update) | async-done | bytes 9437200 | tf_op jit(solution)/shard_map/all_gather | solution.py:162
  222.3 8.6 %copy.22 = bf16[768,6144]{1,0:T(8,128)(2,1)} copy(bf16[768,6144]{1,0:T(8,128)(2,1)} %all-gather.2.cloned.1.call-done) | data formatting | bytes 18874368
  (85 shorter events, 9.7 us)
Async XLA Ops:
  7.2 215.2 %all-gather.2.cloned.1.call-start = ((), (), s32[]{:S(2)}) async-start(), calls=%async_computation | async-start | bytes 9732096 | tf_op jit(solution)/shard_map/all_gather | solution.py:162
  7.2 6.9 %copy-start.9 = (f32[192]{0:T(256)S(1)}, f32[192]{0:T(256)}, u32[]{:S(2)}) copy-start(f32[192]{0:T(256)} %param.19) | copy-start | bytes 2308
  7.3 6.9 %copy-start.10 = (f32[192]{0:T(256)S(1)}, f32[192]{0:T(256)}, u32[]{:S(2)}) copy-start(f32[192]{0:T(256)} %param.18) | copy-start | bytes 2308
  7.3 6.9 %copy-start.11 = (f32[192]{0:T(256)S(1)}, f32[192]{0:T(256)}, u32[]{:S(2)}) copy-start(f32[192]{0:T(256)} %param.17) | copy-start | bytes 2308
  7.3 6.9 %copy-start.12 = (f32[192]{0:T(256)S(1)}, f32[192]{0:T(256)}, u32[]{:S(2)}) copy-start(f32[192]{0:T(256)} %param.16) | copy-start | bytes 2308
  12.2 14.5 %collective-permute-start.8 = (bf16[1024,1536]{1,0:T(8,128)(2,1)}, bf16[1024,1536]{1,0:T(8,128)(2,1)}, u32[]{:S(2)}, u32[]{:S(2)}) collective-permute-start(bf16[1024,1536]{1,0:T(8,128)(2,1)} %get-tuple-element.25), channel_id=1, source_target_pairs={{0,4},{4,0},{8,12},{12,8},{16,20},{20,16},{24,28},{28,24},{32,36},... | collective-permute-start | bytes 9437192 | tf_op jit(solution)/shard_map/ppermute | solution.py:43
  13.6 13.0 %collective-permute-start.1 = (bf16[1024,768]{1,0:T(8,128)(2,1)}, bf16[1024,768]{1,0:T(8,128)(2,1)}, u32[]{:S(2)}, u32[]{:S(2)}) collective-permute-start(bf16[1024,768]{1,0:T(8,128)(2,1)} %param.10), channel_id=1, source_target_pairs={{0,4},{4,0},{8,12},{12,8},{16,20},{20,16},{24,28},{28,24},{32,36},... | collective-permute-start | bytes 4718600 | tf_op jit(solution)/shard_map/ppermute | solution.py:43
  13.7 33.6 %collective-permute-start = (bf16[1024,1536]{1,0:T(8,128)(2,1)S(1)}, bf16[1024,1536]{1,0:T(8,128)(2,1)}, u32[]{:S(2)}, u32[]{:S(2)}) collective-permute-start(bf16[1024,1536]{1,0:T(8,128)(2,1)S(1)} %get-tuple-element.24), channel_id=1, source_target_pairs={{0,4},{4,0},{8,12},{12,8},{16,20},{20,16},{24,28},{28,24},{32,36},... | collective-permute-start | bytes 9437192 | tf_op jit(solution)/shard_map/ppermute | solution.py:43
  14.6 6.4 %copy-start.2 = (f32[192,128]{1,0:T(8,128)}, f32[192,128]{1,0:T(8,128)S(1)}, u32[]{:S(2)}) copy-start(f32[192,128]{1,0:T(8,128)S(1)} %reshape.66) | copy-start | bytes 294916
  21.1 0.6 copy-start.7
  21.7 38.1 %collective-permute-start.25 = (f32[240,128]{1,0:T(8,128)S(1)}, f32[240,128]{1,0:T(8,128)S(1)}, u32[]{:S(2)}, u32[]{:S(2)}) collective-permute-start(f32[240,128]{1,0:T(8,128)S(1)} %pad_maximum_fusion.1), channel_id=1, source_target_pairs={{0,4},{4,0},{8,12},{12,8},{16,20},{20,16},{24,28},{28,24},{32,36},... | collective-permute-start | bytes 368648 | tf_op jit(solution)/shard_map/ppermute | solution.py:43
  31.7 3.3 %copy-start = (f32[1536,768]{0,1:T(8,128)}, f32[1536,768]{0,1:T(8,128)S(1)}, u32[]{:S(2)}) copy-start(f32[1536,768]{0,1:T(8,128)S(1)} %convolution_add_fusion) | copy-start | bytes 14155780
  35.0 29.9 %collective-permute-start.9 = (f32[4,48,1536]{2,1,0:T(8,128)}, f32[4,48,1536]{2,1,0:T(8,128)}, u32[]{:S(2)}, u32[]{:S(2)}) collective-permute-start(f32[4,48,1536]{2,1,0:T(8,128)} %get-tuple-element.29), channel_id=1, source_target_pairs={{0,16},{4,20},{8,24},{12,28},{16,0},{20,4},{24,8},{28,12},{32,48},... | collective-permute-start | bytes 3538952 | tf_op jit(solution)/shard_map/ppermute | solution.py:43
  45.8 44.8 %collective-permute-start.11 = (f32[4,48,1536]{2,1,0:T(8,128)}, f32[4,48,1536]{2,1,0:T(8,128)}, u32[]{:S(2)}, u32[]{:S(2)}) collective-permute-start(f32[4,48,1536]{2,1,0:T(8,128)} %get-tuple-element.30), channel_id=1, source_target_pairs={{0,24},{4,28},{8,0},{12,4},{16,8},{20,12},{24,16},{28,20},{32,56},... | collective-permute-start | bytes 3538952 | tf_op jit(solution)/shard_map/ppermute | solution.py:43
  46.3 46.8 %collective-permute-start.10 = (f32[4,48,1536]{2,1,0:T(8,128)}, f32[4,48,1536]{2,1,0:T(8,128)}, u32[]{:S(2)}, u32[]{:S(2)}) collective-permute-start(f32[4,48,1536]{2,1,0:T(8,128)} %get-tuple-element.31), channel_id=1, source_target_pairs={{0,8},{4,12},{8,16},{12,20},{16,24},{20,28},{24,0},{28,4},{32,40},... | collective-permute-start | bytes 3538952 | tf_op jit(solution)/shard_map/ppermute | solution.py:43
  53.7 3.3 %copy-start.1 = (f32[1536,768]{0,1:T(8,128)}, f32[1536,768]{0,1:T(8,128)S(1)}, u32[]{:S(2)}) copy-start(f32[1536,768]{0,1:T(8,128)S(1)} %convolution_add_fusion.1) | copy-start | bytes 14155780
  57.0 39.4 %collective-permute-start.2 = (f32[4,48,1536]{2,1,0:T(8,128)}, f32[4,48,1536]{2,1,0:T(8,128)S(1)}, u32[]{:S(2)}, u32[]{:S(2)}) collective-permute-start(f32[4,48,1536]{2,1,0:T(8,128)} %get-tuple-element.26), channel_id=1, source_target_pairs={{0,64},{4,68},{8,72},{12,76},{16,80},{20,84},{24,88},{28,92},{32,9... | collective-permute-start | bytes 3538952 | tf_op jit(solution)/shard_map/ppermute | solution.py:43
  59.8 5.1 %copy-start.8 = (f32[240,128]{1,0:T(8,128)}, f32[240,128]{1,0:T(8,128)S(1)}, u32[]{:S(2)}) copy-start(f32[240,128]{1,0:T(8,128)S(1)} %collective-permute-done.25) | copy-start | bytes 368644
  59.8 51.3 %collective-permute-start.4 = (f32[4,48,1536]{2,1,0:T(8,128)}, f32[4,48,1536]{2,1,0:T(8,128)S(1)}, u32[]{:S(2)}, u32[]{:S(2)}) collective-permute-start(f32[4,48,1536]{2,1,0:T(8,128)} %get-tuple-element.27), channel_id=1, source_target_pairs={{0,96},{4,100},{8,104},{12,108},{16,112},{20,116},{24,120},{28,124... | collective-permute-start | bytes 3538952 | tf_op jit(solution)/shard_map/ppermute | solution.py:43
  64.9 48.3 %collective-permute-start.3 = (f32[4,48,1536]{2,1,0:T(8,128)}, f32[4,48,1536]{2,1,0:T(8,128)S(1)}, u32[]{:S(2)}, u32[]{:S(2)}) collective-permute-start(f32[4,48,1536]{2,1,0:T(8,128)} %get-tuple-element.28), channel_id=1, source_target_pairs={{0,32},{4,36},{8,40},{12,44},{16,48},{20,52},{24,56},{28,60},{32,6... | collective-permute-start | bytes 3538952 | tf_op jit(solution)/shard_map/ppermute | solution.py:43
  90.6 26.6 %collective-permute-start.28 = (f32[240,128]{1,0:T(8,128)S(1)}, f32[240,128]{1,0:T(8,128)S(1)}, u32[]{:S(2)}, u32[]{:S(2)}) collective-permute-start(f32[240,128]{1,0:T(8,128)S(1)} %fusion.21), channel_id=1, source_target_pairs={{0,96},{4,100},{8,104},{12,108},{16,112},{20,116},{24,120},{28,124... | collective-permute-start | bytes 368648 | tf_op jit(solution)/shard_map/ppermute | solution.py:43
  93.0 24.3 %collective-permute-start.27 = (f32[240,128]{1,0:T(8,128)S(1)}, f32[240,128]{1,0:T(8,128)S(1)}, u32[]{:S(2)}, u32[]{:S(2)}) collective-permute-start(f32[240,128]{1,0:T(8,128)S(1)} %fusion.21), channel_id=1, source_target_pairs={{0,64},{4,68},{8,72},{12,76},{16,80},{20,84},{24,88},{28,92},{32,9... | collective-permute-start | bytes 368648 | tf_op jit(solution)/shard_map/ppermute | solution.py:43
  96.4 22.5 %collective-permute-start.26 = (f32[240,128]{1,0:T(8,128)S(1)}, f32[240,128]{1,0:T(8,128)S(1)}, u32[]{:S(2)}, u32[]{:S(2)}) collective-permute-start(f32[240,128]{1,0:T(8,128)S(1)} %fusion.21), channel_id=1, source_target_pairs={{0,32},{4,36},{8,40},{12,44},{16,48},{20,52},{24,56},{28,60},{32,6... | collective-permute-start | bytes 368648 | tf_op jit(solution)/shard_map/ppermute | solution.py:43
  111.1 10.7 %collective-permute-start.12 = (f32[48,1536]{1,0:T(8,128)S(1)}, f32[48,1536]{1,0:T(8,128)S(1)}, u32[]{:S(2)}, u32[]{:S(2)}) collective-permute-start(f32[48,1536]{1,0:T(8,128)S(1)} %get-tuple-element.35), channel_id=1, source_target_pairs={{0,64},{4,68},{8,72},{12,76},{16,80},{20,84},{24,88},{28,92},{32,9... | collective-permute-start | bytes 884744 | tf_op jit(solution)/shard_map/ppermute | solution.py:43
  113.2 15.7 %collective-permute-start.14 = (f32[48,1536]{1,0:T(8,128)S(1)}, f32[48,1536]{1,0:T(8,128)S(1)}, u32[]{:S(2)}, u32[]{:S(2)}) collective-permute-start(f32[48,1536]{1,0:T(8,128)S(1)} %get-tuple-element.36), channel_id=1, source_target_pairs={{0,96},{4,100},{8,104},{12,108},{16,112},{20,116},{24,120},{28,124... | collective-permute-start | bytes 884744 | tf_op jit(solution)/shard_map/ppermute | solution.py:43
  117.2 13.4 %collective-permute-start.13 = (f32[48,1536]{1,0:T(8,128)S(1)}, f32[48,1536]{1,0:T(8,128)S(1)}, u32[]{:S(2)}, u32[]{:S(2)}) collective-permute-start(f32[48,1536]{1,0:T(8,128)S(1)} %get-tuple-element.37), channel_id=1, source_target_pairs={{0,32},{4,36},{8,40},{12,44},{16,48},{20,52},{24,56},{28,60},{32,6... | collective-permute-start | bytes 884744 | tf_op jit(solution)/shard_map/ppermute | solution.py:43
  117.4 14.2 %collective-permute-start.5 = (f32[48,1536]{1,0:T(8,128)S(1)}, f32[48,1536]{1,0:T(8,128)S(1)}, u32[]{:S(2)}, u32[]{:S(2)}) collective-permute-start(f32[48,1536]{1,0:T(8,128)S(1)} %get-tuple-element.32), channel_id=1, source_target_pairs={{0,16},{4,20},{8,24},{12,28},{16,0},{20,4},{24,8},{28,12},{32,48},... | collective-permute-start | bytes 884744 | tf_op jit(solution)/shard_map/ppermute | solution.py:43
  118.9 13.0 %collective-permute-start.7 = (f32[48,1536]{1,0:T(8,128)S(1)}, f32[48,1536]{1,0:T(8,128)S(1)}, u32[]{:S(2)}, u32[]{:S(2)}) collective-permute-start(f32[48,1536]{1,0:T(8,128)S(1)} %get-tuple-element.33), channel_id=1, source_target_pairs={{0,24},{4,28},{8,0},{12,4},{16,8},{20,12},{24,16},{28,20},{32,56},... | collective-permute-start | bytes 884744 | tf_op jit(solution)/shard_map/ppermute | solution.py:43
  121.8 10.4 %collective-permute-start.6 = (f32[48,1536]{1,0:T(8,128)S(1)}, f32[48,1536]{1,0:T(8,128)S(1)}, u32[]{:S(2)}, u32[]{:S(2)}) collective-permute-start(f32[48,1536]{1,0:T(8,128)S(1)} %get-tuple-element.34), channel_id=1, source_target_pairs={{0,8},{4,12},{8,16},{12,20},{16,24},{20,28},{24,0},{28,4},{32,40},... | collective-permute-start | bytes 884744 | tf_op jit(solution)/shard_map/ppermute | solution.py:43
  129.0 7.1 %collective-permute-start.31 = (f32[240,128]{1,0:T(8,128)S(1)}, f32[240,128]{1,0:T(8,128)S(1)}, u32[]{:S(2)}, u32[]{:S(2)}) collective-permute-start(f32[240,128]{1,0:T(8,128)S(1)} %add_add_fusion.1), channel_id=1, source_target_pairs={{0,24},{4,28},{8,0},{12,4},{16,8},{20,12},{24,16},{28,20},{32,56},... | collective-permute-start | bytes 368648 | tf_op jit(solution)/shard_map/ppermute | solution.py:43
  130.6 5.5 %collective-permute-start.30 = (f32[240,128]{1,0:T(8,128)S(1)}, f32[240,128]{1,0:T(8,128)S(1)}, u32[]{:S(2)}, u32[]{:S(2)}) collective-permute-start(f32[240,128]{1,0:T(8,128)S(1)} %add_add_fusion.1), channel_id=1, source_target_pairs={{0,16},{4,20},{8,24},{12,28},{16,0},{20,4},{24,8},{28,12},{32,48},... | collective-permute-start | bytes 368648 | tf_op jit(solution)/shard_map/ppermute | solution.py:43
  131.6 6.2 %collective-permute-start.29 = (f32[240,128]{1,0:T(8,128)S(1)}, f32[240,128]{1,0:T(8,128)S(1)}, u32[]{:S(2)}, u32[]{:S(2)}) collective-permute-start(f32[240,128]{1,0:T(8,128)S(1)} %add_add_fusion.1), channel_id=1, source_target_pairs={{0,8},{4,12},{8,16},{12,20},{16,24},{20,28},{24,0},{28,4},{32,40},... | collective-permute-start | bytes 368648 | tf_op jit(solution)/shard_map/ppermute | solution.py:43
  132.4 5.5 %collective-permute-start.15 = (f32[8,128]{1,0:T(8,128)S(1)}, f32[8,128]{1,0:T(8,128)S(1)}, u32[]{:S(2)}, u32[]{:S(2)}) collective-permute-start(f32[8,128]{1,0:T(8,128)S(1)} %add.332), channel_id=1, source_target_pairs={{0,4},{4,0},{8,12},{12,8},{16,20},{20,16},{24,28},{28,24},{32,36},... | collective-permute-start | bytes 12296 | tf_op jit(solution)/shard_map/ppermute | solution.py:43
  137.8 24.7 %copy-start.3 = (f32[24,6144]{1,0:T(8,128)S(1)}, f32[24,6144]{1,0:T(8,128)}, u32[]{:S(2)}) copy-start(f32[24,6144]{1,0:T(8,128)} %param.15) | copy-start | bytes 1769476
  137.8 24.7 %copy-start.4 = (f32[24,6144]{1,0:T(8,128)S(1)}, f32[24,6144]{1,0:T(8,128)}, u32[]{:S(2)}) copy-start(f32[24,6144]{1,0:T(8,128)} %param.12) | copy-start | bytes 1769476
  137.8 24.7 %copy-start.5 = (f32[24,6144]{1,0:T(8,128)S(1)}, f32[24,6144]{1,0:T(8,128)}, u32[]{:S(2)}) copy-start(f32[24,6144]{1,0:T(8,128)} %param.14) | copy-start | bytes 1769476
  137.8 24.7 %copy-start.6 = (f32[24,6144]{1,0:T(8,128)S(1)}, f32[24,6144]{1,0:T(8,128)}, u32[]{:S(2)}) copy-start(f32[24,6144]{1,0:T(8,128)} %param.13) | copy-start | bytes 1769476
  137.9 6.0 %collective-permute-start.18 = (f32[8,128]{1,0:T(8,128)S(1)}, f32[8,128]{1,0:T(8,128)S(1)}, u32[]{:S(2)}, u32[]{:S(2)}) collective-permute-start(f32[8,128]{1,0:T(8,128)S(1)} %add.333), channel_id=1, source_target_pairs={{0,96},{4,100},{8,104},{12,108},{16,112},{20,116},{24,120},{28,124... | collective-permute-start | bytes 12296 | tf_op jit(solution)/shard_map/ppermute | solution.py:43
  143.2 4.0 %collective-permute-start.17 = (f32[8,128]{1,0:T(8,128)S(1)}, f32[8,128]{1,0:T(8,128)S(1)}, u32[]{:S(2)}, u32[]{:S(2)}) collective-permute-start(f32[8,128]{1,0:T(8,128)S(1)} %add.333), channel_id=1, source_target_pairs={{0,64},{4,68},{8,72},{12,76},{16,80},{20,84},{24,88},{28,92},{32,9... | collective-permute-start | bytes 12296 | tf_op jit(solution)/shard_map/ppermute | solution.py:43
  143.7 3.7 %collective-permute-start.16 = (f32[8,128]{1,0:T(8,128)S(1)}, f32[8,128]{1,0:T(8,128)S(1)}, u32[]{:S(2)}, u32[]{:S(2)}) collective-permute-start(f32[8,128]{1,0:T(8,128)S(1)} %add.333), channel_id=1, source_target_pairs={{0,32},{4,36},{8,40},{12,44},{16,48},{20,52},{24,56},{28,60},{32,6... | collective-permute-start | bytes 12296 | tf_op jit(solution)/shard_map/ppermute | solution.py:43
  147.3 5.3 %collective-permute-start.21 = (f32[8,128]{1,0:T(8,128)S(1)}, f32[8,128]{1,0:T(8,128)S(1)}, u32[]{:S(2)}, u32[]{:S(2)}) collective-permute-start(f32[8,128]{1,0:T(8,128)S(1)} %add_add_fusion.3), channel_id=1, source_target_pairs={{0,24},{4,28},{8,0},{12,4},{16,8},{20,12},{24,16},{28,20},{32,56},... | collective-permute-start | bytes 12296 | tf_op jit(solution)/shard_map/ppermute | solution.py:43
  147.3 5.3 %collective-permute-start.20 = (f32[8,128]{1,0:T(8,128)S(1)}, f32[8,128]{1,0:T(8,128)S(1)}, u32[]{:S(2)}, u32[]{:S(2)}) collective-permute-start(f32[8,128]{1,0:T(8,128)S(1)} %add_add_fusion.3), channel_id=1, source_target_pairs={{0,16},{4,20},{8,24},{12,28},{16,0},{20,4},{24,8},{28,12},{32,48},... | collective-permute-start | bytes 12296 | tf_op jit(solution)/shard_map/ppermute | solution.py:43
  148.3 4.4 %collective-permute-start.19 = (f32[8,128]{1,0:T(8,128)S(1)}, f32[8,128]{1,0:T(8,128)S(1)}, u32[]{:S(2)}, u32[]{:S(2)}) collective-permute-start(f32[8,128]{1,0:T(8,128)S(1)} %add_add_fusion.3), channel_id=1, source_target_pairs={{0,8},{4,12},{8,16},{12,20},{16,24},{20,28},{24,0},{28,4},{32,40},... | collective-permute-start | bytes 12296 | tf_op jit(solution)/shard_map/ppermute | solution.py:43
  149.1 12.3 %collective-permute-start.32 = (f32[24,3072]{1,0:T(8,128)S(1)}, f32[24,3072]{1,0:T(8,128)}, u32[]{:S(2)}, u32[]{:S(2)}) collective-permute-start(f32[24,3072]{1,0:T(8,128)S(1)} %dynamic-slice_bitcast_fusion.6), channel_id=1, source_target_pairs={{0,4},{4,0},{8,12},{12,8},{16,20},{20,16},{24,28},{28,24},{32,36},... | collective-permute-start | bytes 884744 | tf_op jit(solution)/shard_map/ppermute | solution.py:43
  152.7 4.5 %collective-permute-start.24 = (f32[8,128]{1,0:T(8,128)S(1)}, f32[8,128]{1,0:T(8,128)S(1)}, u32[]{:S(2)}, u32[]{:S(2)}) collective-permute-start(f32[8,128]{1,0:T(8,128)S(1)} %add_add_fusion.2), channel_id=1, source_target_pairs={{0,3},{1,0},{2,1},{3,2},{4,7},{5,4},{6,5},{7,6},{8,11},{9,8},{10,9... | collective-permute-start | bytes 12296 | tf_op jit(solution)/shard_map/ppermute | solution.py:47
  155.5 4.0 %collective-permute-start.23 = (f32[8,128]{1,0:T(8,128)S(1)}, f32[8,128]{1,0:T(8,128)S(1)}, u32[]{:S(2)}, u32[]{:S(2)}) collective-permute-start(f32[8,128]{1,0:T(8,128)S(1)} %add_add_fusion.2), channel_id=1, source_target_pairs={{0,2},{1,3},{2,0},{3,1},{4,6},{5,7},{6,4},{7,5},{8,10},{9,11},{10,... | collective-permute-start | bytes 12296 | tf_op jit(solution)/shard_map/ppermute | solution.py:47
  155.8 3.7 %collective-permute-start.22 = (f32[8,128]{1,0:T(8,128)S(1)}, f32[8,128]{1,0:T(8,128)S(1)}, u32[]{:S(2)}, u32[]{:S(2)}) collective-permute-start(f32[8,128]{1,0:T(8,128)S(1)} %add_add_fusion.2), channel_id=1, source_target_pairs={{0,1},{1,2},{2,3},{3,0},{4,5},{5,6},{6,7},{7,4},{8,9},{9,10},{10,1... | collective-permute-start | bytes 12296 | tf_op jit(solution)/shard_map/ppermute | solution.py:47
Sparse Core Ops, SparseCore 0:
  164.5 57.8 all-gather.1

commit v2 on v1

--- a/solution.py
+++ b/solution.py
@@ -1,6 +1,9 @@
+import functools
 import jax
 import jax.numpy as jnp
 from jax import lax
+from jax.experimental import pallas as pl
+from jax.experimental.pallas import tpu as pltpu
 from jax.sharding import PartitionSpec as P
 
 beta_one = 0.9
@@ -23,10 +26,54 @@
     return (new_master, new_moment, new_second, new_teacher)
 
 
-def transposed_product(left, right):
-    return lax.dot_general(
-        left, right, (((0,), (0,)), ((), ())), preferred_element_type=jnp.float32
-    )
+NOTE = 8
+
+
+def product_kernel(x_first, side, own, other, own_cols, other_cols, out):
+    dims = (((0,), (0,)), ((), ()))
+    value = lax.dot_general(own[...], own_cols[...], dims, preferred_element_type=jnp.float32)
+    value += lax.dot_general(other[...], other_cols[...], dims, preferred_element_type=jnp.float32)
+    peak = jnp.max(jnp.abs(value), axis=0, keepdims=True)
+    power = jnp.ceil(jnp.log2(jnp.maximum(peak, 1e-30))) + 1.0
+    value = value * jnp.exp2(15.0 - power)
+    rows, cols = value.shape
+    block = rows // X
+    small = block // Z
+    for i in range(X):
+        if x_first:
+            out[i, :block, :] = value[i * block : (i + 1) * block]
+        else:
+            for j in range(X):
+                at = j * block + i * small
+                out[i, j * small : (j + 1) * small, :] = value[at : at + small]
+        out[i, block:, :] = jnp.broadcast_to(power, (NOTE, cols))
+
+
+def chip_product(attn_own, attn_other, cotangent, start, other_cols, x_first):
+    tokens, rows = attn_own.shape
+    cols = other_cols.shape[1]
+    step = 512
+    whole = pl.BlockSpec((tokens, rows), lambda n, side: (0, 0))
+    shape = (X, rows // X + NOTE, cols)
+    return pl.pallas_call(
+        functools.partial(product_kernel, x_first),
+        grid_spec=pltpu.PrefetchScalarGridSpec(
+            num_scalar_prefetch=1,
+            grid=(cols // step,),
+            in_specs=[
+                whole,
+                whole,
+                pl.BlockSpec((tokens, step), lambda n, side: (0, side[0] + n)),
+                pl.BlockSpec((tokens, step), lambda n, side: (0, n)),
+            ],
+            out_specs=pl.BlockSpec((*shape[:2], step), lambda n, side: (0, 0, n)),
+        ),
+        out_shape=jax.ShapeDtypeStruct(shape, jnp.float32),
+        compiler_params=pltpu.CompilerParams(
+            dimension_semantics=("arbitrary",), vmem_limit_bytes=40 * 2**20
+        ),
+        cost_estimate=pl.CostEstimate(flops=1, bytes_accessed=1, transcendentals=0),
+    )((start // step).reshape(1).astype(jnp.int32), attn_own, attn_other, cotangent, other_cols)
 
 
 def place(x, z, c):
@@ -76,18 +123,64 @@
     return total
 
 
-def reduce_x_first(product, x, z):
-    rows, cols = product.shape
-    blocks = product.reshape(X, Z, rows // (X * Z), cols)
-    part = scatter_sum(blocks, 0, x, along_x)
-    return scatter_sum(part, 0, z, along_z)
-
-
-def reduce_z_first(product, x, z):
-    rows, cols = product.shape
-    blocks = product.reshape(X, Z, rows // (X * Z), cols)
-    part = scatter_sum(blocks, 1, z, along_z)
-    return scatter_sum(part, 0, x, along_x)
+def coded_pieces(blocks, me):
+    return [pick(blocks, 0, me + d).astype(jnp.float16) for d in (2, 1, 3)]
+
+
+def decoded(piece):
+    piece = piece.astype(jnp.float32)
+    rows = piece.shape[0] - NOTE
+    return piece[:rows] * jnp.exp2(piece[rows : rows + 1] - 15.0)
+
+
+def coded_sum(blocks, pieces, me, move):
+    total = decoded(pick(blocks, 0, me))
+    for d, piece in zip((2, 1, 3), pieces):
+        total = total + decoded(move(piece, d))
+    return total.reshape(X, -1, total.shape[1])
+
+
+def gather_line(own, me, move):
+    got = [own] + [move(own, d) for d in (1, 2, 3)]
+    turned = jnp.stack([got[3], got[2], got[1], got[0], got[3], got[2], got[1]])
+    return lax.dynamic_slice_in_dim(turned, 3 - me, 4, axis=0)
+
+
+def nothing(out):
+    pass
+
+
+def blank(shape, dtype):
+    return pl.pallas_call(
+        nothing,
+        out_shape=jax.ShapeDtypeStruct(shape, dtype),
+        out_specs=pl.BlockSpec(memory_space=pl.ANY),
+    )()
+
+
+def gather_plane(rows, x, z, c):
+    count, width = rows.shape
+    half = width // 2
+    full = blank((X, Z, C, count, width), rows.dtype)
+    lines = [gather_line(rows[:, :half], z, along_z), gather_line(rows[:, half:], x, along_x)]
+    lines = lax.optimization_barrier(lines)
+    moves = (along_x, along_z)
+    near = [(which, d, moves[which](lines[which], d)) for d in (1, -1) for which in (0, 1)]
+    far = []
+    for which, d, line in near:
+        low = 0 if d == 1 else 2
+        far.append((which, 2, low, moves[which](line[low : low + 2], d)))
+    parts = [(which, 0, 0, lines[which]) for which in (0, 1)]
+    parts += [(which, d, 0, line) for which, d, line in near]
+    for which, d, low, part in parts + far:
+        zero, start = jnp.int32(0), jnp.int32(which * half)
+        for side, piece in ((c, part), (1 - c, shift(part, dc=1))):
+            if which == 0:
+                piece, at = piece[None, :, None], ((x - d) % X, jnp.int32(low))
+            else:
+                piece, at = piece[:, None, None], (jnp.int32(low), (z - d) % Z)
+            full = lax.dynamic_update_slice(full, piece, (*at, side, zero, start))
+    return full.reshape(X * Z * C * count, width)
 
 
 def squares(array):
@@ -118,14 +211,27 @@
         return lax.dynamic_slice(cotangent, (0, start), (tokens, quarter))
 
     attn_other = shift(attn_out, dc=1)
-    grads, sums = [], []
-    for which, reduce_in in ((0, reduce_x_first), (1, reduce_z_first)):
-        other = shift(columns((1 - c) * half + which * quarter), dc=1)
-        product = transposed_product(attn_out, columns(c * half + which * quarter))
-        product = product + transposed_product(attn_other, other)
-        grad = reduce_in(product, x, z)
-        grads.append(grad)
-        sums.append(squares(grad))
+    sent = [columns((1 - c) * half)]
+    held, sent[0] = lax.optimization_barrier((cotangent, sent[0]))
+    sent.append(lax.dynamic_slice(held, (0, (1 - c) * half + quarter), (tokens, quarter)))
+    others = [shift(part, dc=1) for part in sent]
+    bias_term = jnp.sum(held, axis=0, dtype=jnp.float32)
+
+    others[0], bias_term = lax.optimization_barrier((others[0], bias_term))
+
+    def blocks_of(which):
+        start = c * half + which * quarter
+        return chip_product(attn_out, attn_other, cotangent, start, others[which], which == 0)
+
+    blocks_a = blocks_of(0)
+    pieces_a = coded_pieces(blocks_a, x)
+    others[1], pieces_a = lax.optimization_barrier((others[1], pieces_a))
+    blocks_b = blocks_of(1)
+    pieces_b = coded_pieces(blocks_b, z)
+    part_a = coded_sum(blocks_a, pieces_a, x, along_x)
+    part_b = coded_sum(blocks_b, pieces_b, z, along_z)
+    grads = [scatter_sum(part_a, 0, z, along_z), scatter_sum(part_b, 0, x, along_x)]
+    sums = [squares(g) for g in grads]
     chip_grad = jnp.concatenate(grads, axis=1).reshape(C, own_rows, half)
     own_half = pick(chip_grad, 0, c)
     other_half = shift(pick(chip_grad, 0, 1 - c), dc=1)
@@ -133,11 +239,9 @@
     last = jnp.where(c == 0, other_half, own_half)
     weight_grad = jnp.concatenate([first, last], axis=1)
 
-    bias_term = jnp.sum(cotangent, axis=0, dtype=jnp.float32)
+    count = master_bias.shape[0]
     state = jnp.stack([master_bias, moment_bias, second_bias, teacher_bias])
-    spread = lax.dynamic_update_slice(
-        jnp.zeros((4, width), jnp.float32), state, (0, index * master_bias.shape[0])
-    )
+    spread = lax.dynamic_update_slice(jnp.zeros((4, width), jnp.float32), state, (0, index * count))
     packed = jnp.concatenate([bias_term.reshape(-1, 128), spread.reshape(-1, 128)], axis=0)
     packed = all_sum(packed, ("core", "x", "z")).reshape(5, width)
     bias_grad, bias_state = packed[0], packed[1:]
@@ -156,10 +260,9 @@
         decay_rate,
     )
     bias_new = adamw_update(bias_grad, *bias_state, clip_factor, 0.0)
-    count = master_bias.shape[0]
     own_bias = [lax.dynamic_slice(b, (index * count,), (count,)) for b in bias_new]
     full_bias = bias_new[3].astype(jnp.bfloat16)
-    full_weight = lax.all_gather(teacher_w.astype(jnp.bfloat16), "dp", axis=0, tiled=True)
+    full_weight = gather_plane(teacher_w.astype(jnp.bfloat16), x, z, c)
     return (master_w, moment_w, second_w, teacher_w, *own_bias, full_weight, full_bias)
 
 

time: 238 us -> 207 us (0.87)
  waiting for transfers between devices: 113 us -> 55.4 us
  starting transfers between devices: 44.8 us -> 80.8 us
  matrix products: 23.6 us -> 0 us
  Pallas kernels: 0 us -> 16 us
  between operations: 15.8 us -> 2.63 us
  local copies, waits for them, and re-layouts: 23.8 us -> 31.6 us
  other arithmetic: 16.9 us -> 20.2 us
    all_gather x1 -> x0, waiting for transfers between devices: 54.8 us -> none  [per_device(): lax.all_gather(teacher_w.astype(jnp.bfloat16), 'dp', axis=0, tiled=True)]
    ppermute x30 -> x54, starting transfers between devices: 41 us -> 77 us  [shift(): return lax.ppermute(array, 'dp', pairs)]
    dot_general x4 -> x0, matrix products: 23.6 us -> none  [transposed_product(): lax.dot_general(left, right, (((0,), (0,)), ((), ())), preferred_element_...]
    dynamic_update_slice x0 -> x20, local copies, waits for them, and re-layouts: none -> 16.1 us  [gather_plane(): full = lax.dynamic_update_slice(full, piece, (*at, side, zero, start))]
    pallas_call x0 -> x3, Pallas kernels: none -> 16 us  [the longest x2 16 us: chip_product(): pl.pallas_call(functools.partial(product_kernel, x_first), grid_spec=pltp...]
    unnamed x27 -> x36, local copies, waits for them, and re-layouts: 11.8 us -> 4.63 us
    squeeze x5 -> x3, local copies, waits for them, and re-layouts: 4.16 us -> 0.15 us  [pick(): lax.dynamic_index_in_dim(array, index % array.shape[axis], axis, keepdims...]
    dynamic_slice x0 -> x3, local copies, waits for them, and re-layouts: none -> 3.85 us  [the longest x1 3.75 us: per_device(): lax.dynamic_slice(held, (0, (1 - c) * half + quarter), (tokens, quarter))]
  transfers between devices with their start and end apart: 34 -> 57, of which waited for: 14 -> 20; matrix products, arithmetic and copies ran while one was open for 19% -> 19% of each run, Pallas kernels for 0% -> 4%
where the time goes in v2:
time: 207 us
  starting transfers between devices  80.8 us (39%)
  waiting for transfers between devices  55.4 us (27%)
  local copies, waits for them, and re-layouts  31.6 us (15%)
  other arithmetic  20.2 us (10%)
  Pallas kernels  16 us (8%)
  between operations  2.63 us (1%)
    ppermute x54, starting transfers between devices, shift(): return lax.ppermute(array, 'dp', pairs)  77 us
    ppermute x54, waiting for transfers between devices, shift(): return lax.ppermute(array, 'dp', pairs)  53 us
    dynamic_update_slice x20, local copies, waits for them, and re-layouts, gather_plane(): full = lax.dynamic_update_slice(full, piece, (*at, side, zero, start))  16.1 us
    pallas_call x2, Pallas kernels, chip_product(): pl.pallas_call(functools.partial(product_kernel, x_first), grid_spec=pltp...  16 us
    reduce_sum x1, other arithmetic, per_device(): bias_term = jnp.sum(held, axis=0, dtype=jnp.float32)  6.39 us
    unnamed x36, local copies, waits for them, and re-layouts  4.63 us
  transfers between devices with their start and end apart: 57, of which 20 were waited for; matrix products, arithmetic and copies ran while one was open for 19% of the time, Pallas kernels for 4%

profile of v2, /device:TPU:1, one launch (start us, length us, event | category | flops | bytes accessed | tf_op | source)
XLA Modules:
  0.0 206.7 jit_solution(8239895537095194918)
XLA Ops:
  0.7 3.9 %constant_dynamic-slice_fusion.5 = bf16[1024,1536]{1,0:T(8,128)(2,1)} fusion(bf16[1024,6144]{1,0:T(8,128)(2,1)} %own_cols.3, s32[]{:T(128)S(6)} %select_n.254), kind=kLoop, calls=%fused_computation.110 | loop fusion | bytes 6291460 | tf_op jit(solution)/shard_map/dynamic_slice | solution.py:211
  4.5 1.4 collective-permute-start.1
  6.0 3.8 %constant_dynamic-slice_fusion.3 = bf16[1024,1536]{1,0:T(8,128)(2,1)} fusion(bf16[1024,6144]{1,0:T(8,128)(2,1)} %own_cols.3, s32[]{:T(128)S(6)} %select_n.258), kind=kLoop, calls=%fused_computation.108 | loop fusion | bytes 6291460 | tf_op jit(solution)/shard_map/dynamic_slice | solution.py:216
  10.2 6.4 %convert_reduce_fusion = f32[6144]{0:T(1024)S(1)} fusion(bf16[1024,6144]{1,0:T(8,128)(2,1)} %own_cols.3), kind=kLoop, calls=%fused_computation | loop fusion | flops 12576768 | bytes 12607488 | tf_op jit(solution)/shard_map/reduce_sum | solution.py:218
  16.6 8.0 %shard_map.177 = f32[4,200,1536]{2,1,0:T(8,128)S(1)} custom-call(s32[1]{0:T(128)} %bitcast.side, bf16[1024,768]{1,0:T(8,128)(2,1)S(1)} %copy-done.2, bf16[1024,768]{1,0:T(8,128)(2,1)S(1)} %collective-permute-done.other, bf16[1024,6144]{1,0:T(8,128)(2,1)} %own_cols.3, bf16[1024,1536]{1,0:T(8,128)(2,1)} %collective-permute-done.1.other_cols), custom_call_target="tpu_custom_call" | custom-call | flops 1 | bytes 1 | tf_op jit(solution)/shard_map/pallas_call | solution.py:58
  24.7 2.2 %copy-done = f32[4,200,1536]{2,1,0:T(8,128)} copy-done((f32[4,200,1536]{2,1,0:T(8,128)}, f32[4,200,1536]{2,1,0:T(8,128)S(1)}, u32[]{:S(2)}) %copy-start) | copy-done | bytes 4915224
  26.9 1.3 fusion.10
  28.2 8.0 %shard_map.178 = f32[4,200,1536]{2,1,0:T(8,128)S(1)} custom-call(s32[1]{0:T(128)} %bitcast.11.side, bf16[1024,768]{1,0:T(8,128)(2,1)S(1)} %copy-done.2, bf16[1024,768]{1,0:T(8,128)(2,1)S(1)} %collective-permute-done.other, bf16[1024,6144]{1,0:T(8,128)(2,1)} %own_cols.3, bf16[1024,1536]{1,0:T(8,128)(2,1)} %collective-permute-done.2.other_cols), custom_call_target="tpu_custom_call" | custom-call | flops 1 | bytes 1 | tf_op jit(solution)/shard_map/pallas_call | solution.py:58
  36.2 2.2 %copy-done.1 = f32[4,200,1536]{2,1,0:T(8,128)} copy-done((f32[4,200,1536]{2,1,0:T(8,128)}, f32[4,200,1536]{2,1,0:T(8,128)S(1)}, u32[]{:S(2)}) %copy-start.1) | copy-done | bytes 4915224
  38.4 1.4 fusion.11
  39.8 3.9 %collective-permute-start.11 = (f16[200,1536]{1,0:T(8,128)(2,1)}, f16[200,1536]{1,0:T(8,128)(2,1)S(1)}, u32[]{:S(2)}, u32[]{:S(2)}) collective-permute-start(f16[200,1536]{1,0:T(8,128)(2,1)} %get-tuple-element.45), channel_id=1, source_target_pairs={{0,24},{4,28},{8,0},{12,4},{16,8},{20,12},{24,16},{28,20},{32,56},... | collective-permute-start | bytes 1843208 | tf_op jit(solution)/shard_map/ppermute | solution.py:90
  44.2 1.4 collective-permute-start.9
  46.5 2.5 %collective-permute-start.5 = (f16[200,1536]{1,0:T(8,128)(2,1)}, f16[200,1536]{1,0:T(8,128)(2,1)S(1)}, u32[]{:S(2)}, u32[]{:S(2)}) collective-permute-start(f16[200,1536]{1,0:T(8,128)(2,1)} %get-tuple-element.25), channel_id=1, source_target_pairs={{0,96},{4,100},{8,104},{12,108},{16,112},{20,116},{24,120},{28,124... | collective-permute-start | bytes 1843208 | tf_op jit(solution)/shard_map/ppermute | solution.py:90
  50.7 19.6 %collective-permute-done.11 = f16[200,1536]{1,0:T(8,128)(2,1)S(1)} collective-permute-done((f16[200,1536]{1,0:T(8,128)(2,1)}, f16[200,1536]{1,0:T(8,128)(2,1)S(1)}, u32[]{:S(2)}, u32[]{:S(2)}) %collective-permute-start.11) | collective-permute-done | bytes 614432 | tf_op jit(solution)/shard_map/ppermute | solution.py:90
  70.4 2.7 %collective-permute-start.3 = (f16[200,1536]{1,0:T(8,128)(2,1)S(1)}, f16[200,1536]{1,0:T(8,128)(2,1)S(1)}, u32[]{:S(2)}, u32[]{:S(2)}) collective-permute-start(f16[200,1536]{1,0:T(8,128)(2,1)S(1)} %copy-done.3), channel_id=1, source_target_pairs={{0,64},{4,68},{8,72},{12,76},{16,80},{20,84},{24,88},{28,92},{32,9... | collective-permute-start | bytes 1843208 | tf_op jit(solution)/shard_map/ppermute | solution.py:90
  73.4 2.5 %collective-permute-start.28 = (f32[240,128]{1,0:T(8,128)S(1)}, f32[240,128]{1,0:T(8,128)S(1)}, u32[]{:S(2)}, u32[]{:S(2)}) collective-permute-start(f32[240,128]{1,0:T(8,128)S(1)} %fusion.47), channel_id=1, source_target_pairs={{0,96},{4,100},{8,104},{12,108},{16,112},{20,116},{24,120},{28,124... | collective-permute-start | bytes 368648 | tf_op jit(solution)/shard_map/ppermute | solution.py:90
  76.8 1.8 fusion
  79.5 2.3 %collective-permute-start.14 = (f32[48,1536]{1,0:T(8,128)S(1)}, f32[48,1536]{1,0:T(8,128)S(1)}, u32[]{:S(2)}, u32[]{:S(2)}) collective-permute-start(f32[48,1536]{1,0:T(8,128)S(1)} %get-tuple-element.54), channel_id=1, source_target_pairs={{0,96},{4,100},{8,104},{12,108},{16,112},{20,116},{24,120},{28,124... | collective-permute-start | bytes 884744 | tf_op jit(solution)/shard_map/ppermute | solution.py:90
  82.0 4.4 %collective-permute-done.3 = f16[200,1536]{1,0:T(8,128)(2,1)S(1)} collective-permute-done((f16[200,1536]{1,0:T(8,128)(2,1)S(1)}, f16[200,1536]{1,0:T(8,128)(2,1)S(1)}, u32[]{:S(2)}, u32[]{:S(2)}) %collective-permute-start.3) | collective-permute-done | bytes 614432 | tf_op jit(solution)/shard_map/ppermute | solution.py:90
  86.4 1.2 collective-permute-start.13
  87.8 1.8 fusion.4
  90.1 2.1 %collective-permute-start.12 = (f32[48,1536]{1,0:T(8,128)S(1)}, f32[48,1536]{1,0:T(8,128)S(1)}, u32[]{:S(2)}, u32[]{:S(2)}) collective-permute-start(f32[48,1536]{1,0:T(8,128)S(1)} %get-tuple-element.53), channel_id=1, source_target_pairs={{0,64},{4,68},{8,72},{12,76},{16,80},{20,84},{24,88},{28,92},{32,9... | collective-permute-start | bytes 884744 | tf_op jit(solution)/shard_map/ppermute | solution.py:90
  92.2 3.4 %collective-permute-start.8 = (f32[48,1536]{1,0:T(8,128)S(1)}, f32[48,1536]{1,0:T(8,128)S(1)}, u32[]{:S(2)}, u32[]{:S(2)}) collective-permute-start(f32[48,1536]{1,0:T(8,128)S(1)} %get-tuple-element.51), channel_id=1, source_target_pairs={{0,24},{4,28},{8,0},{12,4},{16,8},{20,12},{24,16},{28,20},{32,56},... | collective-permute-start | bytes 884744 | tf_op jit(solution)/shard_map/ppermute | solution.py:90
  95.6 3.4 %collective-permute-done.14 = f32[48,1536]{1,0:T(8,128)S(1)} collective-permute-done((f32[48,1536]{1,0:T(8,128)S(1)}, f32[48,1536]{1,0:T(8,128)S(1)}, u32[]{:S(2)}, u32[]{:S(2)}) %collective-permute-start.14) | collective-permute-done | bytes 294944 | tf_op jit(solution)/shard_map/ppermute | solution.py:90
  99.2 3.3 %collective-permute-start.31 = (f32[240,128]{1,0:T(8,128)S(1)}, f32[240,128]{1,0:T(8,128)S(1)}, u32[]{:S(2)}, u32[]{:S(2)}) collective-permute-start(f32[240,128]{1,0:T(8,128)S(1)} %add_add_fusion.1), channel_id=1, source_target_pairs={{0,24},{4,28},{8,0},{12,4},{16,8},{20,12},{24,16},{28,20},{32,56},... | collective-permute-start | bytes 368648 | tf_op jit(solution)/shard_map/ppermute | solution.py:90
  102.5 1.2 collective-permute-done.12
  104.9 2.9 %collective-permute-start.29 = (f32[240,128]{1,0:T(8,128)S(1)}, f32[240,128]{1,0:T(8,128)S(1)}, u32[]{:S(2)}, u32[]{:S(2)}) collective-permute-start(f32[240,128]{1,0:T(8,128)S(1)} %add_add_fusion.1), channel_id=1, source_target_pairs={{0,8},{4,12},{8,16},{12,20},{16,24},{20,28},{24,0},{28,4},{32,40},... | collective-permute-start | bytes 368648 | tf_op jit(solution)/shard_map/ppermute | solution.py:90
  107.8 1.8 collective-permute-done.6
  109.7 7.8 %collective-permute-start.15 = (f32[8,128]{1,0:T(8,128)S(1)}, f32[8,128]{1,0:T(8,128)S(1)}, u32[]{:S(2)}, u32[]{:S(2)}) collective-permute-start(f32[8,128]{1,0:T(8,128)S(1)} %add.422), channel_id=1, source_target_pairs={{0,4},{4,0},{8,12},{12,8},{16,20},{20,16},{24,28},{28,24},{32,36},... | collective-permute-start | bytes 12296 | tf_op jit(solution)/shard_map/ppermute | solution.py:90
  118.3 2.1 %collective-permute-start.18 = (f32[8,128]{1,0:T(8,128)S(1)}, f32[8,128]{1,0:T(8,128)S(1)}, u32[]{:S(2)}, u32[]{:S(2)}) collective-permute-start(f32[8,128]{1,0:T(8,128)S(1)} %add.423), channel_id=1, source_target_pairs={{0,96},{4,100},{8,104},{12,108},{16,112},{20,116},{24,120},{28,124... | collective-permute-start | bytes 12296 | tf_op jit(solution)/shard_map/ppermute | solution.py:90
  120.4 1.3 collective-permute-start.17
  121.7 2.7 %collective-permute-done.17 = f32[8,128]{1,0:T(8,128)S(1)} collective-permute-done((f32[8,128]{1,0:T(8,128)S(1)}, f32[8,128]{1,0:T(8,128)S(1)}, u32[]{:S(2)}, u32[]{:S(2)}) %collective-permute-start.17) | collective-permute-done | bytes 4128 | tf_op jit(solution)/shard_map/ppermute | solution.py:90
  124.4 1.3 collective-permute-done.16
  127.1 2.7 %collective-permute-start.32 = (f32[24,3072]{1,0:T(8,128)S(1)}, f32[24,3072]{1,0:T(8,128)}, u32[]{:S(2)}, u32[]{:S(2)}) collective-permute-start(f32[24,3072]{1,0:T(8,128)S(1)} %dynamic-slice_bitcast_fusion.2), channel_id=1, source_target_pairs={{0,4},{4,0},{8,12},{12,8},{16,20},{20,16},{24,28},{28,24},{32,36},... | collective-permute-start | bytes 884744 | tf_op jit(solution)/shard_map/ppermute | solution.py:90
  130.5 2.7 %collective-permute-start.24 = (f32[8,128]{1,0:T(8,128)S(1)}, f32[8,128]{1,0:T(8,128)S(1)}, u32[]{:S(2)}, u32[]{:S(2)}) collective-permute-start(f32[8,128]{1,0:T(8,128)S(1)} %add_add_fusion.2), channel_id=1, source_target_pairs={{0,3},{1,0},{2,1},{3,2},{4,7},{5,4},{6,5},{7,6},{8,11},{9,8},{10,9... | collective-permute-start | bytes 12296 | tf_op jit(solution)/shard_map/ppermute | solution.py:94
  134.9 2.3 %collective-permute-done.23 = f32[8,128]{1,0:T(8,128)S(1)} collective-permute-done((f32[8,128]{1,0:T(8,128)S(1)}, f32[8,128]{1,0:T(8,128)S(1)}, u32[]{:S(2)}, u32[]{:S(2)}) %collective-permute-start.23) | collective-permute-done | bytes 4128 | tf_op jit(solution)/shard_map/ppermute | solution.py:94
  140.3 1.7 fusion.52
  146.8 2.0 collective-permute-start.33
  148.8 2.0 collective-permute-start.34
  152.4 2.0 collective-permute-done.34
  154.3 2.0 collective-permute-done.35
  156.6 6.5 %collective-permute-start.39 = (bf16[4,24,3072]{2,1,0:T(8,128)(2,1)S(1)}, bf16[4,24,3072]{2,1,0:T(8,128)(2,1)S(1)}, u32[]{:S(2)}, u32[]{:S(2)}) collective-permute-start(bf16[4,24,3072]{2,1,0:T(8,128)(2,1)S(1)} %constant_dynamic-slice_fusion.1), channel_id=1, source_target_pairs={{0,4},{4,0},{8,12},{12,8},{16,20},{20,16},{24,28},{28,24},{32,36},... | collective-permute-start | bytes 1769480 | tf_op jit(solution)/shard_map/ppermute | solution.py:90
  164.1 1.7 collective-permute-start.45
  165.8 2.7 %collective-permute-start.47 = (bf16[4,24,3072]{2,1,0:T(8,128)(2,1)S(1)}, bf16[4,24,3072]{2,1,0:T(8,128)(2,1)S(1)}, u32[]{:S(2)}, u32[]{:S(2)}) collective-permute-start(bf16[4,24,3072]{2,1,0:T(8,128)(2,1)S(1)} %constant_dynamic-slice_fusion), channel_id=1, source_target_pairs={{0,24},{4,28},{8,0},{12,4},{16,8},{20,12},{24,16},{28,20},{32,56},... | collective-permute-start | bytes 1769480 | tf_op jit(solution)/shard_map/ppermute | solution.py:90
  169.3 9.9 %collective-permute-done.41 = bf16[4,24,3072]{2,1,0:T(8,128)(2,1)S(1)} collective-permute-done((bf16[4,24,3072]{2,1,0:T(8,128)(2,1)S(1)}, bf16[4,24,3072]{2,1,0:T(8,128)(2,1)S(1)}, u32[]{:S(2)}, u32[]{:S(2)}) %collective-permute-start.41) | collective-permute-done | bytes 589856 | tf_op jit(solution)/shard_map/ppermute | solution.py:90
  182.4 1.8 collective-permute-start.53
  184.2 2.7 %collective-permute-start.55 = (bf16[2,24,3072]{2,1,0:T(8,128)(2,1)S(1)}, bf16[2,24,3072]{2,1,0:T(8,128)(2,1)S(1)}, u32[]{:S(2)}, u32[]{:S(2)}) collective-permute-start(bf16[2,24,3072]{2,1,0:T(8,128)(2,1)S(1)} %slice.131), channel_id=1, source_target_pairs={{0,24},{4,28},{8,0},{12,4},{16,8},{20,12},{24,16},{28,20},{32,56},... | collective-permute-start | bytes 884744 | tf_op jit(solution)/shard_map/ppermute | solution.py:90
  188.6 2.6 %collective-permute-start.42 = (bf16[4,24,3072]{2,1,0:T(8,128)(2,1)S(1)}, bf16[4,24,3072]{2,1,0:T(8,128)(2,1)S(1)}, u32[]{:S(2)}, u32[]{:S(2)}) collective-permute-start(bf16[4,24,3072]{2,1,0:T(8,128)(2,1)S(1)} %collective-permute-done.41), channel_id=1, source_target_pairs={{0,4},{4,0},{8,12},{12,8},{16,20},{20,16},{24,28},{28,24},{32,36},... | collective-permute-start | bytes 1769480 | tf_op jit(solution)/shard_map/ppermute | solution.py:90
  (182 shorter events, 43.1 us)
Async XLA Ops:
  4.5 12.1 %collective-permute-start.1 = (bf16[1024,1536]{1,0:T(8,128)(2,1)}, bf16[1024,1536]{1,0:T(8,128)(2,1)}, u32[]{:S(2)}, u32[]{:S(2)}) collective-permute-start(bf16[1024,1536]{1,0:T(8,128)(2,1)} %constant_dynamic-slice_fusion.5), channel_id=1, source_target_pairs={{0,4},{4,0},{8,12},{12,8},{16,20},{20,16},{24,28},{28,24},{32,36},... | collective-permute-start | bytes 9437192 | tf_op jit(solution)/shard_map/ppermute | solution.py:90
  9.7 18.5 %collective-permute-start.2 = (bf16[1024,1536]{1,0:T(8,128)(2,1)}, bf16[1024,1536]{1,0:T(8,128)(2,1)}, u32[]{:S(2)}, u32[]{:S(2)}) collective-permute-start(bf16[1024,1536]{1,0:T(8,128)(2,1)} %constant_dynamic-slice_fusion.3), channel_id=1, source_target_pairs={{0,4},{4,0},{8,12},{12,8},{16,20},{20,16},{24,28},{28,24},{32,36},... | collective-permute-start | bytes 9437192 | tf_op jit(solution)/shard_map/ppermute | solution.py:90
  9.7 6.9 %collective-permute-start = (bf16[1024,768]{1,0:T(8,128)(2,1)S(1)}, bf16[1024,768]{1,0:T(8,128)(2,1)S(1)}, u32[]{:S(2)}, u32[]{:S(2)}) collective-permute-start(bf16[1024,768]{1,0:T(8,128)(2,1)S(1)} %copy-done.2), channel_id=1, source_target_pairs={{0,4},{4,0},{8,12},{12,8},{16,20},{20,16},{24,28},{28,24},{32,36},... | collective-permute-start | bytes 4718600 | tf_op jit(solution)/shard_map/ppermute | solution.py:90
  39.8 30.5 %collective-permute-start.11 = (f16[200,1536]{1,0:T(8,128)(2,1)}, f16[200,1536]{1,0:T(8,128)(2,1)S(1)}, u32[]{:S(2)}, u32[]{:S(2)}) collective-permute-start(f16[200,1536]{1,0:T(8,128)(2,1)} %get-tuple-element.45), channel_id=1, source_target_pairs={{0,24},{4,28},{8,0},{12,4},{16,8},{20,12},{24,16},{28,20},{32,56},... | collective-permute-start | bytes 1843208 | tf_op jit(solution)/shard_map/ppermute | solution.py:90
  43.7 29.7 %collective-permute-start.10 = (f16[200,1536]{1,0:T(8,128)(2,1)}, f16[200,1536]{1,0:T(8,128)(2,1)S(1)}, u32[]{:S(2)}, u32[]{:S(2)}) collective-permute-start(f16[200,1536]{1,0:T(8,128)(2,1)} %get-tuple-element.46), channel_id=1, source_target_pairs={{0,8},{4,12},{8,16},{12,20},{16,24},{20,28},{24,0},{28,4},{32,40},... | collective-permute-start | bytes 1843208 | tf_op jit(solution)/shard_map/ppermute | solution.py:90
  44.2 31.9 %collective-permute-start.9 = (f16[200,1536]{1,0:T(8,128)(2,1)}, f16[200,1536]{1,0:T(8,128)(2,1)S(1)}, u32[]{:S(2)}, u32[]{:S(2)}) collective-permute-start(f16[200,1536]{1,0:T(8,128)(2,1)} %get-tuple-element.44), channel_id=1, source_target_pairs={{0,16},{4,20},{8,24},{12,28},{16,0},{20,4},{24,8},{28,12},{32,48},... | collective-permute-start | bytes 1843208 | tf_op jit(solution)/shard_map/ppermute | solution.py:90
  45.5 5.1 %collective-permute-start.25 = (f32[240,128]{1,0:T(8,128)S(1)}, f32[240,128]{1,0:T(8,128)S(1)}, u32[]{:S(2)}, u32[]{:S(2)}) collective-permute-start(f32[240,128]{1,0:T(8,128)S(1)} %pad_maximum_fusion.1), channel_id=1, source_target_pairs={{0,4},{4,0},{8,12},{12,8},{16,20},{20,16},{24,28},{28,24},{32,36},... | collective-permute-start | bytes 368648 | tf_op jit(solution)/shard_map/ppermute | solution.py:90
  46.5 32.1 %collective-permute-start.5 = (f16[200,1536]{1,0:T(8,128)(2,1)}, f16[200,1536]{1,0:T(8,128)(2,1)S(1)}, u32[]{:S(2)}, u32[]{:S(2)}) collective-permute-start(f16[200,1536]{1,0:T(8,128)(2,1)} %get-tuple-element.25), channel_id=1, source_target_pairs={{0,96},{4,100},{8,104},{12,108},{16,112},{20,116},{24,120},{28,124... | collective-permute-start | bytes 1843208 | tf_op jit(solution)/shard_map/ppermute | solution.py:90
  50.6 28.9 %collective-permute-start.4 = (f16[200,1536]{1,0:T(8,128)(2,1)S(1)}, f16[200,1536]{1,0:T(8,128)(2,1)S(1)}, u32[]{:S(2)}, u32[]{:S(2)}) collective-permute-start(f16[200,1536]{1,0:T(8,128)(2,1)S(1)} %copy-done.4), channel_id=1, source_target_pairs={{0,32},{4,36},{8,40},{12,44},{16,48},{20,52},{24,56},{28,60},{32,6... | collective-permute-start | bytes 1843208 | tf_op jit(solution)/shard_map/ppermute | solution.py:90
  70.4 16.0 %collective-permute-start.3 = (f16[200,1536]{1,0:T(8,128)(2,1)S(1)}, f16[200,1536]{1,0:T(8,128)(2,1)S(1)}, u32[]{:S(2)}, u32[]{:S(2)}) collective-permute-start(f16[200,1536]{1,0:T(8,128)(2,1)S(1)} %copy-done.3), channel_id=1, source_target_pairs={{0,64},{4,68},{8,72},{12,76},{16,80},{20,84},{24,88},{28,92},{32,9... | collective-permute-start | bytes 1843208 | tf_op jit(solution)/shard_map/ppermute | solution.py:90
  73.4 16.7 %collective-permute-start.28 = (f32[240,128]{1,0:T(8,128)S(1)}, f32[240,128]{1,0:T(8,128)S(1)}, u32[]{:S(2)}, u32[]{:S(2)}) collective-permute-start(f32[240,128]{1,0:T(8,128)S(1)} %fusion.47), channel_id=1, source_target_pairs={{0,96},{4,100},{8,104},{12,108},{16,112},{20,116},{24,120},{28,124... | collective-permute-start | bytes 368648 | tf_op jit(solution)/shard_map/ppermute | solution.py:90
  76.1 16.2 %collective-permute-start.27 = (f32[240,128]{1,0:T(8,128)S(1)}, f32[240,128]{1,0:T(8,128)S(1)}, u32[]{:S(2)}, u32[]{:S(2)}) collective-permute-start(f32[240,128]{1,0:T(8,128)S(1)} %fusion.47), channel_id=1, source_target_pairs={{0,64},{4,68},{8,72},{12,76},{16,80},{20,84},{24,88},{28,92},{32,9... | collective-permute-start | bytes 368648 | tf_op jit(solution)/shard_map/ppermute | solution.py:90
  78.6 17.0 %collective-permute-start.26 = (f32[240,128]{1,0:T(8,128)S(1)}, f32[240,128]{1,0:T(8,128)S(1)}, u32[]{:S(2)}, u32[]{:S(2)}) collective-permute-start(f32[240,128]{1,0:T(8,128)S(1)} %fusion.47), channel_id=1, source_target_pairs={{0,32},{4,36},{8,40},{12,44},{16,48},{20,52},{24,56},{28,60},{32,6... | collective-permute-start | bytes 368648 | tf_op jit(solution)/shard_map/ppermute | solution.py:90
  79.5 19.5 %collective-permute-start.14 = (f32[48,1536]{1,0:T(8,128)S(1)}, f32[48,1536]{1,0:T(8,128)S(1)}, u32[]{:S(2)}, u32[]{:S(2)}) collective-permute-start(f32[48,1536]{1,0:T(8,128)S(1)} %get-tuple-element.54), channel_id=1, source_target_pairs={{0,96},{4,100},{8,104},{12,108},{16,112},{20,116},{24,120},{28,124... | collective-permute-start | bytes 884744 | tf_op jit(solution)/shard_map/ppermute | solution.py:90
  86.4 12.8 %collective-permute-start.13 = (f32[48,1536]{1,0:T(8,128)S(1)}, f32[48,1536]{1,0:T(8,128)S(1)}, u32[]{:S(2)}, u32[]{:S(2)}) collective-permute-start(f32[48,1536]{1,0:T(8,128)S(1)} %get-tuple-element.55), channel_id=1, source_target_pairs={{0,32},{4,36},{8,40},{12,44},{16,48},{20,52},{24,56},{28,60},{32,6... | collective-permute-start | bytes 884744 | tf_op jit(solution)/shard_map/ppermute | solution.py:90
  90.1 13.7 %collective-permute-start.12 = (f32[48,1536]{1,0:T(8,128)S(1)}, f32[48,1536]{1,0:T(8,128)S(1)}, u32[]{:S(2)}, u32[]{:S(2)}) collective-permute-start(f32[48,1536]{1,0:T(8,128)S(1)} %get-tuple-element.53), channel_id=1, source_target_pairs={{0,64},{4,68},{8,72},{12,76},{16,80},{20,84},{24,88},{28,92},{32,9... | collective-permute-start | bytes 884744 | tf_op jit(solution)/shard_map/ppermute | solution.py:90
  92.2 12.7 %collective-permute-start.8 = (f32[48,1536]{1,0:T(8,128)S(1)}, f32[48,1536]{1,0:T(8,128)S(1)}, u32[]{:S(2)}, u32[]{:S(2)}) collective-permute-start(f32[48,1536]{1,0:T(8,128)S(1)} %get-tuple-element.51), channel_id=1, source_target_pairs={{0,24},{4,28},{8,0},{12,4},{16,8},{20,12},{24,16},{28,20},{32,56},... | collective-permute-start | bytes 884744 | tf_op jit(solution)/shard_map/ppermute | solution.py:90
  95.6 12.2 %collective-permute-start.7 = (f32[48,1536]{1,0:T(8,128)S(1)}, f32[48,1536]{1,0:T(8,128)S(1)}, u32[]{:S(2)}, u32[]{:S(2)}) collective-permute-start(f32[48,1536]{1,0:T(8,128)S(1)} %get-tuple-element.52), channel_id=1, source_target_pairs={{0,8},{4,12},{8,16},{12,20},{16,24},{20,28},{24,0},{28,4},{32,40},... | collective-permute-start | bytes 884744 | tf_op jit(solution)/shard_map/ppermute | solution.py:90
  99.0 10.6 %collective-permute-start.6 = (f32[48,1536]{1,0:T(8,128)S(1)}, f32[48,1536]{1,0:T(8,128)S(1)}, u32[]{:S(2)}, u32[]{:S(2)}) collective-permute-start(f32[48,1536]{1,0:T(8,128)S(1)} %get-tuple-element.50), channel_id=1, source_target_pairs={{0,16},{4,20},{8,24},{12,28},{16,0},{20,4},{24,8},{28,12},{32,48},... | collective-permute-start | bytes 884744 | tf_op jit(solution)/shard_map/ppermute | solution.py:90
  99.2 18.3 %collective-permute-start.31 = (f32[240,128]{1,0:T(8,128)S(1)}, f32[240,128]{1,0:T(8,128)S(1)}, u32[]{:S(2)}, u32[]{:S(2)}) collective-permute-start(f32[240,128]{1,0:T(8,128)S(1)} %add_add_fusion.1), channel_id=1, source_target_pairs={{0,24},{4,28},{8,0},{12,4},{16,8},{20,12},{24,16},{28,20},{32,56},... | collective-permute-start | bytes 368648 | tf_op jit(solution)/shard_map/ppermute | solution.py:90
  103.8 13.7 %collective-permute-start.30 = (f32[240,128]{1,0:T(8,128)S(1)}, f32[240,128]{1,0:T(8,128)S(1)}, u32[]{:S(2)}, u32[]{:S(2)}) collective-permute-start(f32[240,128]{1,0:T(8,128)S(1)} %add_add_fusion.1), channel_id=1, source_target_pairs={{0,16},{4,20},{8,24},{12,28},{16,0},{20,4},{24,8},{28,12},{32,48},... | collective-permute-start | bytes 368648 | tf_op jit(solution)/shard_map/ppermute | solution.py:90
  104.9 12.6 %collective-permute-start.29 = (f32[240,128]{1,0:T(8,128)S(1)}, f32[240,128]{1,0:T(8,128)S(1)}, u32[]{:S(2)}, u32[]{:S(2)}) collective-permute-start(f32[240,128]{1,0:T(8,128)S(1)} %add_add_fusion.1), channel_id=1, source_target_pairs={{0,8},{4,12},{8,16},{12,20},{16,24},{20,28},{24,0},{28,4},{32,40},... | collective-permute-start | bytes 368648 | tf_op jit(solution)/shard_map/ppermute | solution.py:90
  109.7 8.6 %collective-permute-start.15 = (f32[8,128]{1,0:T(8,128)S(1)}, f32[8,128]{1,0:T(8,128)S(1)}, u32[]{:S(2)}, u32[]{:S(2)}) collective-permute-start(f32[8,128]{1,0:T(8,128)S(1)} %add.422), channel_id=1, source_target_pairs={{0,4},{4,0},{8,12},{12,8},{16,20},{20,16},{24,28},{28,24},{32,36},... | collective-permute-start | bytes 12296 | tf_op jit(solution)/shard_map/ppermute | solution.py:90
  125.6 4.2 %collective-permute-start.21 = (f32[8,128]{1,0:T(8,128)S(1)}, f32[8,128]{1,0:T(8,128)S(1)}, u32[]{:S(2)}, u32[]{:S(2)}) collective-permute-start(f32[8,128]{1,0:T(8,128)S(1)} %add_add_fusion.3), channel_id=1, source_target_pairs={{0,24},{4,28},{8,0},{12,4},{16,8},{20,12},{24,16},{28,20},{32,56},... | collective-permute-start | bytes 12296 | tf_op jit(solution)/shard_map/ppermute | solution.py:90
  126.0 4.5 %collective-permute-start.19 = (f32[8,128]{1,0:T(8,128)S(1)}, f32[8,128]{1,0:T(8,128)S(1)}, u32[]{:S(2)}, u32[]{:S(2)}) collective-permute-start(f32[8,128]{1,0:T(8,128)S(1)} %add_add_fusion.3), channel_id=1, source_target_pairs={{0,8},{4,12},{8,16},{12,20},{16,24},{20,28},{24,0},{28,4},{32,40},... | collective-permute-start | bytes 12296 | tf_op jit(solution)/shard_map/ppermute | solution.py:90
  127.1 12.1 %collective-permute-start.32 = (f32[24,3072]{1,0:T(8,128)S(1)}, f32[24,3072]{1,0:T(8,128)}, u32[]{:S(2)}, u32[]{:S(2)}) collective-permute-start(f32[24,3072]{1,0:T(8,128)S(1)} %dynamic-slice_bitcast_fusion.2), channel_id=1, source_target_pairs={{0,4},{4,0},{8,12},{12,8},{16,20},{20,16},{24,28},{28,24},{32,36},... | collective-permute-start | bytes 884744 | tf_op jit(solution)/shard_map/ppermute | solution.py:90
  130.5 4.4 %collective-permute-start.24 = (f32[8,128]{1,0:T(8,128)S(1)}, f32[8,128]{1,0:T(8,128)S(1)}, u32[]{:S(2)}, u32[]{:S(2)}) collective-permute-start(f32[8,128]{1,0:T(8,128)S(1)} %add_add_fusion.2), channel_id=1, source_target_pairs={{0,3},{1,0},{2,1},{3,2},{4,7},{5,4},{6,5},{7,6},{8,11},{9,8},{10,9... | collective-permute-start | bytes 12296 | tf_op jit(solution)/shard_map/ppermute | solution.py:94
  142.0 8.9 %collective-permute-start.36 = (bf16[24,3072]{1,0:T(8,128)(2,1)S(1)}, bf16[24,3072]{1,0:T(8,128)(2,1)S(1)}, u32[]{:S(2)}, u32[]{:S(2)}) collective-permute-start(bf16[24,3072]{1,0:T(8,128)(2,1)S(1)} %get-tuple-element.60), channel_id=1, source_target_pairs={{0,96},{4,100},{8,104},{12,108},{16,112},{20,116},{24,120},{28,124... | collective-permute-start | bytes 442376 | tf_op jit(solution)/shard_map/ppermute | solution.py:90
  145.3 6.6 %collective-permute-start.37 = (bf16[24,3072]{1,0:T(8,128)(2,1)S(1)}, bf16[24,3072]{1,0:T(8,128)(2,1)S(1)}, u32[]{:S(2)}, u32[]{:S(2)}) collective-permute-start(bf16[24,3072]{1,0:T(8,128)(2,1)S(1)} %get-tuple-element.60), channel_id=1, source_target_pairs={{0,64},{4,68},{8,72},{12,76},{16,80},{20,84},{24,88},{28,92},{32,9... | collective-permute-start | bytes 442376 | tf_op jit(solution)/shard_map/ppermute | solution.py:90
  146.0 6.4 %collective-permute-start.38 = (bf16[24,3072]{1,0:T(8,128)(2,1)S(1)}, bf16[24,3072]{1,0:T(8,128)(2,1)S(1)}, u32[]{:S(2)}, u32[]{:S(2)}) collective-permute-start(bf16[24,3072]{1,0:T(8,128)(2,1)S(1)} %get-tuple-element.60), channel_id=1, source_target_pairs={{0,32},{4,36},{8,40},{12,44},{16,48},{20,52},{24,56},{28,60},{32,6... | collective-permute-start | bytes 442376 | tf_op jit(solution)/shard_map/ppermute | solution.py:90
  146.8 5.1 %collective-permute-start.33 = (bf16[24,3072]{1,0:T(8,128)(2,1)S(1)}, bf16[24,3072]{1,0:T(8,128)(2,1)S(1)}, u32[]{:S(2)}, u32[]{:S(2)}) collective-permute-start(bf16[24,3072]{1,0:T(8,128)(2,1)S(1)} %get-tuple-element.61), channel_id=1, source_target_pairs={{0,24},{4,28},{8,0},{12,4},{16,8},{20,12},{24,16},{28,20},{32,56},... | collective-permute-start | bytes 442376 | tf_op jit(solution)/shard_map/ppermute | solution.py:90
  148.8 5.5 %collective-permute-start.34 = (bf16[24,3072]{1,0:T(8,128)(2,1)S(1)}, bf16[24,3072]{1,0:T(8,128)(2,1)S(1)}, u32[]{:S(2)}, u32[]{:S(2)}) collective-permute-start(bf16[24,3072]{1,0:T(8,128)(2,1)S(1)} %get-tuple-element.61), channel_id=1, source_target_pairs={{0,16},{4,20},{8,24},{12,28},{16,0},{20,4},{24,8},{28,12},{32,48},... | collective-permute-start | bytes 442376 | tf_op jit(solution)/shard_map/ppermute | solution.py:90
  150.9 5.5 %collective-permute-start.35 = (bf16[24,3072]{1,0:T(8,128)(2,1)S(1)}, bf16[24,3072]{1,0:T(8,128)(2,1)S(1)}, u32[]{:S(2)}, u32[]{:S(2)}) collective-permute-start(bf16[24,3072]{1,0:T(8,128)(2,1)S(1)} %get-tuple-element.61), channel_id=1, source_target_pairs={{0,8},{4,12},{8,16},{12,20},{16,24},{20,28},{24,0},{28,4},{32,40},... | collective-permute-start | bytes 442376 | tf_op jit(solution)/shard_map/ppermute | solution.py:90
  156.6 27.6 %collective-permute-start.39 = (bf16[4,24,3072]{2,1,0:T(8,128)(2,1)S(1)}, bf16[4,24,3072]{2,1,0:T(8,128)(2,1)S(1)}, u32[]{:S(2)}, u32[]{:S(2)}) collective-permute-start(bf16[4,24,3072]{2,1,0:T(8,128)(2,1)S(1)} %constant_dynamic-slice_fusion.1), channel_id=1, source_target_pairs={{0,4},{4,0},{8,12},{12,8},{16,20},{20,16},{24,28},{28,24},{32,36},... | collective-permute-start | bytes 1769480 | tf_op jit(solution)/shard_map/ppermute | solution.py:90
  163.1 16.1 %collective-permute-start.41 = (bf16[4,24,3072]{2,1,0:T(8,128)(2,1)S(1)}, bf16[4,24,3072]{2,1,0:T(8,128)(2,1)S(1)}, u32[]{:S(2)}, u32[]{:S(2)}) collective-permute-start(bf16[4,24,3072]{2,1,0:T(8,128)(2,1)S(1)} %constant_dynamic-slice_fusion.1), channel_id=1, source_target_pairs={{0,32},{4,36},{8,40},{12,44},{16,48},{20,52},{24,56},{28,60},{32,6... | collective-permute-start | bytes 1769480 | tf_op jit(solution)/shard_map/ppermute | solution.py:90
  164.1 18.1 %collective-permute-start.45 = (bf16[4,24,3072]{2,1,0:T(8,128)(2,1)S(1)}, bf16[4,24,3072]{2,1,0:T(8,128)(2,1)S(1)}, u32[]{:S(2)}, u32[]{:S(2)}) collective-permute-start(bf16[4,24,3072]{2,1,0:T(8,128)(2,1)S(1)} %constant_dynamic-slice_fusion.1), channel_id=1, source_target_pairs={{0,96},{4,100},{8,104},{12,108},{16,112},{20,116},{24,120},{28,124... | collective-permute-start | bytes 1769480 | tf_op jit(solution)/shard_map/ppermute | solution.py:90
  165.8 15.5 %collective-permute-start.43 = (bf16[4,24,3072]{2,1,0:T(8,128)(2,1)S(1)}, bf16[4,24,3072]{2,1,0:T(8,128)(2,1)S(1)}, u32[]{:S(2)}, u32[]{:S(2)}) collective-permute-start(bf16[4,24,3072]{2,1,0:T(8,128)(2,1)S(1)} %constant_dynamic-slice_fusion), channel_id=1, source_target_pairs={{0,8},{4,12},{8,16},{12,20},{16,24},{20,28},{24,0},{28,4},{32,40},... | collective-permute-start | bytes 1769480 | tf_op jit(solution)/shard_map/ppermute | solution.py:90
  165.8 16.6 %collective-permute-start.47 = (bf16[4,24,3072]{2,1,0:T(8,128)(2,1)S(1)}, bf16[4,24,3072]{2,1,0:T(8,128)(2,1)S(1)}, u32[]{:S(2)}, u32[]{:S(2)}) collective-permute-start(bf16[4,24,3072]{2,1,0:T(8,128)(2,1)S(1)} %constant_dynamic-slice_fusion), channel_id=1, source_target_pairs={{0,24},{4,28},{8,0},{12,4},{16,8},{20,12},{24,16},{28,20},{32,56},... | collective-permute-start | bytes 1769480 | tf_op jit(solution)/shard_map/ppermute | solution.py:90
  179.2 9.4 %collective-permute-start.40 = (bf16[4,24,3072]{2,1,0:T(8,128)(2,1)S(1)}, bf16[4,24,3072]{2,1,0:T(8,128)(2,1)S(1)}, u32[]{:S(2)}, u32[]{:S(2)}) collective-permute-start(bf16[4,24,3072]{2,1,0:T(8,128)(2,1)S(1)} %constant_dynamic-slice_fusion), channel_id=1, source_target_pairs={{0,4},{4,0},{8,12},{12,8},{16,20},{20,16},{24,28},{28,24},{32,36},... | collective-permute-start | bytes 1769480 | tf_op jit(solution)/shard_map/ppermute | solution.py:90
  181.3 15.7 %collective-permute-start.49 = (bf16[2,24,3072]{2,1,0:T(8,128)(2,1)S(1)}, bf16[2,24,3072]{2,1,0:T(8,128)(2,1)S(1)}, u32[]{:S(2)}, u32[]{:S(2)}) collective-permute-start(bf16[2,24,3072]{2,1,0:T(8,128)(2,1)S(1)} %slice.128), channel_id=1, source_target_pairs={{0,32},{4,36},{8,40},{12,44},{16,48},{20,52},{24,56},{28,60},{32,6... | collective-permute-start | bytes 884744 | tf_op jit(solution)/shard_map/ppermute | solution.py:90
  182.3 14.9 %collective-permute-start.51 = (bf16[2,24,3072]{2,1,0:T(8,128)(2,1)S(1)}, bf16[2,24,3072]{2,1,0:T(8,128)(2,1)S(1)}, u32[]{:S(2)}, u32[]{:S(2)}) collective-permute-start(bf16[2,24,3072]{2,1,0:T(8,128)(2,1)S(1)} %slice.129), channel_id=1, source_target_pairs={{0,8},{4,12},{8,16},{12,20},{16,24},{20,28},{24,0},{28,4},{32,40},... | collective-permute-start | bytes 884744 | tf_op jit(solution)/shard_map/ppermute | solution.py:90
  182.4 15.1 %collective-permute-start.53 = (bf16[2,24,3072]{2,1,0:T(8,128)(2,1)S(1)}, bf16[2,24,3072]{2,1,0:T(8,128)(2,1)S(1)}, u32[]{:S(2)}, u32[]{:S(2)}) collective-permute-start(bf16[2,24,3072]{2,1,0:T(8,128)(2,1)S(1)} %slice.130), channel_id=1, source_target_pairs={{0,96},{4,100},{8,104},{12,108},{16,112},{20,116},{24,120},{28,124... | collective-permute-start | bytes 884744 | tf_op jit(solution)/shard_map/ppermute | solution.py:90
  184.2 13.5 %collective-permute-start.55 = (bf16[2,24,3072]{2,1,0:T(8,128)(2,1)S(1)}, bf16[2,24,3072]{2,1,0:T(8,128)(2,1)S(1)}, u32[]{:S(2)}, u32[]{:S(2)}) collective-permute-start(bf16[2,24,3072]{2,1,0:T(8,128)(2,1)S(1)} %slice.131), channel_id=1, source_target_pairs={{0,24},{4,28},{8,0},{12,4},{16,8},{20,12},{24,16},{28,20},{32,56},... | collective-permute-start | bytes 884744 | tf_op jit(solution)/shard_map/ppermute | solution.py:90
  188.6 4.3 %collective-permute-start.42 = (bf16[4,24,3072]{2,1,0:T(8,128)(2,1)S(1)}, bf16[4,24,3072]{2,1,0:T(8,128)(2,1)S(1)}, u32[]{:S(2)}, u32[]{:S(2)}) collective-permute-start(bf16[4,24,3072]{2,1,0:T(8,128)(2,1)S(1)} %collective-permute-done.41), channel_id=1, source_target_pairs={{0,4},{4,0},{8,12},{12,8},{16,20},{20,16},{24,28},{28,24},{32,36},... | collective-permute-start | bytes 1769480 | tf_op jit(solution)/shard_map/ppermute | solution.py:90
  197.2 4.3 %collective-permute-start.50 = (bf16[2,24,3072]{2,1,0:T(8,128)(2,1)S(1)}, bf16[2,24,3072]{2,1,0:T(8,128)(2,1)S(1)}, u32[]{:S(2)}, u32[]{:S(2)}) collective-permute-start(bf16[2,24,3072]{2,1,0:T(8,128)(2,1)S(1)} %collective-permute-done.49), channel_id=1, source_target_pairs={{0,4},{4,0},{8,12},{12,8},{16,20},{20,16},{24,28},{28,24},{32,36},... | collective-permute-start | bytes 884744 | tf_op jit(solution)/shard_map/ppermute | solution.py:90
  197.5 5.5 %collective-permute-start.52 = (bf16[2,24,3072]{2,1,0:T(8,128)(2,1)S(1)}, bf16[2,24,3072]{2,1,0:T(8,128)(2,1)S(1)}, u32[]{:S(2)}, u32[]{:S(2)}) collective-permute-start(bf16[2,24,3072]{2,1,0:T(8,128)(2,1)S(1)} %collective-permute-done.51), channel_id=1, source_target_pairs={{0,4},{4,0},{8,12},{12,8},{16,20},{20,16},{24,28},{28,24},{32,36},... | collective-permute-start | bytes 884744 | tf_op jit(solution)/shard_map/ppermute | solution.py:90
  197.7 6.8 %collective-permute-start.54 = (bf16[2,24,3072]{2,1,0:T(8,128)(2,1)S(1)}, bf16[2,24,3072]{2,1,0:T(8,128)(2,1)S(1)}, u32[]{:S(2)}, u32[]{:S(2)}) collective-permute-start(bf16[2,24,3072]{2,1,0:T(8,128)(2,1)S(1)} %collective-permute-done.53), channel_id=1, source_target_pairs={{0,4},{4,0},{8,12},{12,8},{16,20},{20,16},{24,28},{28,24},{32,36},... | collective-permute-start | bytes 884744 | tf_op jit(solution)/shard_map/ppermute | solution.py:90
  198.0 7.9 %collective-permute-start.56 = (bf16[2,24,3072]{2,1,0:T(8,128)(2,1)S(1)}, bf16[2,24,3072]{2,1,0:T(8,128)(2,1)S(1)}, u32[]{:S(2)}, u32[]{:S(2)}) collective-permute-start(bf16[2,24,3072]{2,1,0:T(8,128)(2,1)S(1)} %collective-permute-done.55), channel_id=1, source_target_pairs={{0,4},{4,0},{8,12},{12,8},{16,20},{20,16},{24,28},{28,24},{32,36},... | collective-permute-start | bytes 884744 | tf_op jit(solution)/shard_map/ppermute | solution.py:90
  (22 other events, 297.4 us)

commit v3 on v2

--- a/solution.py
+++ b/solution.py
@@ -27,9 +27,10 @@
 
 
 NOTE = 8
-
-
-def product_kernel(x_first, side, own, other, own_cols, other_cols, out):
+STATE_SCALE = 2.0**14
+
+
+def product_kernel(x_first, side, own, other, own_cols, other_cols, extra, out):
     dims = (((0,), (0,)), ((), ()))
     value = lax.dot_general(own[...], own_cols[...], dims, preferred_element_type=jnp.float32)
     value += lax.dot_general(other[...], other_cols[...], dims, preferred_element_type=jnp.float32)
@@ -37,6 +38,19 @@
     power = jnp.ceil(jnp.log2(jnp.maximum(peak, 1e-30))) + 1.0
     value = value * jnp.exp2(15.0 - power)
     rows, cols = value.shape
+    bias = sum(jnp.sum(r[...].astype(jnp.float32), axis=0, keepdims=True) for r in (own_cols, other_cols))
+    bias_power = jnp.ceil(jnp.log2(jnp.maximum(jnp.abs(bias), 1e-30))) + 1.0
+    rest = bias * jnp.exp2(15.0 - bias_power)
+    lines = [power]
+    for _ in range(2):
+        piece = rest.astype(jnp.bfloat16).astype(jnp.float32)
+        lines.append(piece)
+        rest = rest - piece
+    lines += [rest, bias_power]
+    row = lax.broadcasted_iota(jnp.int32, (NOTE, cols), 0)
+    note = extra[...]
+    for at, line in enumerate(lines):
+        note = jnp.where(row == at, line, note)
     block = rows // X
     small = block // Z
     for i in range(X):
@@ -46,10 +60,10 @@
             for j in range(X):
                 at = j * block + i * small
                 out[i, j * small : (j + 1) * small, :] = value[at : at + small]
-        out[i, block:, :] = jnp.broadcast_to(power, (NOTE, cols))
-
-
-def chip_product(attn_own, attn_other, cotangent, start, other_cols, x_first):
+        out[i, block:, :] = note
+
+
+def chip_product(attn_own, attn_other, cotangent, start, other_cols, extra, x_first):
     tokens, rows = attn_own.shape
     cols = other_cols.shape[1]
     step = 512
@@ -65,6 +79,7 @@
                 whole,
                 pl.BlockSpec((tokens, step), lambda n, side: (0, side[0] + n)),
                 pl.BlockSpec((tokens, step), lambda n, side: (0, n)),
+                pl.BlockSpec((NOTE, step), lambda n, side: (0, n)),
             ],
             out_specs=pl.BlockSpec((*shape[:2], step), lambda n, side: (0, 0, n)),
         ),
@@ -73,7 +88,7 @@
             dimension_semantics=("arbitrary",), vmem_limit_bytes=40 * 2**20
         ),
         cost_estimate=pl.CostEstimate(flops=1, bytes_accessed=1, transcendentals=0),
-    )((start // step).reshape(1).astype(jnp.int32), attn_own, attn_other, cotangent, other_cols)
+    )((start // step).reshape(1).astype(jnp.int32), attn_own, attn_other, cotangent, other_cols, extra)
 
 
 def place(x, z, c):
@@ -116,11 +131,20 @@
     return lax.dynamic_index_in_dim(array, index % array.shape[axis], axis, keepdims=False)
 
 
-def scatter_sum(blocks, axis, me, move):
-    total = pick(blocks, axis, me)
+def turn(array, me, axis):
+    back = jnp.flip(array, axis)
+    size = array.shape[axis]
+    twice = jnp.concatenate([back, lax.slice_in_dim(back, 0, size - 1, axis=axis)], axis=axis)
+    return lax.dynamic_slice_in_dim(twice, size - 1 - me, size, axis=axis)
+
+
+def scatter_sum(blocks, me, rows, move):
+    own = pick(blocks, 0, me)
+    total, rest = own[:rows], {0: own[rows:]}
     for d in (2, 1, 3):
-        total = total + move(pick(blocks, axis, me + d), d)
-    return total
+        got = move(pick(blocks, 0, me + d), d)
+        total, rest[d] = total + got[:rows], got[rows:]
+    return total, [rest[d] for d in range(4)]
 
 
 def coded_pieces(blocks, me):
@@ -130,14 +154,28 @@
 def decoded(piece):
     piece = piece.astype(jnp.float32)
     rows = piece.shape[0] - NOTE
-    return piece[:rows] * jnp.exp2(piece[rows : rows + 1] - 15.0)
-
-
-def coded_sum(blocks, pieces, me, move):
-    total = decoded(pick(blocks, 0, me))
+    note = [piece[rows + i : rows + i + 1] for i in range(5)]
+    value = piece[:rows] * jnp.exp2(note[0] - 15.0)
+    return value, (note[1] + note[2] + note[3]) * jnp.exp2(note[4] - 15.0)
+
+
+def coded_sum(blocks, pieces, me, move, entries):
+    own = pick(blocks, 0, me)
+    total, bias = decoded(own)
+    noted = {0: own[5 - NOTE :, :entries]}
     for d, piece in zip((2, 1, 3), pieces):
-        total = total + decoded(move(piece, d))
-    return total.reshape(X, -1, total.shape[1])
+        got = move(piece, d)
+        value, line = decoded(got)
+        total, bias = total + value, bias + line
+        noted[d] = got[5 - NOTE :, :entries].astype(jnp.float32)
+    cols = total.shape[1]
+    lines = [bias]
+    if entries:
+        lines.append(jnp.stack([jnp.sum(noted[d], axis=0) for d in range(4)]).reshape(-1, cols))
+    below = jnp.concatenate(lines, axis=0)
+    below = jnp.pad(below, ((0, 8 - below.shape[0]), (0, 0)))
+    below = jnp.broadcast_to(below[None], (X, 8, cols))
+    return jnp.concatenate([total.reshape(X, -1, cols), below], axis=1)
 
 
 def gather_line(own, me, move):
@@ -158,28 +196,44 @@
     )()
 
 
+def by_core(own, twin, axis, c):
+    own, twin = jnp.expand_dims(own, axis), jnp.expand_dims(twin, axis)
+    shape = [1] * own.ndim
+    shape[axis] = C
+    return jnp.where(lax.broadcasted_iota(jnp.int32, shape, axis) == c, own, twin)
+
+
 def gather_plane(rows, x, z, c):
     count, width = rows.shape
     half = width // 2
     full = blank((X, Z, C, count, width), rows.dtype)
-    lines = [gather_line(rows[:, :half], z, along_z), gather_line(rows[:, half:], x, along_x)]
-    lines = lax.optimization_barrier(lines)
-    moves = (along_x, along_z)
-    near = [(which, d, moves[which](lines[which], d)) for d in (1, -1) for which in (0, 1)]
+    line_a = gather_line(rows[:, :half], z, along_z)
+    line_b = gather_line(rows[:, half:], x, along_x)
+    line_a, line_b = lax.optimization_barrier((line_a, line_b))
+    lines, moves = (line_a, line_b), (along_x, along_z)
+
+    def put(full, which, d, low, part, twin):
+        zero, low, start = jnp.int32(0), jnp.int32(low), jnp.int32(which * half)
+        piece = by_core(part, twin, 1, c)
+        if which == 0:
+            piece, at = piece[None], ((x - d) % X, low, zero, zero, start)
+        else:
+            piece, at = piece[:, None], (low, (z - d) % Z, zero, zero, start)
+        return lax.dynamic_update_slice(full, piece, at)
+
+    near = [(i, d, moves[i](lines[i], d)) for d in (1, -1) for i in (0, 1)]
+    for i in (0, 1):
+        full = put(full, i, 0, 0, lines[i], shift(lines[i], dc=1))
+    near_parts, full = lax.optimization_barrier(([part for _, _, part in near], full))
     far = []
-    for which, d, line in near:
+    for (i, d, _), part in zip(near, near_parts):
         low = 0 if d == 1 else 2
-        far.append((which, 2, low, moves[which](line[low : low + 2], d)))
-    parts = [(which, 0, 0, lines[which]) for which in (0, 1)]
-    parts += [(which, d, 0, line) for which, d, line in near]
-    for which, d, low, part in parts + far:
-        zero, start = jnp.int32(0), jnp.int32(which * half)
-        for side, piece in ((c, part), (1 - c, shift(part, dc=1))):
-            if which == 0:
-                piece, at = piece[None, :, None], ((x - d) % X, jnp.int32(low))
-            else:
-                piece, at = piece[:, None, None], (jnp.int32(low), (z - d) % Z)
-            full = lax.dynamic_update_slice(full, piece, (*at, side, zero, start))
+        far.append((i, low, moves[i](part[low : low + 2], d)))
+    for (i, d, _), part in zip(near, near_parts):
+        full = put(full, i, d, 0, part, shift(part, dc=1))
+    far_parts, full = lax.optimization_barrier(([part for _, _, part in far], full))
+    for (i, low, _), part in zip(far, far_parts):
+        full = put(full, i, 2, low, part, shift(part, dc=1))
     return full.reshape(X * Z * C * count, width)
 
 
@@ -215,36 +269,53 @@
     held, sent[0] = lax.optimization_barrier((cotangent, sent[0]))
     sent.append(lax.dynamic_slice(held, (0, (1 - c) * half + quarter), (tokens, quarter)))
     others = [shift(part, dc=1) for part in sent]
-    bias_term = jnp.sum(held, axis=0, dtype=jnp.float32)
-
-    others[0], bias_term = lax.optimization_barrier((others[0], bias_term))
+    count = master_bias.shape[0]
+    rest = jnp.concatenate([master_bias, moment_bias, second_bias, teacher_bias])[None] * STATE_SCALE
+    state = []
+    for _ in range(2):
+        state.append(lax.reduce_precision(rest, 8, 7))
+        rest = rest - state[-1]
+    state = jnp.concatenate([*state, rest], axis=0)
+    entries = state.shape[1]
+    extras = [jnp.pad(state, ((NOTE - 3, 0), (0, quarter - entries))), jnp.zeros((NOTE, quarter), jnp.float32)]
 
     def blocks_of(which):
         start = c * half + which * quarter
-        return chip_product(attn_out, attn_other, cotangent, start, others[which], which == 0)
+        return chip_product(attn_out, attn_other, cotangent, start, others[which], extras[which], which == 0)
 
     blocks_a = blocks_of(0)
     pieces_a = coded_pieces(blocks_a, x)
     others[1], pieces_a = lax.optimization_barrier((others[1], pieces_a))
     blocks_b = blocks_of(1)
     pieces_b = coded_pieces(blocks_b, z)
-    part_a = coded_sum(blocks_a, pieces_a, x, along_x)
-    part_b = coded_sum(blocks_b, pieces_b, z, along_z)
-    grads = [scatter_sum(part_a, 0, z, along_z), scatter_sum(part_b, 0, x, along_x)]
-    sums = [squares(g) for g in grads]
-    chip_grad = jnp.concatenate(grads, axis=1).reshape(C, own_rows, half)
+    part_a = coded_sum(blocks_a, pieces_a, x, along_x, entries)
+    part_b = coded_sum(blocks_b, pieces_b, z, along_z, 0)
+    rows = own_rows * C
+    grad_a, noted = scatter_sum(part_a, z, rows + 1, along_z)
+    grad_b, _ = scatter_sum(part_b, x, rows + 1, along_x)
+    grads = [grad_a, grad_b]
+    used = X * entries // quarter
+    own_state = jnp.stack([n[:used] for n in noted]).reshape(-1, half)
+    sums = [squares(g[:rows]) for g in grads]
+    bias_half = jnp.concatenate([g[rows : rows + 1] for g in grads], axis=1)
+    chip_grad = jnp.concatenate([g[:rows] for g in grads], axis=1).reshape(C, own_rows, half)
     own_half = pick(chip_grad, 0, c)
-    other_half = shift(pick(chip_grad, 0, 1 - c), dc=1)
-    first = jnp.where(c == 0, own_half, other_half)
-    last = jnp.where(c == 0, other_half, own_half)
-    weight_grad = jnp.concatenate([first, last], axis=1)
-
-    count = master_bias.shape[0]
-    state = jnp.stack([master_bias, moment_bias, second_bias, teacher_bias])
-    spread = lax.dynamic_update_slice(jnp.zeros((4, width), jnp.float32), state, (0, index * count))
-    packed = jnp.concatenate([bias_term.reshape(-1, 128), spread.reshape(-1, 128)], axis=0)
-    packed = all_sum(packed, ("core", "x", "z")).reshape(5, width)
-    bias_grad, bias_state = packed[0], packed[1:]
+    other_half = pick(chip_grad, 0, 1 - c)
+    below = jnp.concatenate([bias_half, own_state], axis=0)
+    below = jnp.pad(below, ((0, -below.shape[0] % 8), (0, 0)))
+    got = shift(jnp.concatenate([other_half, below], axis=0), dc=1)
+    other_half, bias_other = got[:own_rows], got[own_rows : own_rows + 1]
+    other_state = got[own_rows + 1 : own_rows + 1 + own_state.shape[0]]
+    all_state = by_core(*(a.reshape(Z, X, 4, count) for a in (own_state, other_state)), 3, c)
+    all_state = turn(turn(all_state, z, 0), x, 1) * (1.0 / STATE_SCALE)
+    bias_state = all_state.transpose(2, 1, 0, 3, 4).reshape(4, width)
+
+    def in_order(own, other):
+        first, last = jnp.where(c == 0, own, other), jnp.where(c == 0, other, own)
+        return jnp.concatenate([first, last], axis=1)
+
+    weight_grad = in_order(own_half, other_half)
+    bias_grad = in_order(bias_half, bias_other)[0]
 
     sq_norm = jnp.sum(all_sum(sums[0] + sums[1], ("core", "x", "z", "y")))
     sq_norm = sq_norm + jnp.sum(bias_grad * bias_grad)
@@ -259,10 +330,19 @@
         clip_factor,
         decay_rate,
     )
-    bias_new = adamw_update(bias_grad, *bias_state, clip_factor, 0.0)
-    own_bias = [lax.dynamic_slice(b, (index * count,), (count,)) for b in bias_new]
-    full_bias = bias_new[3].astype(jnp.bfloat16)
-    full_weight = gather_plane(teacher_w.astype(jnp.bfloat16), x, z, c)
+    own_bias = adamw_update(
+        lax.dynamic_slice(bias_grad, (index * count,), (count,)),
+        master_bias,
+        moment_bias,
+        second_bias,
+        teacher_bias,
+        clip_factor,
+        0.0,
+    )
+    full_bias = adamw_update(bias_grad, *bias_state, clip_factor, 0.0)[3].astype(jnp.bfloat16)
+    teacher_half = teacher_w.astype(jnp.bfloat16)
+    teacher_half, own_bias, full_bias = lax.optimization_barrier((teacher_half, own_bias, full_bias))
+    full_weight = gather_plane(teacher_half, x, z, c)
     return (master_w, moment_w, second_w, teacher_w, *own_bias, full_weight, full_bias)
 
 

time: 207 us -> 191 us (0.923)
  local copies, waits for them, and re-layouts: 31.6 us -> 10.6 us
  other arithmetic: 20.2 us -> 39.4 us
  starting transfers between devices: 80.8 us -> 65.3 us
    ppermute x54 -> x47, starting transfers between devices: 77 us -> 60.3 us  [shift(): return lax.ppermute(array, 'dp', pairs)]
    dynamic_update_slice x21 -> x0, local copies, waits for them, and re-layouts: 16.4 us -> none  [the longest x20 16.1 us: gather_plane(): full = lax.dynamic_update_slice(full, piece, (*at, side, zero, start))]
    dynamic_update_slice x0 -> x10, other arithmetic: none -> 13.3 us  [put(): return lax.dynamic_update_slice(full, piece, at)]
    reduce_sum x1 -> x4, other arithmetic: 6.39 us -> 2.24 us  [coded_sum(): jnp.sum(noted[d], axis=0)]
    add x2 -> x7, other arithmetic: 3.52 us -> 7.42 us  [the longest x4 5.69 us: coded_sum(): total, bias = (total + value, bias + line)]
    convert_element_type x6, other arithmetic: 0.8 us -> 4.02 us  [decoded(): piece = piece.astype(jnp.float32)]
    unnamed x36 -> x46, local copies, waits for them, and re-layouts: 4.63 us -> 1.43 us
    squeeze x0 -> x2, other arithmetic: none -> 2.99 us  [pick(): lax.dynamic_index_in_dim(array, index % array.shape[axis], axis, keepdims...]
  transfers between devices with their start and end apart: 57 -> 50, of which waited for: 20 -> 21; matrix products, arithmetic and copies ran while one was open for 19% -> 19% of each run, Pallas kernels for 4% -> 8%
where the time goes in v3:
time: 191 us; the launch traced here: 190 us
  starting transfers between devices  65.3 us (34%)
  waiting for transfers between devices  55.9 us (29%)
  other arithmetic  39.4 us (21%)
  Pallas kernels  16 us (8%)
  local copies, waits for them, and re-layouts  10.6 us (6%)
  between operations  2.89 us (2%)
    ppermute x47, starting transfers between devices, shift(): return lax.ppermute(array, 'dp', pairs)  60.3 us
    ppermute x47, waiting for transfers between devices, shift(): return lax.ppermute(array, 'dp', pairs)  54.6 us
    pallas_call x2, Pallas kernels, chip_product(): pl.pallas_call(functools.partial(product_kernel, x_first), grid_spec=pltp...  16 us
    dynamic_update_slice x10, other arithmetic, put(): return lax.dynamic_update_slice(full, piece, at)  13.3 us
    add x4, other arithmetic, coded_sum(): total, bias = (total + value, bias + line)  5.69 us
    ppermute x3, starting transfers between devices, shift_y(): return lax.ppermute(array, 'mp', [(y, (y + dy) % Y) for y in range(Y)])  5.05 us
    convert_element_type x6, other arithmetic, decoded(): piece = piece.astype(jnp.float32)  4.02 us
    dynamic_slice x1, local copies, waits for them, and re-layouts, per_device(): lax.dynamic_slice(held, (0, (1 - c) * half + quarter), (tokens, quarter))  3.87 us
  transfers between devices with their start and end apart: 50, of which 21 were waited for; matrix products, arithmetic and copies ran while one was open for 19% of the time, Pallas kernels for 8%

profile of v3, /device:TPU:1, one launch (start us, length us, event | category | flops | bytes accessed | tf_op | source)
XLA Modules:
  0.0 190.0 jit_solution(10130327674194772773)
XLA Ops:
  0.7 3.7 %constant_dynamic-slice_fusion.13 = bf16[1024,1536]{1,0:T(8,128)(2,1)} fusion(bf16[1024,6144]{1,0:T(8,128)(2,1)} %own_cols.3, s32[]{:T(128)S(6)} %select_n.316), kind=kLoop, calls=%fused_computation.152 | loop fusion | bytes 6291460 | tf_op jit(solution)/shard_map/dynamic_slice | solution.py:265
  4.4 1.4 collective-permute-start.1
  5.8 3.9 %constant_dynamic-slice_fusion.12 = bf16[1024,1536]{1,0:T(8,128)(2,1)} fusion(bf16[1024,6144]{1,0:T(8,128)(2,1)} %own_cols.3, s32[]{:T(128)S(6)} %select_n.320), kind=kLoop, calls=%fused_computation.151 | loop fusion | bytes 6291460 | tf_op jit(solution)/shard_map/dynamic_slice | solution.py:270
  10.4 5.2 %collective-permute-done.other = bf16[1024,768]{1,0:T(8,128)(2,1)S(1)} collective-permute-done((bf16[1024,768]{1,0:T(8,128)(2,1)S(1)}, bf16[1024,768]{1,0:T(8,128)(2,1)S(1)}, u32[]{:S(2)}, u32[]{:S(2)}) %collective-permute-start) | collective-permute-done | bytes 1572896 | tf_op jit(solution)/shard_map/ppermute | solution.py:105
  15.6 8.0 %shard_map.177 = f32[4,200,1536]{2,1,0:T(8,128)S(1)} custom-call(s32[1]{0:T(128)} %bitcast.side, bf16[1024,768]{1,0:T(8,128)(2,1)S(1)} %copy-done.2, bf16[1024,768]{1,0:T(8,128)(2,1)S(1)} %collective-permute-done.other, bf16[1024,6144]{1,0:T(8,128)(2,1)} %own_cols.3, bf16[1024,1536]{1,0:T(8,128)(2,1)} %collective-permute-done.1.other_cols, ...), custom_call_target="tpu_custom_call" | custom-call | flops 1 | bytes 1 | tf_op jit(solution)/shard_map/pallas_call | solution.py:72
  23.6 2.0 %dynamic-slice_bitcast_fusion = (f32[200,1536]{1,0:T(8,128)}, f16[200,1536]{1,0:T(8,128)(2,1)}, f16[200,1536]{1,0:T(8,128)(2,1)}, f16[200,1536]{1,0:T(8,128)(2,1)}) fusion(f32[4,200,1536]{2,1,0:T(8,128)S(1)} %shard_map.177, s32[]{:T(128)S(6)} %select_n.319, s32[]{:T(128)S(6)} %select_n.326, s32[]{:T(128)S(6)} %select_n.324, s32[]{:T(128)S(6)} %select_n.322), kind=kLoop, calls=%fused_computation.22 | loop fusion | flops 921600 | bytes 7987216 | tf_op jit(solution)/shard_map/jit(dynamic_index_in_dim)/squeeze | solution.py:131
  28.0 1.4 collective-permute-start.5
  29.4 1.6 collective-permute-start.3
  31.1 8.0 %shard_map.178 = f32[4,200,1536]{2,1,0:T(8,128)S(1)} custom-call(s32[1]{0:T(128)} %bitcast.17.side, bf16[1024,768]{1,0:T(8,128)(2,1)S(1)} %copy-done.2, bf16[1024,768]{1,0:T(8,128)(2,1)S(1)} %collective-permute-done.other, bf16[1024,6144]{1,0:T(8,128)(2,1)} %own_cols.3, bf16[1024,1536]{1,0:T(8,128)(2,1)} %collective-permute-done.2.other_cols, ...), custom_call_target="tpu_custom_call" | custom-call | flops 1 | bytes 1 | tf_op jit(solution)/shard_map/pallas_call | solution.py:72
  39.9 1.8 fusion.11
  41.7 3.6 %collective-permute-start.9 = (f16[200,1536]{1,0:T(8,128)(2,1)}, f16[200,1536]{1,0:T(8,128)(2,1)S(1)}, u32[]{:S(2)}, u32[]{:S(2)}) collective-permute-start(f16[200,1536]{1,0:T(8,128)(2,1)} %get-tuple-element.73), channel_id=1, source_target_pairs={{0,16},{4,20},{8,24},{12,28},{16,0},{20,4},{24,8},{28,12},{32,48},... | collective-permute-start | bytes 1843208 | tf_op jit(solution)/shard_map/ppermute | solution.py:105
  46.9 2.0 %collective-permute-start.11 = (f16[200,1536]{1,0:T(8,128)(2,1)}, f16[200,1536]{1,0:T(8,128)(2,1)}, u32[]{:S(2)}, u32[]{:S(2)}) collective-permute-start(f16[200,1536]{1,0:T(8,128)(2,1)} %get-tuple-element.74), channel_id=1, source_target_pairs={{0,24},{4,28},{8,0},{12,4},{16,8},{20,12},{24,16},{28,20},{32,56},... | collective-permute-start | bytes 1843208 | tf_op jit(solution)/shard_map/ppermute | solution.py:105
  51.5 6.0 %collective-permute-done.3 = f16[200,1536]{1,0:T(8,128)(2,1)S(1)} collective-permute-done((f16[200,1536]{1,0:T(8,128)(2,1)}, f16[200,1536]{1,0:T(8,128)(2,1)S(1)}, u32[]{:S(2)}, u32[]{:S(2)}) %collective-permute-start.3) | collective-permute-done | bytes 614432 | tf_op jit(solution)/shard_map/ppermute | solution.py:105
  58.7 1.8 fusion.4
  63.0 3.6 %collective-permute-start.6 = (f32[56,1536]{1,0:T(8,128)}, f32[56,1536]{1,0:T(8,128)S(1)}, u32[]{:S(2)}, u32[]{:S(2)}) collective-permute-start(f32[56,1536]{1,0:T(8,128)} %get-tuple-element.77), channel_id=1, source_target_pairs={{0,16},{4,20},{8,24},{12,28},{16,0},{20,4},{24,8},{28,12},{32,48},... | collective-permute-start | bytes 1032200 | tf_op jit(solution)/shard_map/ppermute | solution.py:105
  67.3 7.0 %collective-permute-done.10 = f16[200,1536]{1,0:T(8,128)(2,1)S(1)} collective-permute-done((f16[200,1536]{1,0:T(8,128)(2,1)}, f16[200,1536]{1,0:T(8,128)(2,1)S(1)}, u32[]{:S(2)}, u32[]{:S(2)}) %collective-permute-start.10) | collective-permute-done | bytes 614432 | tf_op jit(solution)/shard_map/ppermute | solution.py:105
  77.0 1.8 fusion
  79.8 1.4 collective-permute-start.12
  81.3 2.7 %collective-permute-start.14 = (f32[56,1536]{1,0:T(8,128)}, f32[56,1536]{1,0:T(8,128)S(1)}, u32[]{:S(2)}, u32[]{:S(2)}) collective-permute-start(f32[56,1536]{1,0:T(8,128)} %get-tuple-element.82), channel_id=1, source_target_pairs={{0,96},{4,100},{8,104},{12,108},{16,112},{20,116},{24,120},{28,124... | collective-permute-start | bytes 1032200 | tf_op jit(solution)/shard_map/ppermute | solution.py:105
  84.1 3.7 %collective-permute-done.7 = f32[56,1536]{1,0:T(8,128)S(1)} collective-permute-done((f32[56,1536]{1,0:T(8,128)}, f32[56,1536]{1,0:T(8,128)S(1)}, u32[]{:S(2)}, u32[]{:S(2)}) %collective-permute-start.7) | collective-permute-done | bytes 344096 | tf_op jit(solution)/shard_map/ppermute | solution.py:105
  87.9 1.5 collective-permute-done.12
  89.5 9.5 %collective-permute-done.13 = f32[56,1536]{1,0:T(8,128)} collective-permute-done((f32[56,1536]{1,0:T(8,128)}, f32[56,1536]{1,0:T(8,128)}, u32[]{:S(2)}, u32[]{:S(2)}) %collective-permute-start.13) | collective-permute-done | bytes 344096 | tf_op jit(solution)/shard_map/ppermute | solution.py:105
  101.7 1.7 collective-permute-start.17
  103.5 1.6 collective-permute-start.18
  106.2 1.5 collective-permute-start.19
  107.7 3.1 %collective-permute-start.20 = (f32[8,128]{1,0:T(8,128)S(1)}, f32[8,128]{1,0:T(8,128)S(1)}, u32[]{:S(2)}, u32[]{:S(2)}) collective-permute-start(f32[8,128]{1,0:T(8,128)S(1)} %add_add_fusion.1), channel_id=1, source_target_pairs={{0,16},{4,20},{8,24},{12,28},{16,0},{20,4},{24,8},{28,12},{32,48},... | collective-permute-start | bytes 12296 | tf_op jit(solution)/shard_map/ppermute | solution.py:105
  110.8 2.4 %collective-permute-start.25 = (f32[32,3072]{1,0:T(8,128)S(1)}, f32[32,3072]{1,0:T(8,128)S(1)}, u32[]{:S(2)}, u32[]{:S(2)}) collective-permute-start(f32[32,3072]{1,0:T(8,128)S(1)} %select_maximum_fusion), channel_id=1, source_target_pairs={{0,4},{4,0},{8,12},{12,8},{16,20},{20,16},{24,28},{28,24},{32,36},... | collective-permute-start | bytes 1179656 | tf_op jit(solution)/shard_map/ppermute | solution.py:105
  114.9 2.6 %collective-permute-start.23 = (f32[8,128]{1,0:T(8,128)S(1)}, f32[8,128]{1,0:T(8,128)S(1)}, u32[]{:S(2)}, u32[]{:S(2)}) collective-permute-start(f32[8,128]{1,0:T(8,128)S(1)} %add_add_fusion), channel_id=1, source_target_pairs={{0,2},{1,3},{2,0},{3,1},{4,6},{5,7},{6,4},{7,5},{8,10},{9,11},{10,... | collective-permute-start | bytes 12296 | tf_op jit(solution)/shard_map/ppermute | solution.py:109
  126.3 1.7 fusion.104
  129.0 3.0 %collective-permute-start.27 = (bf16[24,3072]{1,0:T(8,128)(2,1)S(1)}, bf16[24,3072]{1,0:T(8,128)(2,1)S(1)}, u32[]{:S(2)}, u32[]{:S(2)}) collective-permute-start(bf16[24,3072]{1,0:T(8,128)(2,1)S(1)} %get-tuple-element.102), channel_id=1, source_target_pairs={{0,16},{4,20},{8,24},{12,28},{16,0},{20,4},{24,8},{28,12},{32,48},... | collective-permute-start | bytes 442376 | tf_op jit(solution)/shard_map/ppermute | solution.py:105
  131.9 2.8 %collective-permute-start.29 = (bf16[24,3072]{1,0:T(8,128)(2,1)S(1)}, bf16[24,3072]{1,0:T(8,128)(2,1)S(1)}, u32[]{:S(2)}, u32[]{:S(2)}) collective-permute-start(bf16[24,3072]{1,0:T(8,128)(2,1)S(1)} %get-tuple-element.101), channel_id=1, source_target_pairs={{0,96},{4,100},{8,104},{12,108},{16,112},{20,116},{24,120},{28,124... | collective-permute-start | bytes 442376 | tf_op jit(solution)/shard_map/ppermute | solution.py:105
  135.3 3.1 %collective-permute-done.29 = bf16[24,3072]{1,0:T(8,128)(2,1)S(1)} collective-permute-done((bf16[24,3072]{1,0:T(8,128)(2,1)S(1)}, bf16[24,3072]{1,0:T(8,128)(2,1)S(1)}, u32[]{:S(2)}, u32[]{:S(2)}) %collective-permute-start.29) | collective-permute-done | bytes 147488 | tf_op jit(solution)/shard_map/ppermute | solution.py:105
  138.5 1.9 %collective-permute-done.30 = bf16[24,3072]{1,0:T(8,128)(2,1)S(1)} collective-permute-done((bf16[24,3072]{1,0:T(8,128)(2,1)S(1)}, bf16[24,3072]{1,0:T(8,128)(2,1)S(1)}, u32[]{:S(2)}, u32[]{:S(2)}) %collective-permute-start.30) | collective-permute-done | bytes 147488 | tf_op jit(solution)/shard_map/ppermute | solution.py:105
  140.4 1.6 collective-permute-done.31
  142.2 5.3 %collective-permute-start.36 = (bf16[4,24,3072]{2,1,0:T(8,128)(2,1)S(1)}, bf16[4,24,3072]{2,1,0:T(8,128)(2,1)}, u32[]{:S(2)}, u32[]{:S(2)}) collective-permute-start(bf16[4,24,3072]{2,1,0:T(8,128)(2,1)S(1)} %constant_dynamic-slice_fusion.7), channel_id=1, source_target_pairs={{0,4},{4,0},{8,12},{12,8},{16,20},{20,16},{24,28},{28,24},{32,36},... | collective-permute-start | bytes 1769480 | tf_op jit(solution)/shard_map/ppermute | solution.py:105
  147.8 1.4 collective-permute-start.33
  149.2 2.9 %collective-permute-start.34 = (bf16[4,24,3072]{2,1,0:T(8,128)(2,1)S(1)}, bf16[4,24,3072]{2,1,0:T(8,128)(2,1)S(1)}, u32[]{:S(2)}, u32[]{:S(2)}) collective-permute-start(bf16[4,24,3072]{2,1,0:T(8,128)(2,1)S(1)} %constant_dynamic-slice_fusion.7), channel_id=1, source_target_pairs={{0,96},{4,100},{8,104},{12,108},{16,112},{20,116},{24,120},{28,124... | collective-permute-start | bytes 1769480 | tf_op jit(solution)/shard_map/ppermute | solution.py:105
  153.3 2.4 %select_dynamic-update-slice_fusion.5 = bf16[4,4,2,24,6144]{4,3,2,1,0:T(8,128)(2,1)} fusion(bf16[4,4,2,24,6144]{4,3,2,1,0:T(8,128)(2,1)} %shard_map.179, s32[]{:T(128)S(6)} %select_n.319, pred[2]{0:T(512)(128)(4,1)S(1)} %iota_compare_fusion.4, bf16[4,24,3072]{2,1,0:T(8,128)(2,1)} %collective-permute-done.36, ...), kind=kLoop, calls=%fused_computation.44 | loop fusion | flops 589824 | bytes 2359302 | tf_op jit(solution)/shard_map/dynamic_update_slice | solution.py:222
  155.7 1.4 select_dynamic-update-slice_fusion.4
  157.1 6.6 %collective-permute-done.32 = bf16[4,24,3072]{2,1,0:T(8,128)(2,1)S(1)} collective-permute-done((bf16[4,24,3072]{2,1,0:T(8,128)(2,1)S(1)}, bf16[4,24,3072]{2,1,0:T(8,128)(2,1)S(1)}, u32[]{:S(2)}, u32[]{:S(2)}) %collective-permute-start.32) | collective-permute-done | bytes 589856 | tf_op jit(solution)/shard_map/ppermute | solution.py:105
  164.3 1.9 collective-permute-done.35
  166.2 1.6 collective-permute-start.42
  171.9 2.0 %collective-permute-start.40 = (bf16[2,24,3072]{2,1,0:T(8,128)(2,1)S(1)}, bf16[2,24,3072]{2,1,0:T(8,128)(2,1)S(1)}, u32[]{:S(2)}, u32[]{:S(2)}) collective-permute-start(bf16[2,24,3072]{2,1,0:T(8,128)(2,1)S(1)} %slice.364), channel_id=1, source_target_pairs={{0,96},{4,100},{8,104},{12,108},{16,112},{20,116},{24,120},{28,124... | collective-permute-start | bytes 884744 | tf_op jit(solution)/shard_map/ppermute | solution.py:105
  173.9 1.4 select_dynamic-update-slice_fusion.2
  175.3 1.5 collective-permute-start.41
  178.2 1.4 select_dynamic-update-slice_fusion
  179.8 2.6 %collective-permute-done.41 = bf16[2,24,3072]{2,1,0:T(8,128)(2,1)S(1)} collective-permute-done((bf16[2,24,3072]{2,1,0:T(8,128)(2,1)S(1)}, bf16[2,24,3072]{2,1,0:T(8,128)(2,1)S(1)}, u32[]{:S(2)}, u32[]{:S(2)}) %collective-permute-start.41) | collective-permute-done | bytes 294944 | tf_op jit(solution)/shard_map/ppermute | solution.py:105
  182.4 2.3 %collective-permute-start.46 = (bf16[2,24,3072]{2,1,0:T(8,128)(2,1)S(1)}, bf16[2,24,3072]{2,1,0:T(8,128)(2,1)S(1)}, u32[]{:S(2)}, u32[]{:S(2)}) collective-permute-start(bf16[2,24,3072]{2,1,0:T(8,128)(2,1)S(1)} %collective-permute-done.38), channel_id=1, source_target_pairs={{0,4},{4,0},{8,12},{12,8},{16,20},{20,16},{24,28},{28,24},{32,36},... | collective-permute-start | bytes 884744 | tf_op jit(solution)/shard_map/ppermute | solution.py:105
  (214 shorter events, 44.0 us)
Async XLA Ops:
  4.4 11.2 %collective-permute-start.1 = (bf16[1024,1536]{1,0:T(8,128)(2,1)}, bf16[1024,1536]{1,0:T(8,128)(2,1)}, u32[]{:S(2)}, u32[]{:S(2)}) collective-permute-start(bf16[1024,1536]{1,0:T(8,128)(2,1)} %constant_dynamic-slice_fusion.13), channel_id=1, source_target_pairs={{0,4},{4,0},{8,12},{12,8},{16,20},{20,16},{24,28},{28,24},{32,36},... | collective-permute-start | bytes 9437192 | tf_op jit(solution)/shard_map/ppermute | solution.py:105
  9.7 17.0 %collective-permute-start.2 = (bf16[1024,1536]{1,0:T(8,128)(2,1)}, bf16[1024,1536]{1,0:T(8,128)(2,1)}, u32[]{:S(2)}, u32[]{:S(2)}) collective-permute-start(bf16[1024,1536]{1,0:T(8,128)(2,1)} %constant_dynamic-slice_fusion.12), channel_id=1, source_target_pairs={{0,4},{4,0},{8,12},{12,8},{16,20},{20,16},{24,28},{28,24},{32,36},... | collective-permute-start | bytes 9437192 | tf_op jit(solution)/shard_map/ppermute | solution.py:105
  9.7 5.9 %collective-permute-start = (bf16[1024,768]{1,0:T(8,128)(2,1)S(1)}, bf16[1024,768]{1,0:T(8,128)(2,1)S(1)}, u32[]{:S(2)}, u32[]{:S(2)}) collective-permute-start(bf16[1024,768]{1,0:T(8,128)(2,1)S(1)} %copy-done.2), channel_id=1, source_target_pairs={{0,4},{4,0},{8,12},{12,8},{16,20},{20,16},{24,28},{28,24},{32,36},... | collective-permute-start | bytes 4718600 | tf_op jit(solution)/shard_map/ppermute | solution.py:105
  26.7 20.2 %collective-permute-start.4 = (f16[200,1536]{1,0:T(8,128)(2,1)}, f16[200,1536]{1,0:T(8,128)(2,1)}, u32[]{:S(2)}, u32[]{:S(2)}) collective-permute-start(f16[200,1536]{1,0:T(8,128)(2,1)} %get-tuple-element.37), channel_id=1, source_target_pairs={{0,32},{4,36},{8,40},{12,44},{16,48},{20,52},{24,56},{28,60},{32,6... | collective-permute-start | bytes 1843208 | tf_op jit(solution)/shard_map/ppermute | solution.py:105
  28.0 22.1 %collective-permute-start.5 = (f16[200,1536]{1,0:T(8,128)(2,1)}, f16[200,1536]{1,0:T(8,128)(2,1)}, u32[]{:S(2)}, u32[]{:S(2)}) collective-permute-start(f16[200,1536]{1,0:T(8,128)(2,1)} %get-tuple-element.38), channel_id=1, source_target_pairs={{0,96},{4,100},{8,104},{12,108},{16,112},{20,116},{24,120},{28,124... | collective-permute-start | bytes 1843208 | tf_op jit(solution)/shard_map/ppermute | solution.py:105
  29.4 28.0 %collective-permute-start.3 = (f16[200,1536]{1,0:T(8,128)(2,1)}, f16[200,1536]{1,0:T(8,128)(2,1)S(1)}, u32[]{:S(2)}, u32[]{:S(2)}) collective-permute-start(f16[200,1536]{1,0:T(8,128)(2,1)} %get-tuple-element.36), channel_id=1, source_target_pairs={{0,64},{4,68},{8,72},{12,76},{16,80},{20,84},{24,88},{28,92},{32,9... | collective-permute-start | bytes 1843208 | tf_op jit(solution)/shard_map/ppermute | solution.py:105
  41.7 34.0 %collective-permute-start.9 = (f16[200,1536]{1,0:T(8,128)(2,1)}, f16[200,1536]{1,0:T(8,128)(2,1)S(1)}, u32[]{:S(2)}, u32[]{:S(2)}) collective-permute-start(f16[200,1536]{1,0:T(8,128)(2,1)} %get-tuple-element.73), channel_id=1, source_target_pairs={{0,16},{4,20},{8,24},{12,28},{16,0},{20,4},{24,8},{28,12},{32,48},... | collective-permute-start | bytes 1843208 | tf_op jit(solution)/shard_map/ppermute | solution.py:105
  45.3 29.0 %collective-permute-start.10 = (f16[200,1536]{1,0:T(8,128)(2,1)}, f16[200,1536]{1,0:T(8,128)(2,1)S(1)}, u32[]{:S(2)}, u32[]{:S(2)}) collective-permute-start(f16[200,1536]{1,0:T(8,128)(2,1)} %get-tuple-element.75), channel_id=1, source_target_pairs={{0,8},{4,12},{8,16},{12,20},{16,24},{20,28},{24,0},{28,4},{32,40},... | collective-permute-start | bytes 1843208 | tf_op jit(solution)/shard_map/ppermute | solution.py:105
  46.9 27.5 %collective-permute-start.11 = (f16[200,1536]{1,0:T(8,128)(2,1)}, f16[200,1536]{1,0:T(8,128)(2,1)}, u32[]{:S(2)}, u32[]{:S(2)}) collective-permute-start(f16[200,1536]{1,0:T(8,128)(2,1)} %get-tuple-element.74), channel_id=1, source_target_pairs={{0,24},{4,28},{8,0},{12,4},{16,8},{20,12},{24,16},{28,20},{32,56},... | collective-permute-start | bytes 1843208 | tf_op jit(solution)/shard_map/ppermute | solution.py:105
  63.0 18.3 %collective-permute-start.6 = (f32[56,1536]{1,0:T(8,128)}, f32[56,1536]{1,0:T(8,128)S(1)}, u32[]{:S(2)}, u32[]{:S(2)}) collective-permute-start(f32[56,1536]{1,0:T(8,128)} %get-tuple-element.77), channel_id=1, source_target_pairs={{0,16},{4,20},{8,24},{12,28},{16,0},{20,4},{24,8},{28,12},{32,48},... | collective-permute-start | bytes 1032200 | tf_op jit(solution)/shard_map/ppermute | solution.py:105
  66.6 21.1 %collective-permute-start.7 = (f32[56,1536]{1,0:T(8,128)}, f32[56,1536]{1,0:T(8,128)S(1)}, u32[]{:S(2)}, u32[]{:S(2)}) collective-permute-start(f32[56,1536]{1,0:T(8,128)} %get-tuple-element.78), channel_id=1, source_target_pairs={{0,8},{4,12},{8,16},{12,20},{16,24},{20,28},{24,0},{28,4},{32,40},... | collective-permute-start | bytes 1032200 | tf_op jit(solution)/shard_map/ppermute | solution.py:105
  74.3 13.4 %collective-permute-start.8 = (f32[56,1536]{1,0:T(8,128)S(1)}, f32[56,1536]{1,0:T(8,128)S(1)}, u32[]{:S(2)}, u32[]{:S(2)}) collective-permute-start(f32[56,1536]{1,0:T(8,128)S(1)} %get-tuple-element.79), channel_id=1, source_target_pairs={{0,24},{4,28},{8,0},{12,4},{16,8},{20,12},{24,16},{28,20},{32,56},... | collective-permute-start | bytes 1032200 | tf_op jit(solution)/shard_map/ppermute | solution.py:105
  79.8 9.7 %collective-permute-start.12 = (f32[56,1536]{1,0:T(8,128)}, f32[56,1536]{1,0:T(8,128)S(1)}, u32[]{:S(2)}, u32[]{:S(2)}) collective-permute-start(f32[56,1536]{1,0:T(8,128)} %get-tuple-element.80), channel_id=1, source_target_pairs={{0,64},{4,68},{8,72},{12,76},{16,80},{20,84},{24,88},{28,92},{32,9... | collective-permute-start | bytes 1032200 | tf_op jit(solution)/shard_map/ppermute | solution.py:105
  81.2 17.8 %collective-permute-start.13 = (f32[56,1536]{1,0:T(8,128)}, f32[56,1536]{1,0:T(8,128)}, u32[]{:S(2)}, u32[]{:S(2)}) collective-permute-start(f32[56,1536]{1,0:T(8,128)} %get-tuple-element.81), channel_id=1, source_target_pairs={{0,32},{4,36},{8,40},{12,44},{16,48},{20,52},{24,56},{28,60},{32,6... | collective-permute-start | bytes 1032200 | tf_op jit(solution)/shard_map/ppermute | solution.py:105
  81.3 17.6 %collective-permute-start.14 = (f32[56,1536]{1,0:T(8,128)}, f32[56,1536]{1,0:T(8,128)S(1)}, u32[]{:S(2)}, u32[]{:S(2)}) collective-permute-start(f32[56,1536]{1,0:T(8,128)} %get-tuple-element.82), channel_id=1, source_target_pairs={{0,96},{4,100},{8,104},{12,108},{16,112},{20,116},{24,120},{28,124... | collective-permute-start | bytes 1032200 | tf_op jit(solution)/shard_map/ppermute | solution.py:105
  101.5 3.7 %collective-permute-start.16 = (f32[8,128]{1,0:T(8,128)S(1)}, f32[8,128]{1,0:T(8,128)S(1)}, u32[]{:S(2)}, u32[]{:S(2)}) collective-permute-start(f32[8,128]{1,0:T(8,128)S(1)} %add.531), channel_id=1, source_target_pairs={{0,32},{4,36},{8,40},{12,44},{16,48},{20,52},{24,56},{28,60},{32,6... | collective-permute-start | bytes 12296 | tf_op jit(solution)/shard_map/ppermute | solution.py:105
  101.7 4.0 %collective-permute-start.17 = (f32[8,128]{1,0:T(8,128)S(1)}, f32[8,128]{1,0:T(8,128)S(1)}, u32[]{:S(2)}, u32[]{:S(2)}) collective-permute-start(f32[8,128]{1,0:T(8,128)S(1)} %add.531), channel_id=1, source_target_pairs={{0,64},{4,68},{8,72},{12,76},{16,80},{20,84},{24,88},{28,92},{32,9... | collective-permute-start | bytes 12296 | tf_op jit(solution)/shard_map/ppermute | solution.py:105
  103.5 2.8 %collective-permute-start.18 = (f32[8,128]{1,0:T(8,128)S(1)}, f32[8,128]{1,0:T(8,128)S(1)}, u32[]{:S(2)}, u32[]{:S(2)}) collective-permute-start(f32[8,128]{1,0:T(8,128)S(1)} %add.531), channel_id=1, source_target_pairs={{0,96},{4,100},{8,104},{12,108},{16,112},{20,116},{24,120},{28,124... | collective-permute-start | bytes 12296 | tf_op jit(solution)/shard_map/ppermute | solution.py:105
  106.2 7.3 %collective-permute-start.19 = (f32[8,128]{1,0:T(8,128)S(1)}, f32[8,128]{1,0:T(8,128)S(1)}, u32[]{:S(2)}, u32[]{:S(2)}) collective-permute-start(f32[8,128]{1,0:T(8,128)S(1)} %add_add_fusion.1), channel_id=1, source_target_pairs={{0,8},{4,12},{8,16},{12,20},{16,24},{20,28},{24,0},{28,4},{32,40},... | collective-permute-start | bytes 12296 | tf_op jit(solution)/shard_map/ppermute | solution.py:105
  107.7 5.8 %collective-permute-start.20 = (f32[8,128]{1,0:T(8,128)S(1)}, f32[8,128]{1,0:T(8,128)S(1)}, u32[]{:S(2)}, u32[]{:S(2)}) collective-permute-start(f32[8,128]{1,0:T(8,128)S(1)} %add_add_fusion.1), channel_id=1, source_target_pairs={{0,16},{4,20},{8,24},{12,28},{16,0},{20,4},{24,8},{28,12},{32,48},... | collective-permute-start | bytes 12296 | tf_op jit(solution)/shard_map/ppermute | solution.py:105
  110.8 2.8 %collective-permute-start.21 = (f32[8,128]{1,0:T(8,128)S(1)}, f32[8,128]{1,0:T(8,128)S(1)}, u32[]{:S(2)}, u32[]{:S(2)}) collective-permute-start(f32[8,128]{1,0:T(8,128)S(1)} %add_add_fusion.1), channel_id=1, source_target_pairs={{0,24},{4,28},{8,0},{12,4},{16,8},{20,12},{24,16},{28,20},{32,56},... | collective-permute-start | bytes 12296 | tf_op jit(solution)/shard_map/ppermute | solution.py:105
  110.8 9.8 %collective-permute-start.25 = (f32[32,3072]{1,0:T(8,128)S(1)}, f32[32,3072]{1,0:T(8,128)S(1)}, u32[]{:S(2)}, u32[]{:S(2)}) collective-permute-start(f32[32,3072]{1,0:T(8,128)S(1)} %select_maximum_fusion), channel_id=1, source_target_pairs={{0,4},{4,0},{8,12},{12,8},{16,20},{20,16},{24,28},{28,24},{32,36},... | collective-permute-start | bytes 1179656 | tf_op jit(solution)/shard_map/ppermute | solution.py:105
  113.5 5.1 %collective-permute-start.22 = (f32[8,128]{1,0:T(8,128)S(1)}, f32[8,128]{1,0:T(8,128)S(1)}, u32[]{:S(2)}, u32[]{:S(2)}) collective-permute-start(f32[8,128]{1,0:T(8,128)S(1)} %add_add_fusion), channel_id=1, source_target_pairs={{0,1},{1,2},{2,3},{3,0},{4,5},{5,6},{6,7},{7,4},{8,9},{9,10},{10,1... | collective-permute-start | bytes 12296 | tf_op jit(solution)/shard_map/ppermute | solution.py:109
  114.9 4.0 %collective-permute-start.23 = (f32[8,128]{1,0:T(8,128)S(1)}, f32[8,128]{1,0:T(8,128)S(1)}, u32[]{:S(2)}, u32[]{:S(2)}) collective-permute-start(f32[8,128]{1,0:T(8,128)S(1)} %add_add_fusion), channel_id=1, source_target_pairs={{0,2},{1,3},{2,0},{3,1},{4,6},{5,7},{6,4},{7,5},{8,10},{9,11},{10,... | collective-permute-start | bytes 12296 | tf_op jit(solution)/shard_map/ppermute | solution.py:109
  117.5 2.5 %collective-permute-start.24 = (f32[8,128]{1,0:T(8,128)S(1)}, f32[8,128]{1,0:T(8,128)S(1)}, u32[]{:S(2)}, u32[]{:S(2)}) collective-permute-start(f32[8,128]{1,0:T(8,128)S(1)} %add_add_fusion), channel_id=1, source_target_pairs={{0,3},{1,0},{2,1},{3,2},{4,7},{5,4},{6,5},{7,6},{8,11},{9,8},{10,9... | collective-permute-start | bytes 12296 | tf_op jit(solution)/shard_map/ppermute | solution.py:109
  128.0 7.0 %collective-permute-start.26 = (bf16[24,3072]{1,0:T(8,128)(2,1)S(1)}, bf16[24,3072]{1,0:T(8,128)(2,1)S(1)}, u32[]{:S(2)}, u32[]{:S(2)}) collective-permute-start(bf16[24,3072]{1,0:T(8,128)(2,1)S(1)} %get-tuple-element.102), channel_id=1, source_target_pairs={{0,24},{4,28},{8,0},{12,4},{16,8},{20,12},{24,16},{28,20},{32,56},... | collective-permute-start | bytes 442376 | tf_op jit(solution)/shard_map/ppermute | solution.py:105
  129.0 9.4 %collective-permute-start.27 = (bf16[24,3072]{1,0:T(8,128)(2,1)S(1)}, bf16[24,3072]{1,0:T(8,128)(2,1)S(1)}, u32[]{:S(2)}, u32[]{:S(2)}) collective-permute-start(bf16[24,3072]{1,0:T(8,128)(2,1)S(1)} %get-tuple-element.102), channel_id=1, source_target_pairs={{0,16},{4,20},{8,24},{12,28},{16,0},{20,4},{24,8},{28,12},{32,48},... | collective-permute-start | bytes 442376 | tf_op jit(solution)/shard_map/ppermute | solution.py:105
  131.9 6.5 %collective-permute-start.28 = (bf16[24,3072]{1,0:T(8,128)(2,1)S(1)}, bf16[24,3072]{1,0:T(8,128)(2,1)S(1)}, u32[]{:S(2)}, u32[]{:S(2)}) collective-permute-start(bf16[24,3072]{1,0:T(8,128)(2,1)S(1)} %get-tuple-element.102), channel_id=1, source_target_pairs={{0,8},{4,12},{8,16},{12,20},{16,24},{20,28},{24,0},{28,4},{32,40},... | collective-permute-start | bytes 442376 | tf_op jit(solution)/shard_map/ppermute | solution.py:105
  131.9 6.5 %collective-permute-start.29 = (bf16[24,3072]{1,0:T(8,128)(2,1)S(1)}, bf16[24,3072]{1,0:T(8,128)(2,1)S(1)}, u32[]{:S(2)}, u32[]{:S(2)}) collective-permute-start(bf16[24,3072]{1,0:T(8,128)(2,1)S(1)} %get-tuple-element.101), channel_id=1, source_target_pairs={{0,96},{4,100},{8,104},{12,108},{16,112},{20,116},{24,120},{28,124... | collective-permute-start | bytes 442376 | tf_op jit(solution)/shard_map/ppermute | solution.py:105
  134.7 5.7 %collective-permute-start.30 = (bf16[24,3072]{1,0:T(8,128)(2,1)S(1)}, bf16[24,3072]{1,0:T(8,128)(2,1)S(1)}, u32[]{:S(2)}, u32[]{:S(2)}) collective-permute-start(bf16[24,3072]{1,0:T(8,128)(2,1)S(1)} %get-tuple-element.101), channel_id=1, source_target_pairs={{0,64},{4,68},{8,72},{12,76},{16,80},{20,84},{24,88},{28,92},{32,9... | collective-permute-start | bytes 442376 | tf_op jit(solution)/shard_map/ppermute | solution.py:105
  135.0 6.9 %collective-permute-start.31 = (bf16[24,3072]{1,0:T(8,128)(2,1)S(1)}, bf16[24,3072]{1,0:T(8,128)(2,1)S(1)}, u32[]{:S(2)}, u32[]{:S(2)}) collective-permute-start(bf16[24,3072]{1,0:T(8,128)(2,1)S(1)} %get-tuple-element.101), channel_id=1, source_target_pairs={{0,32},{4,36},{8,40},{12,44},{16,48},{20,52},{24,56},{28,60},{32,6... | collective-permute-start | bytes 442376 | tf_op jit(solution)/shard_map/ppermute | solution.py:105
  142.2 9.8 %collective-permute-start.36 = (bf16[4,24,3072]{2,1,0:T(8,128)(2,1)S(1)}, bf16[4,24,3072]{2,1,0:T(8,128)(2,1)}, u32[]{:S(2)}, u32[]{:S(2)}) collective-permute-start(bf16[4,24,3072]{2,1,0:T(8,128)(2,1)S(1)} %constant_dynamic-slice_fusion.7), channel_id=1, source_target_pairs={{0,4},{4,0},{8,12},{12,8},{16,20},{20,16},{24,28},{28,24},{32,36},... | collective-permute-start | bytes 1769480 | tf_op jit(solution)/shard_map/ppermute | solution.py:105
  147.6 16.1 %collective-permute-start.32 = (bf16[4,24,3072]{2,1,0:T(8,128)(2,1)S(1)}, bf16[4,24,3072]{2,1,0:T(8,128)(2,1)S(1)}, u32[]{:S(2)}, u32[]{:S(2)}) collective-permute-start(bf16[4,24,3072]{2,1,0:T(8,128)(2,1)S(1)} %constant_dynamic-slice_fusion.7), channel_id=1, source_target_pairs={{0,32},{4,36},{8,40},{12,44},{16,48},{20,52},{24,56},{28,60},{32,6... | collective-permute-start | bytes 1769480 | tf_op jit(solution)/shard_map/ppermute | solution.py:105
  147.6 8.2 %collective-permute-start.37 = (bf16[4,24,3072]{2,1,0:T(8,128)(2,1)S(1)}, bf16[4,24,3072]{2,1,0:T(8,128)(2,1)S(1)}, u32[]{:S(2)}, u32[]{:S(2)}) collective-permute-start(bf16[4,24,3072]{2,1,0:T(8,128)(2,1)S(1)} %constant_dynamic-slice_fusion.6), channel_id=1, source_target_pairs={{0,4},{4,0},{8,12},{12,8},{16,20},{20,16},{24,28},{28,24},{32,36},... | collective-permute-start | bytes 1769480 | tf_op jit(solution)/shard_map/ppermute | solution.py:105
  147.8 15.9 %collective-permute-start.33 = (bf16[4,24,3072]{2,1,0:T(8,128)(2,1)S(1)}, bf16[4,24,3072]{2,1,0:T(8,128)(2,1)S(1)}, u32[]{:S(2)}, u32[]{:S(2)}) collective-permute-start(bf16[4,24,3072]{2,1,0:T(8,128)(2,1)S(1)} %constant_dynamic-slice_fusion.6), channel_id=1, source_target_pairs={{0,8},{4,12},{8,16},{12,20},{16,24},{20,28},{24,0},{28,4},{32,40},... | collective-permute-start | bytes 1769480 | tf_op jit(solution)/shard_map/ppermute | solution.py:105
  149.2 15.1 %collective-permute-start.34 = (bf16[4,24,3072]{2,1,0:T(8,128)(2,1)S(1)}, bf16[4,24,3072]{2,1,0:T(8,128)(2,1)S(1)}, u32[]{:S(2)}, u32[]{:S(2)}) collective-permute-start(bf16[4,24,3072]{2,1,0:T(8,128)(2,1)S(1)} %constant_dynamic-slice_fusion.7), channel_id=1, source_target_pairs={{0,96},{4,100},{8,104},{12,108},{16,112},{20,116},{24,120},{28,124... | collective-permute-start | bytes 1769480 | tf_op jit(solution)/shard_map/ppermute | solution.py:105
  152.0 14.1 %collective-permute-start.35 = (bf16[4,24,3072]{2,1,0:T(8,128)(2,1)S(1)}, bf16[4,24,3072]{2,1,0:T(8,128)(2,1)S(1)}, u32[]{:S(2)}, u32[]{:S(2)}) collective-permute-start(bf16[4,24,3072]{2,1,0:T(8,128)(2,1)S(1)} %constant_dynamic-slice_fusion.6), channel_id=1, source_target_pairs={{0,24},{4,28},{8,0},{12,4},{16,8},{20,12},{24,16},{28,20},{32,56},... | collective-permute-start | bytes 1769480 | tf_op jit(solution)/shard_map/ppermute | solution.py:105
  166.2 3.2 %collective-permute-start.42 = (bf16[4,24,3072]{2,1,0:T(8,128)(2,1)S(1)}, bf16[4,24,3072]{2,1,0:T(8,128)(2,1)S(1)}, u32[]{:S(2)}, u32[]{:S(2)}) collective-permute-start(bf16[4,24,3072]{2,1,0:T(8,128)(2,1)S(1)} %collective-permute-done.32), channel_id=1, source_target_pairs={{0,4},{4,0},{8,12},{12,8},{16,20},{20,16},{24,28},{28,24},{32,36},... | collective-permute-start | bytes 1769480 | tf_op jit(solution)/shard_map/ppermute | solution.py:105
  167.8 4.1 %collective-permute-start.43 = (bf16[4,24,3072]{2,1,0:T(8,128)(2,1)S(1)}, bf16[4,24,3072]{2,1,0:T(8,128)(2,1)S(1)}, u32[]{:S(2)}, u32[]{:S(2)}) collective-permute-start(bf16[4,24,3072]{2,1,0:T(8,128)(2,1)S(1)} %collective-permute-done.33), channel_id=1, source_target_pairs={{0,4},{4,0},{8,12},{12,8},{16,20},{20,16},{24,28},{28,24},{32,36},... | collective-permute-start | bytes 1769480 | tf_op jit(solution)/shard_map/ppermute | solution.py:105
  167.9 7.3 %collective-permute-start.44 = (bf16[4,24,3072]{2,1,0:T(8,128)(2,1)S(1)}, bf16[4,24,3072]{2,1,0:T(8,128)(2,1)S(1)}, u32[]{:S(2)}, u32[]{:S(2)}) collective-permute-start(bf16[4,24,3072]{2,1,0:T(8,128)(2,1)S(1)} %collective-permute-done.34), channel_id=1, source_target_pairs={{0,4},{4,0},{8,12},{12,8},{16,20},{20,16},{24,28},{28,24},{32,36},... | collective-permute-start | bytes 1769480 | tf_op jit(solution)/shard_map/ppermute | solution.py:105
  168.5 9.6 %collective-permute-start.45 = (bf16[4,24,3072]{2,1,0:T(8,128)(2,1)S(1)}, bf16[4,24,3072]{2,1,0:T(8,128)(2,1)S(1)}, u32[]{:S(2)}, u32[]{:S(2)}) collective-permute-start(bf16[4,24,3072]{2,1,0:T(8,128)(2,1)S(1)} %collective-permute-done.35), channel_id=1, source_target_pairs={{0,4},{4,0},{8,12},{12,8},{16,20},{20,16},{24,28},{28,24},{32,36},... | collective-permute-start | bytes 1769480 | tf_op jit(solution)/shard_map/ppermute | solution.py:105
  168.6 10.9 %collective-permute-start.38 = (bf16[2,24,3072]{2,1,0:T(8,128)(2,1)S(1)}, bf16[2,24,3072]{2,1,0:T(8,128)(2,1)S(1)}, u32[]{:S(2)}, u32[]{:S(2)}) collective-permute-start(bf16[2,24,3072]{2,1,0:T(8,128)(2,1)S(1)} %slice.362), channel_id=1, source_target_pairs={{0,32},{4,36},{8,40},{12,44},{16,48},{20,52},{24,56},{28,60},{32,6... | collective-permute-start | bytes 884744 | tf_op jit(solution)/shard_map/ppermute | solution.py:105
  169.4 10.1 %collective-permute-start.39 = (bf16[2,24,3072]{2,1,0:T(8,128)(2,1)S(1)}, bf16[2,24,3072]{2,1,0:T(8,128)(2,1)S(1)}, u32[]{:S(2)}, u32[]{:S(2)}) collective-permute-start(bf16[2,24,3072]{2,1,0:T(8,128)(2,1)S(1)} %slice.363), channel_id=1, source_target_pairs={{0,8},{4,12},{8,16},{12,20},{16,24},{20,28},{24,0},{28,4},{32,40},... | collective-permute-start | bytes 884744 | tf_op jit(solution)/shard_map/ppermute | solution.py:105
  171.9 7.9 %collective-permute-start.40 = (bf16[2,24,3072]{2,1,0:T(8,128)(2,1)S(1)}, bf16[2,24,3072]{2,1,0:T(8,128)(2,1)S(1)}, u32[]{:S(2)}, u32[]{:S(2)}) collective-permute-start(bf16[2,24,3072]{2,1,0:T(8,128)(2,1)S(1)} %slice.364), channel_id=1, source_target_pairs={{0,96},{4,100},{8,104},{12,108},{16,112},{20,116},{24,120},{28,124... | collective-permute-start | bytes 884744 | tf_op jit(solution)/shard_map/ppermute | solution.py:105
  175.3 7.2 %collective-permute-start.41 = (bf16[2,24,3072]{2,1,0:T(8,128)(2,1)S(1)}, bf16[2,24,3072]{2,1,0:T(8,128)(2,1)S(1)}, u32[]{:S(2)}, u32[]{:S(2)}) collective-permute-start(bf16[2,24,3072]{2,1,0:T(8,128)(2,1)S(1)} %slice.365), channel_id=1, source_target_pairs={{0,24},{4,28},{8,0},{12,4},{16,8},{20,12},{24,16},{28,20},{32,56},... | collective-permute-start | bytes 884744 | tf_op jit(solution)/shard_map/ppermute | solution.py:105
  182.4 3.5 %collective-permute-start.46 = (bf16[2,24,3072]{2,1,0:T(8,128)(2,1)S(1)}, bf16[2,24,3072]{2,1,0:T(8,128)(2,1)S(1)}, u32[]{:S(2)}, u32[]{:S(2)}) collective-permute-start(bf16[2,24,3072]{2,1,0:T(8,128)(2,1)S(1)} %collective-permute-done.38), channel_id=1, source_target_pairs={{0,4},{4,0},{8,12},{12,8},{16,20},{20,16},{24,28},{28,24},{32,36},... | collective-permute-start | bytes 884744 | tf_op jit(solution)/shard_map/ppermute | solution.py:105
  184.7 3.3 %collective-permute-start.48 = (bf16[2,24,3072]{2,1,0:T(8,128)(2,1)S(1)}, bf16[2,24,3072]{2,1,0:T(8,128)(2,1)S(1)}, u32[]{:S(2)}, u32[]{:S(2)}) collective-permute-start(bf16[2,24,3072]{2,1,0:T(8,128)(2,1)S(1)} %collective-permute-done.40), channel_id=1, source_target_pairs={{0,4},{4,0},{8,12},{12,8},{16,20},{20,16},{24,28},{28,24},{32,36},... | collective-permute-start | bytes 884744 | tf_op jit(solution)/shard_map/ppermute | solution.py:105
  185.2 3.8 %collective-permute-start.49 = (bf16[2,24,3072]{2,1,0:T(8,128)(2,1)S(1)}, bf16[2,24,3072]{2,1,0:T(8,128)(2,1)S(1)}, u32[]{:S(2)}, u32[]{:S(2)}) collective-permute-start(bf16[2,24,3072]{2,1,0:T(8,128)(2,1)S(1)} %collective-permute-done.41), channel_id=1, source_target_pairs={{0,4},{4,0},{8,12},{12,8},{16,20},{20,16},{24,28},{28,24},{32,36},... | collective-permute-start | bytes 884744 | tf_op jit(solution)/shard_map/ppermute | solution.py:105
  (18 other events, 63.2 us)

commit v4 on v3

--- a/solution.py
+++ b/solution.py
@@ -171,7 +171,8 @@
     cols = total.shape[1]
     lines = [bias]
     if entries:
-        lines.append(jnp.stack([jnp.sum(noted[d], axis=0) for d in range(4)]).reshape(-1, cols))
+        flat = jnp.concatenate([jnp.sum(noted[d], axis=0) for d in range(4)])
+        lines.append(jnp.pad(flat, (0, -flat.size % cols)).reshape(-1, cols))
     below = jnp.concatenate(lines, axis=0)
     below = jnp.pad(below, ((0, 8 - below.shape[0]), (0, 0)))
     below = jnp.broadcast_to(below[None], (X, 8, cols))
@@ -229,8 +230,9 @@
     for (i, d, _), part in zip(near, near_parts):
         low = 0 if d == 1 else 2
         far.append((i, low, moves[i](part[low : low + 2], d)))
-    for (i, d, _), part in zip(near, near_parts):
-        full = put(full, i, d, 0, part, shift(part, dc=1))
+    twins = lax.optimization_barrier([shift(part, dc=1) for part in near_parts])
+    for (i, d, _), part, twin in zip(near, near_parts, twins):
+        full = put(full, i, d, 0, part, twin)
     far_parts, full = lax.optimization_barrier(([part for _, _, part in far], full))
     for (i, low, _), part in zip(far, far_parts):
         full = put(full, i, 2, low, part, shift(part, dc=1))
@@ -257,17 +259,19 @@
     index = lax.axis_index("dp")
     x, z, c = index // (Z * C), (index // C) % Z, index % C
     width = cotangent.shape[1]
-    half, quarter = width // 2, width // 4
+    half = width // 2
+    sizes = (half * 1536 // 3072, half * 1536 // 3072)
     tokens = cotangent.shape[0]
     own_rows = master_weight.shape[0]
 
-    def columns(start):
-        return lax.dynamic_slice(cotangent, (0, start), (tokens, quarter))
+    def columns(array, which):
+        start = (1 - c) * half + which * sizes[0]
+        return lax.dynamic_slice(array, (0, start), (tokens, sizes[which]))
 
     attn_other = shift(attn_out, dc=1)
-    sent = [columns((1 - c) * half)]
+    sent = [columns(cotangent, 0)]
     held, sent[0] = lax.optimization_barrier((cotangent, sent[0]))
-    sent.append(lax.dynamic_slice(held, (0, (1 - c) * half + quarter), (tokens, quarter)))
+    sent.append(columns(held, 1))
     others = [shift(part, dc=1) for part in sent]
     count = master_bias.shape[0]
     rest = jnp.concatenate([master_bias, moment_bias, second_bias, teacher_bias])[None] * STATE_SCALE
@@ -277,10 +281,13 @@
         rest = rest - state[-1]
     state = jnp.concatenate([*state, rest], axis=0)
     entries = state.shape[1]
-    extras = [jnp.pad(state, ((NOTE - 3, 0), (0, quarter - entries))), jnp.zeros((NOTE, quarter), jnp.float32)]
+    extras = [
+        jnp.pad(state, ((NOTE - 3, 0), (0, sizes[0] - entries))),
+        jnp.zeros((NOTE, sizes[1]), jnp.float32),
+    ]
 
     def blocks_of(which):
-        start = c * half + which * quarter
+        start = c * half + which * sizes[0]
         return chip_product(attn_out, attn_other, cotangent, start, others[which], extras[which], which == 0)
 
     blocks_a = blocks_of(0)
@@ -294,8 +301,7 @@
     grad_a, noted = scatter_sum(part_a, z, rows + 1, along_z)
     grad_b, _ = scatter_sum(part_b, x, rows + 1, along_x)
     grads = [grad_a, grad_b]
-    used = X * entries // quarter
-    own_state = jnp.stack([n[:used] for n in noted]).reshape(-1, half)
+    own_state = jnp.stack([n.reshape(-1)[: X * entries] for n in noted]).reshape(-1, half)
     sums = [squares(g[:rows]) for g in grads]
     bias_half = jnp.concatenate([g[rows : rows + 1] for g in grads], axis=1)
     chip_grad = jnp.concatenate([g[:rows] for g in grads], axis=1).reshape(C, own_rows, half)
@@ -317,8 +323,12 @@
     weight_grad = in_order(own_half, other_half)
     bias_grad = in_order(bias_half, bias_other)[0]
 
-    sq_norm = jnp.sum(all_sum(sums[0] + sums[1], ("core", "x", "z", "y")))
-    sq_norm = sq_norm + jnp.sum(bias_grad * bias_grad)
+    squared = all_sum(sums[0] + sums[1], ("core", "x", "z"))
+    bias_squared = jnp.sum(bias_grad * bias_grad)
+    squared, bias_squared, weight_grad, bias_grad, bias_state = lax.optimization_barrier(
+        (squared, bias_squared, weight_grad, bias_grad, bias_state)
+    )
+    sq_norm = jnp.sum(all_sum(squared, ("y",))) + bias_squared
     total_count = width * (own_rows * X * Z * C * Y + 1)
     clip_factor = jnp.minimum(1.0, jnp.sqrt(jnp.float32(total_count)) / jnp.sqrt(sq_norm + 1e-06))
     master_w, moment_w, second_w, teacher_w = adamw_update(
@@ -341,7 +351,6 @@
     )
     full_bias = adamw_update(bias_grad, *bias_state, clip_factor, 0.0)[3].astype(jnp.bfloat16)
     teacher_half = teacher_w.astype(jnp.bfloat16)
-    teacher_half, own_bias, full_bias = lax.optimization_barrier((teacher_half, own_bias, full_bias))
     full_weight = gather_plane(teacher_half, x, z, c)
     return (master_w, moment_w, second_w, teacher_w, *own_bias, full_weight, full_bias)
 

time: 191 us -> 187 us (0.979)
  waiting for transfers between devices: 55.9 us -> 48.3 us
  starting transfers between devices: 65.3 us -> 71.6 us
  other arithmetic: 39.4 us -> 37 us
    ppermute x47, waiting for transfers between devices: 54.6 us -> 46.9 us  [shift(): return lax.ppermute(array, 'dp', pairs)]
    ppermute x47, starting transfers between devices: 60.3 us -> 66.6 us  [shift(): return lax.ppermute(array, 'dp', pairs)]
  transfers between devices with their start and end apart: 50 -> 50, of which waited for: 21 -> 21; matrix products, arithmetic and copies ran while one was open for 19% -> 20% of each run, Pallas kernels for 8% -> 9%
where the time goes in v4:
time: 187 us; the launch traced here: 186 us
  starting transfers between devices  71.6 us (38%)
  waiting for transfers between devices  48.3 us (26%)
  other arithmetic  37 us (20%)
  Pallas kernels  16 us (9%)
  local copies, waits for them, and re-layouts  10.4 us (6%)
  between operations  2.82 us (2%)
    ppermute x47, starting transfers between devices, shift(): return lax.ppermute(array, 'dp', pairs)  66.6 us
    ppermute x47, waiting for transfers between devices, shift(): return lax.ppermute(array, 'dp', pairs)  46.9 us
    pallas_call x2, Pallas kernels, chip_product(): pl.pallas_call(functools.partial(product_kernel, x_first), grid_spec=pltp...  16 us
    dynamic_update_slice x10, other arithmetic, put(): return lax.dynamic_update_slice(full, piece, at)  12.3 us
    dynamic_slice x2, local copies, waits for them, and re-layouts, columns(): return lax.dynamic_slice(array, (0, start), (tokens, sizes[which]))  7.6 us
    add x4, other arithmetic, coded_sum(): total, bias = (total + value, bias + line)  5.7 us
    ppermute x3, starting transfers between devices, shift_y(): return lax.ppermute(array, 'mp', [(y, (y + dy) % Y) for y in range(Y)])  5.05 us
    convert_element_type x6, other arithmetic, decoded(): piece = piece.astype(jnp.float32)  4.01 us
  transfers between devices with their start and end apart: 50, of which 21 were waited for; matrix products, arithmetic and copies ran while one was open for 20% of the time, Pallas kernels for 9%

profile of v4, /device:TPU:1, one launch (start us, length us, event | category | flops | bytes accessed | tf_op | source)
XLA Modules:
  0.0 186.1 jit_solution(5721469457791710540)
XLA Ops:
  0.7 3.7 %constant_dynamic-slice_fusion.13 = bf16[1024,1536]{1,0:T(8,128)(2,1)} fusion(bf16[1024,6144]{1,0:T(8,128)(2,1)} %own_cols.3, s32[]{:T(128)S(6)} %select_n.316), kind=kLoop, calls=%fused_computation.150 | loop fusion | bytes 6291460 | tf_op jit(solution)/shard_map/dynamic_slice | solution.py:269
  4.4 1.4 collective-permute-start.1
  5.8 3.9 %constant_dynamic-slice_fusion.12 = bf16[1024,1536]{1,0:T(8,128)(2,1)} fusion(bf16[1024,6144]{1,0:T(8,128)(2,1)} %own_cols.3, s32[]{:T(128)S(6)} %select_n.320), kind=kLoop, calls=%fused_computation.149 | loop fusion | bytes 6291460 | tf_op jit(solution)/shard_map/dynamic_slice | solution.py:269
  10.4 5.2 %collective-permute-done.other = bf16[1024,768]{1,0:T(8,128)(2,1)S(1)} collective-permute-done((bf16[1024,768]{1,0:T(8,128)(2,1)S(1)}, bf16[1024,768]{1,0:T(8,128)(2,1)S(1)}, u32[]{:S(2)}, u32[]{:S(2)}) %collective-permute-start) | collective-permute-done | bytes 1572896 | tf_op jit(solution)/shard_map/ppermute | solution.py:105
  15.6 8.0 %shard_map.177 = f32[4,200,1536]{2,1,0:T(8,128)S(1)} custom-call(s32[1]{0:T(128)} %bitcast.side, bf16[1024,768]{1,0:T(8,128)(2,1)S(1)} %copy-done.2, bf16[1024,768]{1,0:T(8,128)(2,1)S(1)} %collective-permute-done.other, bf16[1024,6144]{1,0:T(8,128)(2,1)} %own_cols.3, bf16[1024,1536]{1,0:T(8,128)(2,1)} %collective-permute-done.1.other_cols, ...), custom_call_target="tpu_custom_call" | custom-call | flops 1 | bytes 1 | tf_op jit(solution)/shard_map/pallas_call | solution.py:72
  23.6 2.0 %dynamic-slice_bitcast_fusion = (f32[200,1536]{1,0:T(8,128)}, f16[200,1536]{1,0:T(8,128)(2,1)}, f16[200,1536]{1,0:T(8,128)(2,1)}, f16[200,1536]{1,0:T(8,128)(2,1)}) fusion(f32[4,200,1536]{2,1,0:T(8,128)S(1)} %shard_map.177, s32[]{:T(128)S(6)} %select_n.319, s32[]{:T(128)S(6)} %select_n.326, s32[]{:T(128)S(6)} %select_n.324, s32[]{:T(128)S(6)} %select_n.322), kind=kLoop, calls=%fused_computation.22 | loop fusion | flops 921600 | bytes 7987216 | tf_op jit(solution)/shard_map/jit(dynamic_index_in_dim)/squeeze | solution.py:131
  28.1 1.4 collective-permute-start.5
  29.5 1.6 collective-permute-start.3
  31.1 8.0 %shard_map.178 = f32[4,200,1536]{2,1,0:T(8,128)S(1)} custom-call(s32[1]{0:T(128)} %bitcast.17.side, bf16[1024,768]{1,0:T(8,128)(2,1)S(1)} %copy-done.2, bf16[1024,768]{1,0:T(8,128)(2,1)S(1)} %collective-permute-done.other, bf16[1024,6144]{1,0:T(8,128)(2,1)} %own_cols.3, bf16[1024,1536]{1,0:T(8,128)(2,1)} %collective-permute-done.2.other_cols, ...), custom_call_target="tpu_custom_call" | custom-call | flops 1 | bytes 1 | tf_op jit(solution)/shard_map/pallas_call | solution.py:72
  39.1 1.5 fusion.11
  40.6 3.6 %collective-permute-start.9 = (f16[200,1536]{1,0:T(8,128)(2,1)}, f16[200,1536]{1,0:T(8,128)(2,1)S(1)}, u32[]{:S(2)}, u32[]{:S(2)}) collective-permute-start(f16[200,1536]{1,0:T(8,128)(2,1)} %get-tuple-element.75), channel_id=1, source_target_pairs={{0,16},{4,20},{8,24},{12,28},{16,0},{20,4},{24,8},{28,12},{32,48},... | collective-permute-start | bytes 1843208 | tf_op jit(solution)/shard_map/ppermute | solution.py:105
  46.6 2.0 %collective-permute-start.11 = (f16[200,1536]{1,0:T(8,128)(2,1)}, f16[200,1536]{1,0:T(8,128)(2,1)}, u32[]{:S(2)}, u32[]{:S(2)}) collective-permute-start(f16[200,1536]{1,0:T(8,128)(2,1)} %get-tuple-element.76), channel_id=1, source_target_pairs={{0,24},{4,28},{8,0},{12,4},{16,8},{20,12},{24,16},{28,20},{32,56},... | collective-permute-start | bytes 1843208 | tf_op jit(solution)/shard_map/ppermute | solution.py:105
  51.1 6.4 %collective-permute-done.3 = f16[200,1536]{1,0:T(8,128)(2,1)S(1)} collective-permute-done((f16[200,1536]{1,0:T(8,128)(2,1)}, f16[200,1536]{1,0:T(8,128)(2,1)S(1)}, u32[]{:S(2)}, u32[]{:S(2)}) %collective-permute-start.3) | collective-permute-done | bytes 614432 | tf_op jit(solution)/shard_map/ppermute | solution.py:105
  58.8 1.8 fusion.4
  63.0 1.6 collective-permute-start.7
  64.6 3.3 %collective-permute-start.6 = (f32[56,1536]{1,0:T(8,128)S(1)}, f32[56,1536]{1,0:T(8,128)S(1)}, u32[]{:S(2)}, u32[]{:S(2)}) collective-permute-start(f32[56,1536]{1,0:T(8,128)S(1)} %get-tuple-element.86), channel_id=1, source_target_pairs={{0,16},{4,20},{8,24},{12,28},{16,0},{20,4},{24,8},{28,12},{32,48},... | collective-permute-start | bytes 1032200 | tf_op jit(solution)/shard_map/ppermute | solution.py:105
  67.9 4.0 %collective-permute-done.10 = f16[200,1536]{1,0:T(8,128)(2,1)S(1)} collective-permute-done((f16[200,1536]{1,0:T(8,128)(2,1)}, f16[200,1536]{1,0:T(8,128)(2,1)S(1)}, u32[]{:S(2)}, u32[]{:S(2)}) %collective-permute-start.10) | collective-permute-done | bytes 614432 | tf_op jit(solution)/shard_map/ppermute | solution.py:105
  75.4 1.8 fusion
  78.1 1.4 collective-permute-start.12
  79.6 2.7 %collective-permute-start.14 = (f32[56,1536]{1,0:T(8,128)}, f32[56,1536]{1,0:T(8,128)}, u32[]{:S(2)}, u32[]{:S(2)}) collective-permute-start(f32[56,1536]{1,0:T(8,128)} %get-tuple-element.84), channel_id=1, source_target_pairs={{0,96},{4,100},{8,104},{12,108},{16,112},{20,116},{24,120},{28,124... | collective-permute-start | bytes 1032200 | tf_op jit(solution)/shard_map/ppermute | solution.py:105
  82.4 4.9 %collective-permute-done.12 = f32[56,1536]{1,0:T(8,128)S(1)} collective-permute-done((f32[56,1536]{1,0:T(8,128)}, f32[56,1536]{1,0:T(8,128)S(1)}, u32[]{:S(2)}, u32[]{:S(2)}) %collective-permute-start.12) | collective-permute-done | bytes 344096 | tf_op jit(solution)/shard_map/ppermute | solution.py:105
  87.3 5.6 %collective-permute-start.8 = (f32[56,1536]{1,0:T(8,128)S(1)}, f32[56,1536]{1,0:T(8,128)S(1)}, u32[]{:S(2)}, u32[]{:S(2)}) collective-permute-start(f32[56,1536]{1,0:T(8,128)S(1)} %get-tuple-element.88), channel_id=1, source_target_pairs={{0,24},{4,28},{8,0},{12,4},{16,8},{20,12},{24,16},{28,20},{32,56},... | collective-permute-start | bytes 1032200 | tf_op jit(solution)/shard_map/ppermute | solution.py:105
  92.8 4.5 %collective-permute-done.13 = f32[56,1536]{1,0:T(8,128)} collective-permute-done((f32[56,1536]{1,0:T(8,128)}, f32[56,1536]{1,0:T(8,128)}, u32[]{:S(2)}, u32[]{:S(2)}) %collective-permute-start.13) | collective-permute-done | bytes 344096 | tf_op jit(solution)/shard_map/ppermute | solution.py:105
  98.8 2.6 %collective-permute-start.15 = (f32[8,128]{1,0:T(8,128)S(1)}, f32[8,128]{1,0:T(8,128)S(1)}, u32[]{:S(2)}, u32[]{:S(2)}) collective-permute-start(f32[8,128]{1,0:T(8,128)S(1)} %add.530), channel_id=1, source_target_pairs={{0,4},{4,0},{8,12},{12,8},{16,20},{20,16},{24,28},{28,24},{32,36},... | collective-permute-start | bytes 12296 | tf_op jit(solution)/shard_map/ppermute | solution.py:105
  102.6 1.7 collective-permute-start.17
  104.3 1.5 collective-permute-start.18
  107.4 4.6 %collective-permute-start.20 = (f32[8,128]{1,0:T(8,128)S(1)}, f32[8,128]{1,0:T(8,128)S(1)}, u32[]{:S(2)}, u32[]{:S(2)}) collective-permute-start(f32[8,128]{1,0:T(8,128)S(1)} %add_add_fusion.1), channel_id=1, source_target_pairs={{0,16},{4,20},{8,24},{12,28},{16,0},{20,4},{24,8},{28,12},{32,48},... | collective-permute-start | bytes 12296 | tf_op jit(solution)/shard_map/ppermute | solution.py:105
  113.0 1.7 collective-permute-done.21
  116.5 1.4 collective-permute-start.23
  117.8 2.6 %collective-permute-start.24 = (f32[8,128]{1,0:T(8,128)S(1)}, f32[8,128]{1,0:T(8,128)S(1)}, u32[]{:S(2)}, u32[]{:S(2)}) collective-permute-start(f32[8,128]{1,0:T(8,128)S(1)} %add_add_fusion), channel_id=1, source_target_pairs={{0,2},{1,3},{2,0},{3,1},{4,6},{5,7},{6,4},{7,5},{8,10},{9,11},{10,... | collective-permute-start | bytes 12296 | tf_op jit(solution)/shard_map/ppermute | solution.py:109
  124.9 1.7 fusion.101
  128.8 2.1 %collective-permute-start.29 = (bf16[24,3072]{1,0:T(8,128)(2,1)S(1)}, bf16[24,3072]{1,0:T(8,128)(2,1)S(1)}, u32[]{:S(2)}, u32[]{:S(2)}) collective-permute-start(bf16[24,3072]{1,0:T(8,128)(2,1)S(1)} %get-tuple-element.107), channel_id=1, source_target_pairs={{0,96},{4,100},{8,104},{12,108},{16,112},{20,116},{24,120},{28,124... | collective-permute-start | bytes 442376 | tf_op jit(solution)/shard_map/ppermute | solution.py:105
  131.6 2.9 %collective-permute-done.29 = bf16[24,3072]{1,0:T(8,128)(2,1)S(1)} collective-permute-done((bf16[24,3072]{1,0:T(8,128)(2,1)S(1)}, bf16[24,3072]{1,0:T(8,128)(2,1)S(1)}, u32[]{:S(2)}, u32[]{:S(2)}) %collective-permute-start.29) | collective-permute-done | bytes 147488 | tf_op jit(solution)/shard_map/ppermute | solution.py:105
  134.7 1.8 collective-permute-done.30
  136.5 1.8 collective-permute-done.31
  138.5 7.2 %collective-permute-start.36 = (bf16[4,24,3072]{2,1,0:T(8,128)(2,1)S(1)}, bf16[4,24,3072]{2,1,0:T(8,128)(2,1)S(1)}, u32[]{:S(2)}, u32[]{:S(2)}) collective-permute-start(bf16[4,24,3072]{2,1,0:T(8,128)(2,1)S(1)} %constant_dynamic-slice_fusion.6), channel_id=1, source_target_pairs={{0,4},{4,0},{8,12},{12,8},{16,20},{20,16},{24,28},{28,24},{32,36},... | collective-permute-start | bytes 1769480 | tf_op jit(solution)/shard_map/ppermute | solution.py:105
  146.0 1.5 collective-permute-start.33
  147.5 2.9 %collective-permute-start.34 = (bf16[4,24,3072]{2,1,0:T(8,128)(2,1)S(1)}, bf16[4,24,3072]{2,1,0:T(8,128)(2,1)S(1)}, u32[]{:S(2)}, u32[]{:S(2)}) collective-permute-start(bf16[4,24,3072]{2,1,0:T(8,128)(2,1)S(1)} %constant_dynamic-slice_fusion.6), channel_id=1, source_target_pairs={{0,96},{4,100},{8,104},{12,108},{16,112},{20,116},{24,120},{28,124... | collective-permute-start | bytes 1769480 | tf_op jit(solution)/shard_map/ppermute | solution.py:105
  154.3 7.4 %collective-permute-done.32 = bf16[4,24,3072]{2,1,0:T(8,128)(2,1)S(1)} collective-permute-done((bf16[4,24,3072]{2,1,0:T(8,128)(2,1)S(1)}, bf16[4,24,3072]{2,1,0:T(8,128)(2,1)S(1)}, u32[]{:S(2)}, u32[]{:S(2)}) %collective-permute-start.32) | collective-permute-done | bytes 589856 | tf_op jit(solution)/shard_map/ppermute | solution.py:105
  162.7 1.9 %collective-permute-done.35 = bf16[4,24,3072]{2,1,0:T(8,128)(2,1)S(1)} collective-permute-done((bf16[4,24,3072]{2,1,0:T(8,128)(2,1)S(1)}, bf16[4,24,3072]{2,1,0:T(8,128)(2,1)S(1)}, u32[]{:S(2)}, u32[]{:S(2)}) %collective-permute-start.35) | collective-permute-done | bytes 589856 | tf_op jit(solution)/shard_map/ppermute | solution.py:105
  164.6 1.5 collective-permute-start.42
  168.9 1.8 collective-permute-start.40
  170.7 1.5 collective-permute-start.41
  172.3 1.4 select_dynamic-update-slice_fusion.3
  173.6 1.4 select_dynamic-update-slice_fusion.2
  175.0 1.4 select_dynamic-update-slice_fusion.1
  176.4 1.4 select_dynamic-update-slice_fusion
  177.9 2.3 %collective-permute-start.46 = (bf16[2,24,3072]{2,1,0:T(8,128)(2,1)S(1)}, bf16[2,24,3072]{2,1,0:T(8,128)(2,1)S(1)}, u32[]{:S(2)}, u32[]{:S(2)}) collective-permute-start(bf16[2,24,3072]{2,1,0:T(8,128)(2,1)S(1)} %collective-permute-done.38), channel_id=1, source_target_pairs={{0,4},{4,0},{8,12},{12,8},{16,20},{20,16},{24,28},{28,24},{32,36},... | collective-permute-start | bytes 884744 | tf_op jit(solution)/shard_map/ppermute | solution.py:105
  (197 shorter events, 43.3 us)
Async XLA Ops:
  4.4 11.2 %collective-permute-start.1 = (bf16[1024,1536]{1,0:T(8,128)(2,1)}, bf16[1024,1536]{1,0:T(8,128)(2,1)}, u32[]{:S(2)}, u32[]{:S(2)}) collective-permute-start(bf16[1024,1536]{1,0:T(8,128)(2,1)} %constant_dynamic-slice_fusion.13), channel_id=1, source_target_pairs={{0,4},{4,0},{8,12},{12,8},{16,20},{20,16},{24,28},{28,24},{32,36},... | collective-permute-start | bytes 9437192 | tf_op jit(solution)/shard_map/ppermute | solution.py:105
  9.7 17.1 %collective-permute-start.2 = (bf16[1024,1536]{1,0:T(8,128)(2,1)}, bf16[1024,1536]{1,0:T(8,128)(2,1)}, u32[]{:S(2)}, u32[]{:S(2)}) collective-permute-start(bf16[1024,1536]{1,0:T(8,128)(2,1)} %constant_dynamic-slice_fusion.12), channel_id=1, source_target_pairs={{0,4},{4,0},{8,12},{12,8},{16,20},{20,16},{24,28},{28,24},{32,36},... | collective-permute-start | bytes 9437192 | tf_op jit(solution)/shard_map/ppermute | solution.py:105
  9.7 5.9 %collective-permute-start = (bf16[1024,768]{1,0:T(8,128)(2,1)S(1)}, bf16[1024,768]{1,0:T(8,128)(2,1)S(1)}, u32[]{:S(2)}, u32[]{:S(2)}) collective-permute-start(bf16[1024,768]{1,0:T(8,128)(2,1)S(1)} %copy-done.2), channel_id=1, source_target_pairs={{0,4},{4,0},{8,12},{12,8},{16,20},{20,16},{24,28},{28,24},{32,36},... | collective-permute-start | bytes 4718600 | tf_op jit(solution)/shard_map/ppermute | solution.py:105
  26.8 19.8 %collective-permute-start.4 = (f16[200,1536]{1,0:T(8,128)(2,1)}, f16[200,1536]{1,0:T(8,128)(2,1)}, u32[]{:S(2)}, u32[]{:S(2)}) collective-permute-start(f16[200,1536]{1,0:T(8,128)(2,1)} %get-tuple-element.40), channel_id=1, source_target_pairs={{0,32},{4,36},{8,40},{12,44},{16,48},{20,52},{24,56},{28,60},{32,6... | collective-permute-start | bytes 1843208 | tf_op jit(solution)/shard_map/ppermute | solution.py:105
  28.1 21.7 %collective-permute-start.5 = (f16[200,1536]{1,0:T(8,128)(2,1)}, f16[200,1536]{1,0:T(8,128)(2,1)}, u32[]{:S(2)}, u32[]{:S(2)}) collective-permute-start(f16[200,1536]{1,0:T(8,128)(2,1)} %get-tuple-element.41), channel_id=1, source_target_pairs={{0,96},{4,100},{8,104},{12,108},{16,112},{20,116},{24,120},{28,124... | collective-permute-start | bytes 1843208 | tf_op jit(solution)/shard_map/ppermute | solution.py:105
  29.5 28.0 %collective-permute-start.3 = (f16[200,1536]{1,0:T(8,128)(2,1)}, f16[200,1536]{1,0:T(8,128)(2,1)S(1)}, u32[]{:S(2)}, u32[]{:S(2)}) collective-permute-start(f16[200,1536]{1,0:T(8,128)(2,1)} %get-tuple-element.39), channel_id=1, source_target_pairs={{0,64},{4,68},{8,72},{12,76},{16,80},{20,84},{24,88},{28,92},{32,9... | collective-permute-start | bytes 1843208 | tf_op jit(solution)/shard_map/ppermute | solution.py:105
  40.6 33.5 %collective-permute-start.9 = (f16[200,1536]{1,0:T(8,128)(2,1)}, f16[200,1536]{1,0:T(8,128)(2,1)S(1)}, u32[]{:S(2)}, u32[]{:S(2)}) collective-permute-start(f16[200,1536]{1,0:T(8,128)(2,1)} %get-tuple-element.75), channel_id=1, source_target_pairs={{0,16},{4,20},{8,24},{12,28},{16,0},{20,4},{24,8},{28,12},{32,48},... | collective-permute-start | bytes 1843208 | tf_op jit(solution)/shard_map/ppermute | solution.py:105
  44.2 27.7 %collective-permute-start.10 = (f16[200,1536]{1,0:T(8,128)(2,1)}, f16[200,1536]{1,0:T(8,128)(2,1)S(1)}, u32[]{:S(2)}, u32[]{:S(2)}) collective-permute-start(f16[200,1536]{1,0:T(8,128)(2,1)} %get-tuple-element.77), channel_id=1, source_target_pairs={{0,8},{4,12},{8,16},{12,20},{16,24},{20,28},{24,0},{28,4},{32,40},... | collective-permute-start | bytes 1843208 | tf_op jit(solution)/shard_map/ppermute | solution.py:105
  46.6 26.2 %collective-permute-start.11 = (f16[200,1536]{1,0:T(8,128)(2,1)}, f16[200,1536]{1,0:T(8,128)(2,1)}, u32[]{:S(2)}, u32[]{:S(2)}) collective-permute-start(f16[200,1536]{1,0:T(8,128)(2,1)} %get-tuple-element.76), channel_id=1, source_target_pairs={{0,24},{4,28},{8,0},{12,4},{16,8},{20,12},{24,16},{28,20},{32,56},... | collective-permute-start | bytes 1843208 | tf_op jit(solution)/shard_map/ppermute | solution.py:105
  63.0 35.6 %collective-permute-start.7 = (f32[56,1536]{1,0:T(8,128)}, f32[56,1536]{1,0:T(8,128)S(1)}, u32[]{:S(2)}, u32[]{:S(2)}) collective-permute-start(f32[56,1536]{1,0:T(8,128)} %get-tuple-element.87), channel_id=1, source_target_pairs={{0,8},{4,12},{8,16},{12,20},{16,24},{20,28},{24,0},{28,4},{32,40},... | collective-permute-start | bytes 1032200 | tf_op jit(solution)/shard_map/ppermute | solution.py:105
  64.6 33.9 %collective-permute-start.6 = (f32[56,1536]{1,0:T(8,128)S(1)}, f32[56,1536]{1,0:T(8,128)S(1)}, u32[]{:S(2)}, u32[]{:S(2)}) collective-permute-start(f32[56,1536]{1,0:T(8,128)S(1)} %get-tuple-element.86), channel_id=1, source_target_pairs={{0,16},{4,20},{8,24},{12,28},{16,0},{20,4},{24,8},{28,12},{32,48},... | collective-permute-start | bytes 1032200 | tf_op jit(solution)/shard_map/ppermute | solution.py:105
  78.1 9.1 %collective-permute-start.12 = (f32[56,1536]{1,0:T(8,128)}, f32[56,1536]{1,0:T(8,128)S(1)}, u32[]{:S(2)}, u32[]{:S(2)}) collective-permute-start(f32[56,1536]{1,0:T(8,128)} %get-tuple-element.82), channel_id=1, source_target_pairs={{0,64},{4,68},{8,72},{12,76},{16,80},{20,84},{24,88},{28,92},{32,9... | collective-permute-start | bytes 1032200 | tf_op jit(solution)/shard_map/ppermute | solution.py:105
  79.6 17.7 %collective-permute-start.13 = (f32[56,1536]{1,0:T(8,128)}, f32[56,1536]{1,0:T(8,128)}, u32[]{:S(2)}, u32[]{:S(2)}) collective-permute-start(f32[56,1536]{1,0:T(8,128)} %get-tuple-element.83), channel_id=1, source_target_pairs={{0,32},{4,36},{8,40},{12,44},{16,48},{20,52},{24,56},{28,60},{32,6... | collective-permute-start | bytes 1032200 | tf_op jit(solution)/shard_map/ppermute | solution.py:105
  79.6 17.7 %collective-permute-start.14 = (f32[56,1536]{1,0:T(8,128)}, f32[56,1536]{1,0:T(8,128)}, u32[]{:S(2)}, u32[]{:S(2)}) collective-permute-start(f32[56,1536]{1,0:T(8,128)} %get-tuple-element.84), channel_id=1, source_target_pairs={{0,96},{4,100},{8,104},{12,108},{16,112},{20,116},{24,120},{28,124... | collective-permute-start | bytes 1032200 | tf_op jit(solution)/shard_map/ppermute | solution.py:105
  87.3 11.3 %collective-permute-start.8 = (f32[56,1536]{1,0:T(8,128)S(1)}, f32[56,1536]{1,0:T(8,128)S(1)}, u32[]{:S(2)}, u32[]{:S(2)}) collective-permute-start(f32[56,1536]{1,0:T(8,128)S(1)} %get-tuple-element.88), channel_id=1, source_target_pairs={{0,24},{4,28},{8,0},{12,4},{16,8},{20,12},{24,16},{28,20},{32,56},... | collective-permute-start | bytes 1032200 | tf_op jit(solution)/shard_map/ppermute | solution.py:105
  98.8 3.5 %collective-permute-start.15 = (f32[8,128]{1,0:T(8,128)S(1)}, f32[8,128]{1,0:T(8,128)S(1)}, u32[]{:S(2)}, u32[]{:S(2)}) collective-permute-start(f32[8,128]{1,0:T(8,128)S(1)} %add.530), channel_id=1, source_target_pairs={{0,4},{4,0},{8,12},{12,8},{16,20},{20,16},{24,28},{28,24},{32,36},... | collective-permute-start | bytes 12296 | tf_op jit(solution)/shard_map/ppermute | solution.py:105
  102.3 5.0 %collective-permute-start.16 = (f32[8,128]{1,0:T(8,128)S(1)}, f32[8,128]{1,0:T(8,128)S(1)}, u32[]{:S(2)}, u32[]{:S(2)}) collective-permute-start(f32[8,128]{1,0:T(8,128)S(1)} %add.531), channel_id=1, source_target_pairs={{0,32},{4,36},{8,40},{12,44},{16,48},{20,52},{24,56},{28,60},{32,6... | collective-permute-start | bytes 12296 | tf_op jit(solution)/shard_map/ppermute | solution.py:105
  102.6 4.7 %collective-permute-start.17 = (f32[8,128]{1,0:T(8,128)S(1)}, f32[8,128]{1,0:T(8,128)S(1)}, u32[]{:S(2)}, u32[]{:S(2)}) collective-permute-start(f32[8,128]{1,0:T(8,128)S(1)} %add.531), channel_id=1, source_target_pairs={{0,64},{4,68},{8,72},{12,76},{16,80},{20,84},{24,88},{28,92},{32,9... | collective-permute-start | bytes 12296 | tf_op jit(solution)/shard_map/ppermute | solution.py:105
  104.3 3.0 %collective-permute-start.18 = (f32[8,128]{1,0:T(8,128)S(1)}, f32[8,128]{1,0:T(8,128)S(1)}, u32[]{:S(2)}, u32[]{:S(2)}) collective-permute-start(f32[8,128]{1,0:T(8,128)S(1)} %add.531), channel_id=1, source_target_pairs={{0,96},{4,100},{8,104},{12,108},{16,112},{20,116},{24,120},{28,124... | collective-permute-start | bytes 12296 | tf_op jit(solution)/shard_map/ppermute | solution.py:105
  106.1 8.7 %collective-permute-start.22 = (f32[32,3072]{1,0:T(8,128)S(1)}, f32[32,3072]{1,0:T(8,128)S(1)}, u32[]{:S(2)}, u32[]{:S(2)}) collective-permute-start(f32[32,3072]{1,0:T(8,128)S(1)} %select_maximum_fusion), channel_id=1, source_target_pairs={{0,4},{4,0},{8,12},{12,8},{16,20},{20,16},{24,28},{28,24},{32,36},... | collective-permute-start | bytes 1179656 | tf_op jit(solution)/shard_map/ppermute | solution.py:105
  107.3 4.7 %collective-permute-start.19 = (f32[8,128]{1,0:T(8,128)S(1)}, f32[8,128]{1,0:T(8,128)S(1)}, u32[]{:S(2)}, u32[]{:S(2)}) collective-permute-start(f32[8,128]{1,0:T(8,128)S(1)} %add_add_fusion.1), channel_id=1, source_target_pairs={{0,8},{4,12},{8,16},{12,20},{16,24},{20,28},{24,0},{28,4},{32,40},... | collective-permute-start | bytes 12296 | tf_op jit(solution)/shard_map/ppermute | solution.py:105
  107.4 5.6 %collective-permute-start.20 = (f32[8,128]{1,0:T(8,128)S(1)}, f32[8,128]{1,0:T(8,128)S(1)}, u32[]{:S(2)}, u32[]{:S(2)}) collective-permute-start(f32[8,128]{1,0:T(8,128)S(1)} %add_add_fusion.1), channel_id=1, source_target_pairs={{0,16},{4,20},{8,24},{12,28},{16,0},{20,4},{24,8},{28,12},{32,48},... | collective-permute-start | bytes 12296 | tf_op jit(solution)/shard_map/ppermute | solution.py:105
  112.0 2.8 %collective-permute-start.21 = (f32[8,128]{1,0:T(8,128)S(1)}, f32[8,128]{1,0:T(8,128)S(1)}, u32[]{:S(2)}, u32[]{:S(2)}) collective-permute-start(f32[8,128]{1,0:T(8,128)S(1)} %add_add_fusion.1), channel_id=1, source_target_pairs={{0,24},{4,28},{8,0},{12,4},{16,8},{20,12},{24,16},{28,20},{32,56},... | collective-permute-start | bytes 12296 | tf_op jit(solution)/shard_map/ppermute | solution.py:105
  116.5 5.1 %collective-permute-start.23 = (f32[8,128]{1,0:T(8,128)S(1)}, f32[8,128]{1,0:T(8,128)S(1)}, u32[]{:S(2)}, u32[]{:S(2)}) collective-permute-start(f32[8,128]{1,0:T(8,128)S(1)} %add_add_fusion), channel_id=1, source_target_pairs={{0,1},{1,2},{2,3},{3,0},{4,5},{5,6},{6,7},{7,4},{8,9},{9,10},{10,1... | collective-permute-start | bytes 12296 | tf_op jit(solution)/shard_map/ppermute | solution.py:109
  117.8 4.0 %collective-permute-start.24 = (f32[8,128]{1,0:T(8,128)S(1)}, f32[8,128]{1,0:T(8,128)S(1)}, u32[]{:S(2)}, u32[]{:S(2)}) collective-permute-start(f32[8,128]{1,0:T(8,128)S(1)} %add_add_fusion), channel_id=1, source_target_pairs={{0,2},{1,3},{2,0},{3,1},{4,6},{5,7},{6,4},{7,5},{8,10},{9,11},{10,... | collective-permute-start | bytes 12296 | tf_op jit(solution)/shard_map/ppermute | solution.py:109
  126.6 4.9 %collective-permute-start.26 = (bf16[24,3072]{1,0:T(8,128)(2,1)S(1)}, bf16[24,3072]{1,0:T(8,128)(2,1)S(1)}, u32[]{:S(2)}, u32[]{:S(2)}) collective-permute-start(bf16[24,3072]{1,0:T(8,128)(2,1)S(1)} %get-tuple-element.108), channel_id=1, source_target_pairs={{0,24},{4,28},{8,0},{12,4},{16,8},{20,12},{24,16},{28,20},{32,56},... | collective-permute-start | bytes 442376 | tf_op jit(solution)/shard_map/ppermute | solution.py:105
  127.6 6.9 %collective-permute-start.27 = (bf16[24,3072]{1,0:T(8,128)(2,1)S(1)}, bf16[24,3072]{1,0:T(8,128)(2,1)S(1)}, u32[]{:S(2)}, u32[]{:S(2)}) collective-permute-start(bf16[24,3072]{1,0:T(8,128)(2,1)S(1)} %get-tuple-element.108), channel_id=1, source_target_pairs={{0,16},{4,20},{8,24},{12,28},{16,0},{20,4},{24,8},{28,12},{32,48},... | collective-permute-start | bytes 442376 | tf_op jit(solution)/shard_map/ppermute | solution.py:105
  128.0 6.7 %collective-permute-start.28 = (bf16[24,3072]{1,0:T(8,128)(2,1)S(1)}, bf16[24,3072]{1,0:T(8,128)(2,1)S(1)}, u32[]{:S(2)}, u32[]{:S(2)}) collective-permute-start(bf16[24,3072]{1,0:T(8,128)(2,1)S(1)} %get-tuple-element.108), channel_id=1, source_target_pairs={{0,8},{4,12},{8,16},{12,20},{16,24},{20,28},{24,0},{28,4},{32,40},... | collective-permute-start | bytes 442376 | tf_op jit(solution)/shard_map/ppermute | solution.py:105
  128.8 5.7 %collective-permute-start.29 = (bf16[24,3072]{1,0:T(8,128)(2,1)S(1)}, bf16[24,3072]{1,0:T(8,128)(2,1)S(1)}, u32[]{:S(2)}, u32[]{:S(2)}) collective-permute-start(bf16[24,3072]{1,0:T(8,128)(2,1)S(1)} %get-tuple-element.107), channel_id=1, source_target_pairs={{0,96},{4,100},{8,104},{12,108},{16,112},{20,116},{24,120},{28,124... | collective-permute-start | bytes 442376 | tf_op jit(solution)/shard_map/ppermute | solution.py:105
  130.8 5.6 %collective-permute-start.30 = (bf16[24,3072]{1,0:T(8,128)(2,1)S(1)}, bf16[24,3072]{1,0:T(8,128)(2,1)S(1)}, u32[]{:S(2)}, u32[]{:S(2)}) collective-permute-start(bf16[24,3072]{1,0:T(8,128)(2,1)S(1)} %get-tuple-element.107), channel_id=1, source_target_pairs={{0,64},{4,68},{8,72},{12,76},{16,80},{20,84},{24,88},{28,92},{32,9... | collective-permute-start | bytes 442376 | tf_op jit(solution)/shard_map/ppermute | solution.py:105
  131.5 6.7 %collective-permute-start.31 = (bf16[24,3072]{1,0:T(8,128)(2,1)S(1)}, bf16[24,3072]{1,0:T(8,128)(2,1)S(1)}, u32[]{:S(2)}, u32[]{:S(2)}) collective-permute-start(bf16[24,3072]{1,0:T(8,128)(2,1)S(1)} %get-tuple-element.107), channel_id=1, source_target_pairs={{0,32},{4,36},{8,40},{12,44},{16,48},{20,52},{24,56},{28,60},{32,6... | collective-permute-start | bytes 442376 | tf_op jit(solution)/shard_map/ppermute | solution.py:105
  138.5 11.9 %collective-permute-start.36 = (bf16[4,24,3072]{2,1,0:T(8,128)(2,1)S(1)}, bf16[4,24,3072]{2,1,0:T(8,128)(2,1)S(1)}, u32[]{:S(2)}, u32[]{:S(2)}) collective-permute-start(bf16[4,24,3072]{2,1,0:T(8,128)(2,1)S(1)} %constant_dynamic-slice_fusion.6), channel_id=1, source_target_pairs={{0,4},{4,0},{8,12},{12,8},{16,20},{20,16},{24,28},{28,24},{32,36},... | collective-permute-start | bytes 1769480 | tf_op jit(solution)/shard_map/ppermute | solution.py:105
  145.7 16.0 %collective-permute-start.32 = (bf16[4,24,3072]{2,1,0:T(8,128)(2,1)S(1)}, bf16[4,24,3072]{2,1,0:T(8,128)(2,1)S(1)}, u32[]{:S(2)}, u32[]{:S(2)}) collective-permute-start(bf16[4,24,3072]{2,1,0:T(8,128)(2,1)S(1)} %constant_dynamic-slice_fusion.6), channel_id=1, source_target_pairs={{0,32},{4,36},{8,40},{12,44},{16,48},{20,52},{24,56},{28,60},{32,6... | collective-permute-start | bytes 1769480 | tf_op jit(solution)/shard_map/ppermute | solution.py:105
  145.7 7.2 %collective-permute-start.37 = (bf16[4,24,3072]{2,1,0:T(8,128)(2,1)S(1)}, bf16[4,24,3072]{2,1,0:T(8,128)(2,1)S(1)}, u32[]{:S(2)}, u32[]{:S(2)}) collective-permute-start(bf16[4,24,3072]{2,1,0:T(8,128)(2,1)S(1)} %constant_dynamic-slice_fusion.5), channel_id=1, source_target_pairs={{0,4},{4,0},{8,12},{12,8},{16,20},{20,16},{24,28},{28,24},{32,36},... | collective-permute-start | bytes 1769480 | tf_op jit(solution)/shard_map/ppermute | solution.py:105
  146.0 15.9 %collective-permute-start.33 = (bf16[4,24,3072]{2,1,0:T(8,128)(2,1)S(1)}, bf16[4,24,3072]{2,1,0:T(8,128)(2,1)S(1)}, u32[]{:S(2)}, u32[]{:S(2)}) collective-permute-start(bf16[4,24,3072]{2,1,0:T(8,128)(2,1)S(1)} %constant_dynamic-slice_fusion.5), channel_id=1, source_target_pairs={{0,8},{4,12},{8,16},{12,20},{16,24},{20,28},{24,0},{28,4},{32,40},... | collective-permute-start | bytes 1769480 | tf_op jit(solution)/shard_map/ppermute | solution.py:105
  147.5 15.2 %collective-permute-start.34 = (bf16[4,24,3072]{2,1,0:T(8,128)(2,1)S(1)}, bf16[4,24,3072]{2,1,0:T(8,128)(2,1)S(1)}, u32[]{:S(2)}, u32[]{:S(2)}) collective-permute-start(bf16[4,24,3072]{2,1,0:T(8,128)(2,1)S(1)} %constant_dynamic-slice_fusion.6), channel_id=1, source_target_pairs={{0,96},{4,100},{8,104},{12,108},{16,112},{20,116},{24,120},{28,124... | collective-permute-start | bytes 1769480 | tf_op jit(solution)/shard_map/ppermute | solution.py:105
  150.4 14.3 %collective-permute-start.35 = (bf16[4,24,3072]{2,1,0:T(8,128)(2,1)S(1)}, bf16[4,24,3072]{2,1,0:T(8,128)(2,1)S(1)}, u32[]{:S(2)}, u32[]{:S(2)}) collective-permute-start(bf16[4,24,3072]{2,1,0:T(8,128)(2,1)S(1)} %constant_dynamic-slice_fusion.5), channel_id=1, source_target_pairs={{0,24},{4,28},{8,0},{12,4},{16,8},{20,12},{24,16},{28,20},{32,56},... | collective-permute-start | bytes 1769480 | tf_op jit(solution)/shard_map/ppermute | solution.py:105
  164.6 3.1 %collective-permute-start.42 = (bf16[4,24,3072]{2,1,0:T(8,128)(2,1)S(1)}, bf16[4,24,3072]{2,1,0:T(8,128)(2,1)S(1)}, u32[]{:S(2)}, u32[]{:S(2)}) collective-permute-start(bf16[4,24,3072]{2,1,0:T(8,128)(2,1)S(1)} %collective-permute-done.32), channel_id=1, source_target_pairs={{0,4},{4,0},{8,12},{12,8},{16,20},{20,16},{24,28},{28,24},{32,36},... | collective-permute-start | bytes 1769480 | tf_op jit(solution)/shard_map/ppermute | solution.py:105
  166.1 2.8 %collective-permute-start.43 = (bf16[4,24,3072]{2,1,0:T(8,128)(2,1)S(1)}, bf16[4,24,3072]{2,1,0:T(8,128)(2,1)S(1)}, u32[]{:S(2)}, u32[]{:S(2)}) collective-permute-start(bf16[4,24,3072]{2,1,0:T(8,128)(2,1)S(1)} %collective-permute-done.33), channel_id=1, source_target_pairs={{0,4},{4,0},{8,12},{12,8},{16,20},{20,16},{24,28},{28,24},{32,36},... | collective-permute-start | bytes 1769480 | tf_op jit(solution)/shard_map/ppermute | solution.py:105
  166.1 4.6 %collective-permute-start.44 = (bf16[4,24,3072]{2,1,0:T(8,128)(2,1)S(1)}, bf16[4,24,3072]{2,1,0:T(8,128)(2,1)S(1)}, u32[]{:S(2)}, u32[]{:S(2)}) collective-permute-start(bf16[4,24,3072]{2,1,0:T(8,128)(2,1)S(1)} %collective-permute-done.34), channel_id=1, source_target_pairs={{0,4},{4,0},{8,12},{12,8},{16,20},{20,16},{24,28},{28,24},{32,36},... | collective-permute-start | bytes 1769480 | tf_op jit(solution)/shard_map/ppermute | solution.py:105
  166.6 5.7 %collective-permute-start.45 = (bf16[4,24,3072]{2,1,0:T(8,128)(2,1)S(1)}, bf16[4,24,3072]{2,1,0:T(8,128)(2,1)S(1)}, u32[]{:S(2)}, u32[]{:S(2)}) collective-permute-start(bf16[4,24,3072]{2,1,0:T(8,128)(2,1)S(1)} %collective-permute-done.35), channel_id=1, source_target_pairs={{0,4},{4,0},{8,12},{12,8},{16,20},{20,16},{24,28},{28,24},{32,36},... | collective-permute-start | bytes 1769480 | tf_op jit(solution)/shard_map/ppermute | solution.py:105
  166.8 10.9 %collective-permute-start.38 = (bf16[2,24,3072]{2,1,0:T(8,128)(2,1)S(1)}, bf16[2,24,3072]{2,1,0:T(8,128)(2,1)S(1)}, u32[]{:S(2)}, u32[]{:S(2)}) collective-permute-start(bf16[2,24,3072]{2,1,0:T(8,128)(2,1)S(1)} %slice.361), channel_id=1, source_target_pairs={{0,32},{4,36},{8,40},{12,44},{16,48},{20,52},{24,56},{28,60},{32,6... | collective-permute-start | bytes 884744 | tf_op jit(solution)/shard_map/ppermute | solution.py:105
  167.7 10.0 %collective-permute-start.39 = (bf16[2,24,3072]{2,1,0:T(8,128)(2,1)S(1)}, bf16[2,24,3072]{2,1,0:T(8,128)(2,1)S(1)}, u32[]{:S(2)}, u32[]{:S(2)}) collective-permute-start(bf16[2,24,3072]{2,1,0:T(8,128)(2,1)S(1)} %slice.362), channel_id=1, source_target_pairs={{0,8},{4,12},{8,16},{12,20},{16,24},{20,28},{24,0},{28,4},{32,40},... | collective-permute-start | bytes 884744 | tf_op jit(solution)/shard_map/ppermute | solution.py:105
  168.9 8.9 %collective-permute-start.40 = (bf16[2,24,3072]{2,1,0:T(8,128)(2,1)S(1)}, bf16[2,24,3072]{2,1,0:T(8,128)(2,1)S(1)}, u32[]{:S(2)}, u32[]{:S(2)}) collective-permute-start(bf16[2,24,3072]{2,1,0:T(8,128)(2,1)S(1)} %slice.363), channel_id=1, source_target_pairs={{0,96},{4,100},{8,104},{12,108},{16,112},{20,116},{24,120},{28,124... | collective-permute-start | bytes 884744 | tf_op jit(solution)/shard_map/ppermute | solution.py:105
  170.7 7.2 %collective-permute-start.41 = (bf16[2,24,3072]{2,1,0:T(8,128)(2,1)S(1)}, bf16[2,24,3072]{2,1,0:T(8,128)(2,1)S(1)}, u32[]{:S(2)}, u32[]{:S(2)}) collective-permute-start(bf16[2,24,3072]{2,1,0:T(8,128)(2,1)S(1)} %slice.364), channel_id=1, source_target_pairs={{0,24},{4,28},{8,0},{12,4},{16,8},{20,12},{24,16},{28,20},{32,56},... | collective-permute-start | bytes 884744 | tf_op jit(solution)/shard_map/ppermute | solution.py:105
  177.9 4.1 %collective-permute-start.46 = (bf16[2,24,3072]{2,1,0:T(8,128)(2,1)S(1)}, bf16[2,24,3072]{2,1,0:T(8,128)(2,1)S(1)}, u32[]{:S(2)}, u32[]{:S(2)}) collective-permute-start(bf16[2,24,3072]{2,1,0:T(8,128)(2,1)S(1)} %collective-permute-done.38), channel_id=1, source_target_pairs={{0,4},{4,0},{8,12},{12,8},{16,20},{20,16},{24,28},{28,24},{32,36},... | collective-permute-start | bytes 884744 | tf_op jit(solution)/shard_map/ppermute | solution.py:105
  181.4 2.6 %collective-permute-start.48 = (bf16[2,24,3072]{2,1,0:T(8,128)(2,1)S(1)}, bf16[2,24,3072]{2,1,0:T(8,128)(2,1)S(1)}, u32[]{:S(2)}, u32[]{:S(2)}) collective-permute-start(bf16[2,24,3072]{2,1,0:T(8,128)(2,1)S(1)} %collective-permute-done.40), channel_id=1, source_target_pairs={{0,4},{4,0},{8,12},{12,8},{16,20},{20,16},{24,28},{28,24},{32,36},... | collective-permute-start | bytes 884744 | tf_op jit(solution)/shard_map/ppermute | solution.py:105
  182.0 3.1 %collective-permute-start.49 = (bf16[2,24,3072]{2,1,0:T(8,128)(2,1)S(1)}, bf16[2,24,3072]{2,1,0:T(8,128)(2,1)S(1)}, u32[]{:S(2)}, u32[]{:S(2)}) collective-permute-start(bf16[2,24,3072]{2,1,0:T(8,128)(2,1)S(1)} %collective-permute-done.41), channel_id=1, source_target_pairs={{0,4},{4,0},{8,12},{12,8},{16,20},{20,16},{24,28},{28,24},{32,36},... | collective-permute-start | bytes 884744 | tf_op jit(solution)/shard_map/ppermute | solution.py:105
  (13 other events, 72.1 us)

commit v5 on v4

--- a/solution.py
+++ b/solution.py
@@ -141,8 +141,9 @@
 def scatter_sum(blocks, me, rows, move):
     own = pick(blocks, 0, me)
     total, rest = own[:rows], {0: own[rows:]}
-    for d in (2, 1, 3):
-        got = move(pick(blocks, 0, me + d), d)
+    far = (2, 1, 3)
+    parts = lax.optimization_barrier([move(pick(blocks, 0, me + d), d) for d in far])
+    for d, got in zip(far, parts):
         total, rest[d] = total + got[:rows], got[rows:]
     return total, [rest[d] for d in range(4)]
 

time: 187 us -> 182 us (0.973)
  starting transfers between devices: 71.6 us -> 63.4 us
  waiting for transfers between devices: 48.3 us -> 54.5 us
  other arithmetic: 37 us -> 34 us
    ppermute x47, starting transfers between devices: 66.6 us -> 58.4 us  [shift(): return lax.ppermute(array, 'dp', pairs)]
    ppermute x47, waiting for transfers between devices: 46.9 us -> 53.1 us  [shift(): return lax.ppermute(array, 'dp', pairs)]
  transfers between devices with their start and end apart: 50 -> 50, of which waited for: 21 -> 20; matrix products, arithmetic and copies ran while one was open for 20% -> 19% of each run, Pallas kernels for 9% -> 9%
where the time goes in v5:
time: 182 us; the launch traced here: 181 us
  starting transfers between devices  63.4 us (35%)
  waiting for transfers between devices  54.5 us (30%)
  other arithmetic  34 us (19%)
  Pallas kernels  16 us (9%)
  local copies, waits for them, and re-layouts  10.4 us (6%)
  between operations  2.83 us (2%)
    ppermute x47, starting transfers between devices, shift(): return lax.ppermute(array, 'dp', pairs)  58.4 us
    ppermute x47, waiting for transfers between devices, shift(): return lax.ppermute(array, 'dp', pairs)  53.1 us
    pallas_call x2, Pallas kernels, chip_product(): pl.pallas_call(functools.partial(product_kernel, x_first), grid_spec=pltp...  16 us
    dynamic_update_slice x10, other arithmetic, put(): return lax.dynamic_update_slice(full, piece, at)  12.3 us
    dynamic_slice x2, local copies, waits for them, and re-layouts, columns(): return lax.dynamic_slice(array, (0, start), (tokens, sizes[which]))  7.61 us
    add x4, other arithmetic, coded_sum(): total, bias = (total + value, bias + line)  5.7 us
    ppermute x3, starting transfers between devices, shift_y(): return lax.ppermute(array, 'mp', [(y, (y + dy) % Y) for y in range(Y)])  5.04 us
  transfers between devices with their start and end apart: 50, of which 20 were waited for; matrix products, arithmetic and copies ran while one was open for 19% of the time, Pallas kernels for 9%

profile of v5, /device:TPU:1, one launch (start us, length us, event | category | flops | bytes accessed | tf_op | source)
XLA Modules:
  0.0 181.1 jit_solution(8999309718709929611)
XLA Ops:
  0.7 3.7 %constant_dynamic-slice_fusion.13 = bf16[1024,1536]{1,0:T(8,128)(2,1)} fusion(bf16[1024,6144]{1,0:T(8,128)(2,1)} %own_cols.3, s32[]{:T(128)S(6)} %select_n.316), kind=kLoop, calls=%fused_computation.150 | loop fusion | bytes 6291460 | tf_op jit(solution)/shard_map/dynamic_slice | solution.py:270
  4.4 1.4 collective-permute-start.1
  5.8 3.9 %constant_dynamic-slice_fusion.12 = bf16[1024,1536]{1,0:T(8,128)(2,1)} fusion(bf16[1024,6144]{1,0:T(8,128)(2,1)} %own_cols.3, s32[]{:T(128)S(6)} %select_n.320), kind=kLoop, calls=%fused_computation.149 | loop fusion | bytes 6291460 | tf_op jit(solution)/shard_map/dynamic_slice | solution.py:270
  10.4 5.2 %collective-permute-done.other = bf16[1024,768]{1,0:T(8,128)(2,1)S(1)} collective-permute-done((bf16[1024,768]{1,0:T(8,128)(2,1)S(1)}, bf16[1024,768]{1,0:T(8,128)(2,1)S(1)}, u32[]{:S(2)}, u32[]{:S(2)}) %collective-permute-start) | collective-permute-done | bytes 1572896 | tf_op jit(solution)/shard_map/ppermute | solution.py:105
  15.6 8.0 %shard_map.177 = f32[4,200,1536]{2,1,0:T(8,128)S(1)} custom-call(s32[1]{0:T(128)} %bitcast.side, bf16[1024,768]{1,0:T(8,128)(2,1)S(1)} %copy-done.2, bf16[1024,768]{1,0:T(8,128)(2,1)S(1)} %collective-permute-done.other, bf16[1024,6144]{1,0:T(8,128)(2,1)} %own_cols.3, bf16[1024,1536]{1,0:T(8,128)(2,1)} %collective-permute-done.1.other_cols, ...), custom_call_target="tpu_custom_call" | custom-call | flops 1 | bytes 1 | tf_op jit(solution)/shard_map/pallas_call | solution.py:72
  23.6 2.0 %dynamic-slice_bitcast_fusion = (f32[200,1536]{1,0:T(8,128)}, f16[200,1536]{1,0:T(8,128)(2,1)}, f16[200,1536]{1,0:T(8,128)(2,1)}, f16[200,1536]{1,0:T(8,128)(2,1)}) fusion(f32[4,200,1536]{2,1,0:T(8,128)S(1)} %shard_map.177, s32[]{:T(128)S(6)} %select_n.319, s32[]{:T(128)S(6)} %select_n.326, s32[]{:T(128)S(6)} %select_n.324, s32[]{:T(128)S(6)} %select_n.322), kind=kLoop, calls=%fused_computation.22 | loop fusion | flops 921600 | bytes 7987216 | tf_op jit(solution)/shard_map/jit(dynamic_index_in_dim)/squeeze | solution.py:131
  28.1 1.4 collective-permute-start.5
  29.5 1.6 collective-permute-start.3
  31.1 8.0 %shard_map.178 = f32[4,200,1536]{2,1,0:T(8,128)S(1)} custom-call(s32[1]{0:T(128)} %bitcast.17.side, bf16[1024,768]{1,0:T(8,128)(2,1)S(1)} %copy-done.2, bf16[1024,768]{1,0:T(8,128)(2,1)S(1)} %collective-permute-done.other, bf16[1024,6144]{1,0:T(8,128)(2,1)} %own_cols.3, bf16[1024,1536]{1,0:T(8,128)(2,1)} %collective-permute-done.2.other_cols, ...), custom_call_target="tpu_custom_call" | custom-call | flops 1 | bytes 1 | tf_op jit(solution)/shard_map/pallas_call | solution.py:72
  39.1 1.5 fusion.11
  40.6 3.6 %collective-permute-start.9 = (f16[200,1536]{1,0:T(8,128)(2,1)}, f16[200,1536]{1,0:T(8,128)(2,1)S(1)}, u32[]{:S(2)}, u32[]{:S(2)}) collective-permute-start(f16[200,1536]{1,0:T(8,128)(2,1)} %get-tuple-element.87), channel_id=1, source_target_pairs={{0,16},{4,20},{8,24},{12,28},{16,0},{20,4},{24,8},{28,12},{32,48},... | collective-permute-start | bytes 1843208 | tf_op jit(solution)/shard_map/ppermute | solution.py:105
  46.6 2.0 %collective-permute-start.11 = (f16[200,1536]{1,0:T(8,128)(2,1)}, f16[200,1536]{1,0:T(8,128)(2,1)S(1)}, u32[]{:S(2)}, u32[]{:S(2)}) collective-permute-start(f16[200,1536]{1,0:T(8,128)(2,1)} %get-tuple-element.88), channel_id=1, source_target_pairs={{0,24},{4,28},{8,0},{12,4},{16,8},{20,12},{24,16},{28,20},{32,56},... | collective-permute-start | bytes 1843208 | tf_op jit(solution)/shard_map/ppermute | solution.py:105
  51.1 6.4 %collective-permute-done.3 = f16[200,1536]{1,0:T(8,128)(2,1)S(1)} collective-permute-done((f16[200,1536]{1,0:T(8,128)(2,1)}, f16[200,1536]{1,0:T(8,128)(2,1)S(1)}, u32[]{:S(2)}, u32[]{:S(2)}) %collective-permute-start.3) | collective-permute-done | bytes 614432 | tf_op jit(solution)/shard_map/ppermute | solution.py:105
  58.8 1.8 fusion.4
  63.1 3.6 %collective-permute-start.6 = (f32[56,1536]{1,0:T(8,128)}, f32[56,1536]{1,0:T(8,128)S(1)}, u32[]{:S(2)}, u32[]{:S(2)}) collective-permute-start(f32[56,1536]{1,0:T(8,128)} %get-tuple-element.99), channel_id=1, source_target_pairs={{0,16},{4,20},{8,24},{12,28},{16,0},{20,4},{24,8},{28,12},{32,48},... | collective-permute-start | bytes 1032200 | tf_op jit(solution)/shard_map/ppermute | solution.py:105
  67.4 5.8 %collective-permute-done.10 = f16[200,1536]{1,0:T(8,128)(2,1)S(1)} collective-permute-done((f16[200,1536]{1,0:T(8,128)(2,1)}, f16[200,1536]{1,0:T(8,128)(2,1)S(1)}, u32[]{:S(2)}, u32[]{:S(2)}) %collective-permute-start.10) | collective-permute-done | bytes 614432 | tf_op jit(solution)/shard_map/ppermute | solution.py:105
  74.8 1.8 fusion
  76.8 1.5 collective-permute-start.12
  78.3 2.7 %collective-permute-start.14 = (f32[56,1536]{1,0:T(8,128)S(1)}, f32[56,1536]{1,0:T(8,128)S(1)}, u32[]{:S(2)}, u32[]{:S(2)}) collective-permute-start(f32[56,1536]{1,0:T(8,128)S(1)} %get-tuple-element.94), channel_id=1, source_target_pairs={{0,96},{4,100},{8,104},{12,108},{16,112},{20,116},{24,120},{28,124... | collective-permute-start | bytes 1032200 | tf_op jit(solution)/shard_map/ppermute | solution.py:105
  81.1 5.6 %collective-permute-done.7 = f32[56,1536]{1,0:T(8,128)S(1)} collective-permute-done((f32[56,1536]{1,0:T(8,128)}, f32[56,1536]{1,0:T(8,128)S(1)}, u32[]{:S(2)}, u32[]{:S(2)}) %collective-permute-start.7) | collective-permute-done | bytes 344096 | tf_op jit(solution)/shard_map/ppermute | solution.py:105
  86.8 8.9 %collective-permute-done.13 = f32[56,1536]{1,0:T(8,128)S(1)} collective-permute-done((f32[56,1536]{1,0:T(8,128)S(1)}, f32[56,1536]{1,0:T(8,128)S(1)}, u32[]{:S(2)}, u32[]{:S(2)}) %collective-permute-start.13) | collective-permute-done | bytes 344096 | tf_op jit(solution)/shard_map/ppermute | solution.py:105
  97.7 1.7 collective-permute-start.17
  99.4 1.5 collective-permute-start.18
  102.4 1.5 collective-permute-start.19
  103.9 3.0 %collective-permute-start.20 = (f32[8,128]{1,0:T(8,128)S(1)}, f32[8,128]{1,0:T(8,128)S(1)}, u32[]{:S(2)}, u32[]{:S(2)}) collective-permute-start(f32[8,128]{1,0:T(8,128)S(1)} %add_add_fusion.1), channel_id=1, source_target_pairs={{0,16},{4,20},{8,24},{12,28},{16,0},{20,4},{24,8},{28,12},{32,48},... | collective-permute-start | bytes 12296 | tf_op jit(solution)/shard_map/ppermute | solution.py:105
  108.0 1.7 collective-permute-done.21
  111.4 1.4 collective-permute-start.23
  112.8 2.6 %collective-permute-start.24 = (f32[8,128]{1,0:T(8,128)S(1)}, f32[8,128]{1,0:T(8,128)S(1)}, u32[]{:S(2)}, u32[]{:S(2)}) collective-permute-start(f32[8,128]{1,0:T(8,128)S(1)} %add_add_fusion), channel_id=1, source_target_pairs={{0,2},{1,3},{2,0},{3,1},{4,6},{5,7},{6,4},{7,5},{8,10},{9,11},{10,... | collective-permute-start | bytes 12296 | tf_op jit(solution)/shard_map/ppermute | solution.py:109
  119.8 1.7 fusion.104
  123.7 2.1 %collective-permute-start.29 = (bf16[24,3072]{1,0:T(8,128)(2,1)S(1)}, bf16[24,3072]{1,0:T(8,128)(2,1)S(1)}, u32[]{:S(2)}, u32[]{:S(2)}) collective-permute-start(bf16[24,3072]{1,0:T(8,128)(2,1)S(1)} %get-tuple-element.119), channel_id=1, source_target_pairs={{0,96},{4,100},{8,104},{12,108},{16,112},{20,116},{24,120},{28,124... | collective-permute-start | bytes 442376 | tf_op jit(solution)/shard_map/ppermute | solution.py:105
  126.5 2.9 %collective-permute-done.29 = bf16[24,3072]{1,0:T(8,128)(2,1)S(1)} collective-permute-done((bf16[24,3072]{1,0:T(8,128)(2,1)S(1)}, bf16[24,3072]{1,0:T(8,128)(2,1)S(1)}, u32[]{:S(2)}, u32[]{:S(2)}) %collective-permute-start.29) | collective-permute-done | bytes 147488 | tf_op jit(solution)/shard_map/ppermute | solution.py:105
  129.6 1.8 collective-permute-done.30
  131.4 1.8 collective-permute-done.31
  133.4 7.2 %collective-permute-start.36 = (bf16[4,24,3072]{2,1,0:T(8,128)(2,1)S(1)}, bf16[4,24,3072]{2,1,0:T(8,128)(2,1)S(1)}, u32[]{:S(2)}, u32[]{:S(2)}) collective-permute-start(bf16[4,24,3072]{2,1,0:T(8,128)(2,1)S(1)} %constant_dynamic-slice_fusion.6), channel_id=1, source_target_pairs={{0,4},{4,0},{8,12},{12,8},{16,20},{20,16},{24,28},{28,24},{32,36},... | collective-permute-start | bytes 1769480 | tf_op jit(solution)/shard_map/ppermute | solution.py:105
  141.0 1.5 collective-permute-start.33
  142.4 2.9 %collective-permute-start.34 = (bf16[4,24,3072]{2,1,0:T(8,128)(2,1)S(1)}, bf16[4,24,3072]{2,1,0:T(8,128)(2,1)S(1)}, u32[]{:S(2)}, u32[]{:S(2)}) collective-permute-start(bf16[4,24,3072]{2,1,0:T(8,128)(2,1)S(1)} %constant_dynamic-slice_fusion.6), channel_id=1, source_target_pairs={{0,96},{4,100},{8,104},{12,108},{16,112},{20,116},{24,120},{28,124... | collective-permute-start | bytes 1769480 | tf_op jit(solution)/shard_map/ppermute | solution.py:105
  146.5 1.4 select_dynamic-update-slice_fusion.5
  147.9 1.4 select_dynamic-update-slice_fusion.4
  149.2 7.4 %collective-permute-done.32 = bf16[4,24,3072]{2,1,0:T(8,128)(2,1)S(1)} collective-permute-done((bf16[4,24,3072]{2,1,0:T(8,128)(2,1)S(1)}, bf16[4,24,3072]{2,1,0:T(8,128)(2,1)S(1)}, u32[]{:S(2)}, u32[]{:S(2)}) %collective-permute-start.32) | collective-permute-done | bytes 589856 | tf_op jit(solution)/shard_map/ppermute | solution.py:105
  157.7 1.9 %collective-permute-done.35 = bf16[4,24,3072]{2,1,0:T(8,128)(2,1)S(1)} collective-permute-done((bf16[4,24,3072]{2,1,0:T(8,128)(2,1)S(1)}, bf16[4,24,3072]{2,1,0:T(8,128)(2,1)S(1)}, u32[]{:S(2)}, u32[]{:S(2)}) %collective-permute-start.35) | collective-permute-done | bytes 589856 | tf_op jit(solution)/shard_map/ppermute | solution.py:105
  159.6 1.5 collective-permute-start.42
  163.8 1.8 %collective-permute-start.40 = (bf16[2,24,3072]{2,1,0:T(8,128)(2,1)S(1)}, bf16[2,24,3072]{2,1,0:T(8,128)(2,1)S(1)}, u32[]{:S(2)}, u32[]{:S(2)}) collective-permute-start(bf16[2,24,3072]{2,1,0:T(8,128)(2,1)S(1)} %slice.363), channel_id=1, source_target_pairs={{0,96},{4,100},{8,104},{12,108},{16,112},{20,116},{24,120},{28,124... | collective-permute-start | bytes 884744 | tf_op jit(solution)/shard_map/ppermute | solution.py:105
  165.7 1.5 collective-permute-start.41
  167.2 1.4 select_dynamic-update-slice_fusion.3
  168.6 1.4 select_dynamic-update-slice_fusion.2
  170.0 1.4 select_dynamic-update-slice_fusion.1
  171.3 1.4 select_dynamic-update-slice_fusion
  172.8 2.3 %collective-permute-start.46 = (bf16[2,24,3072]{2,1,0:T(8,128)(2,1)S(1)}, bf16[2,24,3072]{2,1,0:T(8,128)(2,1)S(1)}, u32[]{:S(2)}, u32[]{:S(2)}) collective-permute-start(bf16[2,24,3072]{2,1,0:T(8,128)(2,1)S(1)} %collective-permute-done.38), channel_id=1, source_target_pairs={{0,4},{4,0},{8,12},{12,8},{16,20},{20,16},{24,28},{28,24},{32,36},... | collective-permute-start | bytes 884744 | tf_op jit(solution)/shard_map/ppermute | solution.py:105
  (196 shorter events, 38.0 us)
Async XLA Ops:
  4.4 11.2 %collective-permute-start.1 = (bf16[1024,1536]{1,0:T(8,128)(2,1)}, bf16[1024,1536]{1,0:T(8,128)(2,1)}, u32[]{:S(2)}, u32[]{:S(2)}) collective-permute-start(bf16[1024,1536]{1,0:T(8,128)(2,1)} %constant_dynamic-slice_fusion.13), channel_id=1, source_target_pairs={{0,4},{4,0},{8,12},{12,8},{16,20},{20,16},{24,28},{28,24},{32,36},... | collective-permute-start | bytes 9437192 | tf_op jit(solution)/shard_map/ppermute | solution.py:105
  9.7 17.1 %collective-permute-start.2 = (bf16[1024,1536]{1,0:T(8,128)(2,1)}, bf16[1024,1536]{1,0:T(8,128)(2,1)}, u32[]{:S(2)}, u32[]{:S(2)}) collective-permute-start(bf16[1024,1536]{1,0:T(8,128)(2,1)} %constant_dynamic-slice_fusion.12), channel_id=1, source_target_pairs={{0,4},{4,0},{8,12},{12,8},{16,20},{20,16},{24,28},{28,24},{32,36},... | collective-permute-start | bytes 9437192 | tf_op jit(solution)/shard_map/ppermute | solution.py:105
  9.7 5.9 %collective-permute-start = (bf16[1024,768]{1,0:T(8,128)(2,1)S(1)}, bf16[1024,768]{1,0:T(8,128)(2,1)S(1)}, u32[]{:S(2)}, u32[]{:S(2)}) collective-permute-start(bf16[1024,768]{1,0:T(8,128)(2,1)S(1)} %copy-done.2), channel_id=1, source_target_pairs={{0,4},{4,0},{8,12},{12,8},{16,20},{20,16},{24,28},{28,24},{32,36},... | collective-permute-start | bytes 4718600 | tf_op jit(solution)/shard_map/ppermute | solution.py:105
  26.8 19.8 %collective-permute-start.4 = (f16[200,1536]{1,0:T(8,128)(2,1)}, f16[200,1536]{1,0:T(8,128)(2,1)}, u32[]{:S(2)}, u32[]{:S(2)}) collective-permute-start(f16[200,1536]{1,0:T(8,128)(2,1)} %get-tuple-element.46), channel_id=1, source_target_pairs={{0,32},{4,36},{8,40},{12,44},{16,48},{20,52},{24,56},{28,60},{32,6... | collective-permute-start | bytes 1843208 | tf_op jit(solution)/shard_map/ppermute | solution.py:105
  28.1 21.7 %collective-permute-start.5 = (f16[200,1536]{1,0:T(8,128)(2,1)}, f16[200,1536]{1,0:T(8,128)(2,1)}, u32[]{:S(2)}, u32[]{:S(2)}) collective-permute-start(f16[200,1536]{1,0:T(8,128)(2,1)} %get-tuple-element.47), channel_id=1, source_target_pairs={{0,96},{4,100},{8,104},{12,108},{16,112},{20,116},{24,120},{28,124... | collective-permute-start | bytes 1843208 | tf_op jit(solution)/shard_map/ppermute | solution.py:105
  29.5 28.0 %collective-permute-start.3 = (f16[200,1536]{1,0:T(8,128)(2,1)}, f16[200,1536]{1,0:T(8,128)(2,1)S(1)}, u32[]{:S(2)}, u32[]{:S(2)}) collective-permute-start(f16[200,1536]{1,0:T(8,128)(2,1)} %get-tuple-element.45), channel_id=1, source_target_pairs={{0,64},{4,68},{8,72},{12,76},{16,80},{20,84},{24,88},{28,92},{32,9... | collective-permute-start | bytes 1843208 | tf_op jit(solution)/shard_map/ppermute | solution.py:105
  40.6 33.0 %collective-permute-start.9 = (f16[200,1536]{1,0:T(8,128)(2,1)}, f16[200,1536]{1,0:T(8,128)(2,1)S(1)}, u32[]{:S(2)}, u32[]{:S(2)}) collective-permute-start(f16[200,1536]{1,0:T(8,128)(2,1)} %get-tuple-element.87), channel_id=1, source_target_pairs={{0,16},{4,20},{8,24},{12,28},{16,0},{20,4},{24,8},{28,12},{32,48},... | collective-permute-start | bytes 1843208 | tf_op jit(solution)/shard_map/ppermute | solution.py:105
  44.2 29.0 %collective-permute-start.10 = (f16[200,1536]{1,0:T(8,128)(2,1)}, f16[200,1536]{1,0:T(8,128)(2,1)S(1)}, u32[]{:S(2)}, u32[]{:S(2)}) collective-permute-start(f16[200,1536]{1,0:T(8,128)(2,1)} %get-tuple-element.89), channel_id=1, source_target_pairs={{0,8},{4,12},{8,16},{12,20},{16,24},{20,28},{24,0},{28,4},{32,40},... | collective-permute-start | bytes 1843208 | tf_op jit(solution)/shard_map/ppermute | solution.py:105
  46.6 26.8 %collective-permute-start.11 = (f16[200,1536]{1,0:T(8,128)(2,1)}, f16[200,1536]{1,0:T(8,128)(2,1)S(1)}, u32[]{:S(2)}, u32[]{:S(2)}) collective-permute-start(f16[200,1536]{1,0:T(8,128)(2,1)} %get-tuple-element.88), channel_id=1, source_target_pairs={{0,24},{4,28},{8,0},{12,4},{16,8},{20,12},{24,16},{28,20},{32,56},... | collective-permute-start | bytes 1843208 | tf_op jit(solution)/shard_map/ppermute | solution.py:105
  63.1 15.3 %collective-permute-start.6 = (f32[56,1536]{1,0:T(8,128)}, f32[56,1536]{1,0:T(8,128)S(1)}, u32[]{:S(2)}, u32[]{:S(2)}) collective-permute-start(f32[56,1536]{1,0:T(8,128)} %get-tuple-element.99), channel_id=1, source_target_pairs={{0,16},{4,20},{8,24},{12,28},{16,0},{20,4},{24,8},{28,12},{32,48},... | collective-permute-start | bytes 1032200 | tf_op jit(solution)/shard_map/ppermute | solution.py:105
  66.7 19.9 %collective-permute-start.7 = (f32[56,1536]{1,0:T(8,128)}, f32[56,1536]{1,0:T(8,128)S(1)}, u32[]{:S(2)}, u32[]{:S(2)}) collective-permute-start(f32[56,1536]{1,0:T(8,128)} %get-tuple-element.100), channel_id=1, source_target_pairs={{0,8},{4,12},{8,16},{12,20},{16,24},{20,28},{24,0},{28,4},{32,40},... | collective-permute-start | bytes 1032200 | tf_op jit(solution)/shard_map/ppermute | solution.py:105
  73.2 13.4 %collective-permute-start.8 = (f32[56,1536]{1,0:T(8,128)}, f32[56,1536]{1,0:T(8,128)S(1)}, u32[]{:S(2)}, u32[]{:S(2)}) collective-permute-start(f32[56,1536]{1,0:T(8,128)} %get-tuple-element.97), channel_id=1, source_target_pairs={{0,24},{4,28},{8,0},{12,4},{16,8},{20,12},{24,16},{28,20},{32,56},... | collective-permute-start | bytes 1032200 | tf_op jit(solution)/shard_map/ppermute | solution.py:105
  76.8 10.0 %collective-permute-start.12 = (f32[56,1536]{1,0:T(8,128)S(1)}, f32[56,1536]{1,0:T(8,128)S(1)}, u32[]{:S(2)}, u32[]{:S(2)}) collective-permute-start(f32[56,1536]{1,0:T(8,128)S(1)} %get-tuple-element.96), channel_id=1, source_target_pairs={{0,64},{4,68},{8,72},{12,76},{16,80},{20,84},{24,88},{28,92},{32,9... | collective-permute-start | bytes 1032200 | tf_op jit(solution)/shard_map/ppermute | solution.py:105
  78.3 17.4 %collective-permute-start.13 = (f32[56,1536]{1,0:T(8,128)S(1)}, f32[56,1536]{1,0:T(8,128)S(1)}, u32[]{:S(2)}, u32[]{:S(2)}) collective-permute-start(f32[56,1536]{1,0:T(8,128)S(1)} %get-tuple-element.95), channel_id=1, source_target_pairs={{0,32},{4,36},{8,40},{12,44},{16,48},{20,52},{24,56},{28,60},{32,6... | collective-permute-start | bytes 1032200 | tf_op jit(solution)/shard_map/ppermute | solution.py:105
  78.3 17.4 %collective-permute-start.14 = (f32[56,1536]{1,0:T(8,128)S(1)}, f32[56,1536]{1,0:T(8,128)S(1)}, u32[]{:S(2)}, u32[]{:S(2)}) collective-permute-start(f32[56,1536]{1,0:T(8,128)S(1)} %get-tuple-element.94), channel_id=1, source_target_pairs={{0,96},{4,100},{8,104},{12,108},{16,112},{20,116},{24,120},{28,124... | collective-permute-start | bytes 1032200 | tf_op jit(solution)/shard_map/ppermute | solution.py:105
  97.4 5.0 %collective-permute-start.16 = (f32[8,128]{1,0:T(8,128)S(1)}, f32[8,128]{1,0:T(8,128)S(1)}, u32[]{:S(2)}, u32[]{:S(2)}) collective-permute-start(f32[8,128]{1,0:T(8,128)S(1)} %add.531), channel_id=1, source_target_pairs={{0,32},{4,36},{8,40},{12,44},{16,48},{20,52},{24,56},{28,60},{32,6... | collective-permute-start | bytes 12296 | tf_op jit(solution)/shard_map/ppermute | solution.py:105
  97.7 4.7 %collective-permute-start.17 = (f32[8,128]{1,0:T(8,128)S(1)}, f32[8,128]{1,0:T(8,128)S(1)}, u32[]{:S(2)}, u32[]{:S(2)}) collective-permute-start(f32[8,128]{1,0:T(8,128)S(1)} %add.531), channel_id=1, source_target_pairs={{0,64},{4,68},{8,72},{12,76},{16,80},{20,84},{24,88},{28,92},{32,9... | collective-permute-start | bytes 12296 | tf_op jit(solution)/shard_map/ppermute | solution.py:105
  99.4 3.0 %collective-permute-start.18 = (f32[8,128]{1,0:T(8,128)S(1)}, f32[8,128]{1,0:T(8,128)S(1)}, u32[]{:S(2)}, u32[]{:S(2)}) collective-permute-start(f32[8,128]{1,0:T(8,128)S(1)} %add.531), channel_id=1, source_target_pairs={{0,96},{4,100},{8,104},{12,108},{16,112},{20,116},{24,120},{28,124... | collective-permute-start | bytes 12296 | tf_op jit(solution)/shard_map/ppermute | solution.py:105
  101.2 8.5 %collective-permute-start.22 = (f32[32,3072]{1,0:T(8,128)S(1)}, f32[32,3072]{1,0:T(8,128)S(1)}, u32[]{:S(2)}, u32[]{:S(2)}) collective-permute-start(f32[32,3072]{1,0:T(8,128)S(1)} %select_maximum_fusion), channel_id=1, source_target_pairs={{0,4},{4,0},{8,12},{12,8},{16,20},{20,16},{24,28},{28,24},{32,36},... | collective-permute-start | bytes 1179656 | tf_op jit(solution)/shard_map/ppermute | solution.py:105
  102.4 4.6 %collective-permute-start.19 = (f32[8,128]{1,0:T(8,128)S(1)}, f32[8,128]{1,0:T(8,128)S(1)}, u32[]{:S(2)}, u32[]{:S(2)}) collective-permute-start(f32[8,128]{1,0:T(8,128)S(1)} %add_add_fusion.1), channel_id=1, source_target_pairs={{0,8},{4,12},{8,16},{12,20},{16,24},{20,28},{24,0},{28,4},{32,40},... | collective-permute-start | bytes 12296 | tf_op jit(solution)/shard_map/ppermute | solution.py:105
  103.9 4.0 %collective-permute-start.20 = (f32[8,128]{1,0:T(8,128)S(1)}, f32[8,128]{1,0:T(8,128)S(1)}, u32[]{:S(2)}, u32[]{:S(2)}) collective-permute-start(f32[8,128]{1,0:T(8,128)S(1)} %add_add_fusion.1), channel_id=1, source_target_pairs={{0,16},{4,20},{8,24},{12,28},{16,0},{20,4},{24,8},{28,12},{32,48},... | collective-permute-start | bytes 12296 | tf_op jit(solution)/shard_map/ppermute | solution.py:105
  106.9 2.8 %collective-permute-start.21 = (f32[8,128]{1,0:T(8,128)S(1)}, f32[8,128]{1,0:T(8,128)S(1)}, u32[]{:S(2)}, u32[]{:S(2)}) collective-permute-start(f32[8,128]{1,0:T(8,128)S(1)} %add_add_fusion.1), channel_id=1, source_target_pairs={{0,24},{4,28},{8,0},{12,4},{16,8},{20,12},{24,16},{28,20},{32,56},... | collective-permute-start | bytes 12296 | tf_op jit(solution)/shard_map/ppermute | solution.py:105
  111.4 5.0 %collective-permute-start.23 = (f32[8,128]{1,0:T(8,128)S(1)}, f32[8,128]{1,0:T(8,128)S(1)}, u32[]{:S(2)}, u32[]{:S(2)}) collective-permute-start(f32[8,128]{1,0:T(8,128)S(1)} %add_add_fusion), channel_id=1, source_target_pairs={{0,1},{1,2},{2,3},{3,0},{4,5},{5,6},{6,7},{7,4},{8,9},{9,10},{10,1... | collective-permute-start | bytes 12296 | tf_op jit(solution)/shard_map/ppermute | solution.py:109
  112.8 4.0 %collective-permute-start.24 = (f32[8,128]{1,0:T(8,128)S(1)}, f32[8,128]{1,0:T(8,128)S(1)}, u32[]{:S(2)}, u32[]{:S(2)}) collective-permute-start(f32[8,128]{1,0:T(8,128)S(1)} %add_add_fusion), channel_id=1, source_target_pairs={{0,2},{1,3},{2,0},{3,1},{4,6},{5,7},{6,4},{7,5},{8,10},{9,11},{10,... | collective-permute-start | bytes 12296 | tf_op jit(solution)/shard_map/ppermute | solution.py:109
  115.4 2.5 %collective-permute-start.25 = (f32[8,128]{1,0:T(8,128)S(1)}, f32[8,128]{1,0:T(8,128)S(1)}, u32[]{:S(2)}, u32[]{:S(2)}) collective-permute-start(f32[8,128]{1,0:T(8,128)S(1)} %add_add_fusion), channel_id=1, source_target_pairs={{0,3},{1,0},{2,1},{3,2},{4,7},{5,4},{6,5},{7,6},{8,11},{9,8},{10,9... | collective-permute-start | bytes 12296 | tf_op jit(solution)/shard_map/ppermute | solution.py:109
  121.6 4.8 %collective-permute-start.26 = (bf16[24,3072]{1,0:T(8,128)(2,1)S(1)}, bf16[24,3072]{1,0:T(8,128)(2,1)S(1)}, u32[]{:S(2)}, u32[]{:S(2)}) collective-permute-start(bf16[24,3072]{1,0:T(8,128)(2,1)S(1)} %get-tuple-element.120), channel_id=1, source_target_pairs={{0,24},{4,28},{8,0},{12,4},{16,8},{20,12},{24,16},{28,20},{32,56},... | collective-permute-start | bytes 442376 | tf_op jit(solution)/shard_map/ppermute | solution.py:105
  122.5 6.9 %collective-permute-start.27 = (bf16[24,3072]{1,0:T(8,128)(2,1)S(1)}, bf16[24,3072]{1,0:T(8,128)(2,1)S(1)}, u32[]{:S(2)}, u32[]{:S(2)}) collective-permute-start(bf16[24,3072]{1,0:T(8,128)(2,1)S(1)} %get-tuple-element.120), channel_id=1, source_target_pairs={{0,16},{4,20},{8,24},{12,28},{16,0},{20,4},{24,8},{28,12},{32,48},... | collective-permute-start | bytes 442376 | tf_op jit(solution)/shard_map/ppermute | solution.py:105
  122.9 6.7 %collective-permute-start.28 = (bf16[24,3072]{1,0:T(8,128)(2,1)S(1)}, bf16[24,3072]{1,0:T(8,128)(2,1)S(1)}, u32[]{:S(2)}, u32[]{:S(2)}) collective-permute-start(bf16[24,3072]{1,0:T(8,128)(2,1)S(1)} %get-tuple-element.120), channel_id=1, source_target_pairs={{0,8},{4,12},{8,16},{12,20},{16,24},{20,28},{24,0},{28,4},{32,40},... | collective-permute-start | bytes 442376 | tf_op jit(solution)/shard_map/ppermute | solution.py:105
  123.7 5.7 %collective-permute-start.29 = (bf16[24,3072]{1,0:T(8,128)(2,1)S(1)}, bf16[24,3072]{1,0:T(8,128)(2,1)S(1)}, u32[]{:S(2)}, u32[]{:S(2)}) collective-permute-start(bf16[24,3072]{1,0:T(8,128)(2,1)S(1)} %get-tuple-element.119), channel_id=1, source_target_pairs={{0,96},{4,100},{8,104},{12,108},{16,112},{20,116},{24,120},{28,124... | collective-permute-start | bytes 442376 | tf_op jit(solution)/shard_map/ppermute | solution.py:105
  125.8 5.6 %collective-permute-start.30 = (bf16[24,3072]{1,0:T(8,128)(2,1)S(1)}, bf16[24,3072]{1,0:T(8,128)(2,1)S(1)}, u32[]{:S(2)}, u32[]{:S(2)}) collective-permute-start(bf16[24,3072]{1,0:T(8,128)(2,1)S(1)} %get-tuple-element.119), channel_id=1, source_target_pairs={{0,64},{4,68},{8,72},{12,76},{16,80},{20,84},{24,88},{28,92},{32,9... | collective-permute-start | bytes 442376 | tf_op jit(solution)/shard_map/ppermute | solution.py:105
  126.4 6.8 %collective-permute-start.31 = (bf16[24,3072]{1,0:T(8,128)(2,1)S(1)}, bf16[24,3072]{1,0:T(8,128)(2,1)S(1)}, u32[]{:S(2)}, u32[]{:S(2)}) collective-permute-start(bf16[24,3072]{1,0:T(8,128)(2,1)S(1)} %get-tuple-element.119), channel_id=1, source_target_pairs={{0,32},{4,36},{8,40},{12,44},{16,48},{20,52},{24,56},{28,60},{32,6... | collective-permute-start | bytes 442376 | tf_op jit(solution)/shard_map/ppermute | solution.py:105
  133.4 11.9 %collective-permute-start.36 = (bf16[4,24,3072]{2,1,0:T(8,128)(2,1)S(1)}, bf16[4,24,3072]{2,1,0:T(8,128)(2,1)S(1)}, u32[]{:S(2)}, u32[]{:S(2)}) collective-permute-start(bf16[4,24,3072]{2,1,0:T(8,128)(2,1)S(1)} %constant_dynamic-slice_fusion.6), channel_id=1, source_target_pairs={{0,4},{4,0},{8,12},{12,8},{16,20},{20,16},{24,28},{28,24},{32,36},... | collective-permute-start | bytes 1769480 | tf_op jit(solution)/shard_map/ppermute | solution.py:105
  140.7 16.0 %collective-permute-start.32 = (bf16[4,24,3072]{2,1,0:T(8,128)(2,1)S(1)}, bf16[4,24,3072]{2,1,0:T(8,128)(2,1)S(1)}, u32[]{:S(2)}, u32[]{:S(2)}) collective-permute-start(bf16[4,24,3072]{2,1,0:T(8,128)(2,1)S(1)} %constant_dynamic-slice_fusion.6), channel_id=1, source_target_pairs={{0,32},{4,36},{8,40},{12,44},{16,48},{20,52},{24,56},{28,60},{32,6... | collective-permute-start | bytes 1769480 | tf_op jit(solution)/shard_map/ppermute | solution.py:105
  140.7 7.2 %collective-permute-start.37 = (bf16[4,24,3072]{2,1,0:T(8,128)(2,1)S(1)}, bf16[4,24,3072]{2,1,0:T(8,128)(2,1)S(1)}, u32[]{:S(2)}, u32[]{:S(2)}) collective-permute-start(bf16[4,24,3072]{2,1,0:T(8,128)(2,1)S(1)} %constant_dynamic-slice_fusion.5), channel_id=1, source_target_pairs={{0,4},{4,0},{8,12},{12,8},{16,20},{20,16},{24,28},{28,24},{32,36},... | collective-permute-start | bytes 1769480 | tf_op jit(solution)/shard_map/ppermute | solution.py:105
  141.0 15.9 %collective-permute-start.33 = (bf16[4,24,3072]{2,1,0:T(8,128)(2,1)S(1)}, bf16[4,24,3072]{2,1,0:T(8,128)(2,1)S(1)}, u32[]{:S(2)}, u32[]{:S(2)}) collective-permute-start(bf16[4,24,3072]{2,1,0:T(8,128)(2,1)S(1)} %constant_dynamic-slice_fusion.5), channel_id=1, source_target_pairs={{0,8},{4,12},{8,16},{12,20},{16,24},{20,28},{24,0},{28,4},{32,40},... | collective-permute-start | bytes 1769480 | tf_op jit(solution)/shard_map/ppermute | solution.py:105
  142.4 15.2 %collective-permute-start.34 = (bf16[4,24,3072]{2,1,0:T(8,128)(2,1)S(1)}, bf16[4,24,3072]{2,1,0:T(8,128)(2,1)S(1)}, u32[]{:S(2)}, u32[]{:S(2)}) collective-permute-start(bf16[4,24,3072]{2,1,0:T(8,128)(2,1)S(1)} %constant_dynamic-slice_fusion.6), channel_id=1, source_target_pairs={{0,96},{4,100},{8,104},{12,108},{16,112},{20,116},{24,120},{28,124... | collective-permute-start | bytes 1769480 | tf_op jit(solution)/shard_map/ppermute | solution.py:105
  145.3 14.3 %collective-permute-start.35 = (bf16[4,24,3072]{2,1,0:T(8,128)(2,1)S(1)}, bf16[4,24,3072]{2,1,0:T(8,128)(2,1)S(1)}, u32[]{:S(2)}, u32[]{:S(2)}) collective-permute-start(bf16[4,24,3072]{2,1,0:T(8,128)(2,1)S(1)} %constant_dynamic-slice_fusion.5), channel_id=1, source_target_pairs={{0,24},{4,28},{8,0},{12,4},{16,8},{20,12},{24,16},{28,20},{32,56},... | collective-permute-start | bytes 1769480 | tf_op jit(solution)/shard_map/ppermute | solution.py:105
  159.6 3.1 %collective-permute-start.42 = (bf16[4,24,3072]{2,1,0:T(8,128)(2,1)S(1)}, bf16[4,24,3072]{2,1,0:T(8,128)(2,1)S(1)}, u32[]{:S(2)}, u32[]{:S(2)}) collective-permute-start(bf16[4,24,3072]{2,1,0:T(8,128)(2,1)S(1)} %collective-permute-done.32), channel_id=1, source_target_pairs={{0,4},{4,0},{8,12},{12,8},{16,20},{20,16},{24,28},{28,24},{32,36},... | collective-permute-start | bytes 1769480 | tf_op jit(solution)/shard_map/ppermute | solution.py:105
  161.1 2.8 %collective-permute-start.43 = (bf16[4,24,3072]{2,1,0:T(8,128)(2,1)S(1)}, bf16[4,24,3072]{2,1,0:T(8,128)(2,1)S(1)}, u32[]{:S(2)}, u32[]{:S(2)}) collective-permute-start(bf16[4,24,3072]{2,1,0:T(8,128)(2,1)S(1)} %collective-permute-done.33), channel_id=1, source_target_pairs={{0,4},{4,0},{8,12},{12,8},{16,20},{20,16},{24,28},{28,24},{32,36},... | collective-permute-start | bytes 1769480 | tf_op jit(solution)/shard_map/ppermute | solution.py:105
  161.1 4.6 %collective-permute-start.44 = (bf16[4,24,3072]{2,1,0:T(8,128)(2,1)S(1)}, bf16[4,24,3072]{2,1,0:T(8,128)(2,1)S(1)}, u32[]{:S(2)}, u32[]{:S(2)}) collective-permute-start(bf16[4,24,3072]{2,1,0:T(8,128)(2,1)S(1)} %collective-permute-done.34), channel_id=1, source_target_pairs={{0,4},{4,0},{8,12},{12,8},{16,20},{20,16},{24,28},{28,24},{32,36},... | collective-permute-start | bytes 1769480 | tf_op jit(solution)/shard_map/ppermute | solution.py:105
  161.6 5.7 %collective-permute-start.45 = (bf16[4,24,3072]{2,1,0:T(8,128)(2,1)S(1)}, bf16[4,24,3072]{2,1,0:T(8,128)(2,1)S(1)}, u32[]{:S(2)}, u32[]{:S(2)}) collective-permute-start(bf16[4,24,3072]{2,1,0:T(8,128)(2,1)S(1)} %collective-permute-done.35), channel_id=1, source_target_pairs={{0,4},{4,0},{8,12},{12,8},{16,20},{20,16},{24,28},{28,24},{32,36},... | collective-permute-start | bytes 1769480 | tf_op jit(solution)/shard_map/ppermute | solution.py:105
  161.8 10.9 %collective-permute-start.38 = (bf16[2,24,3072]{2,1,0:T(8,128)(2,1)S(1)}, bf16[2,24,3072]{2,1,0:T(8,128)(2,1)S(1)}, u32[]{:S(2)}, u32[]{:S(2)}) collective-permute-start(bf16[2,24,3072]{2,1,0:T(8,128)(2,1)S(1)} %slice.361), channel_id=1, source_target_pairs={{0,32},{4,36},{8,40},{12,44},{16,48},{20,52},{24,56},{28,60},{32,6... | collective-permute-start | bytes 884744 | tf_op jit(solution)/shard_map/ppermute | solution.py:105
  162.7 10.0 %collective-permute-start.39 = (bf16[2,24,3072]{2,1,0:T(8,128)(2,1)S(1)}, bf16[2,24,3072]{2,1,0:T(8,128)(2,1)S(1)}, u32[]{:S(2)}, u32[]{:S(2)}) collective-permute-start(bf16[2,24,3072]{2,1,0:T(8,128)(2,1)S(1)} %slice.362), channel_id=1, source_target_pairs={{0,8},{4,12},{8,16},{12,20},{16,24},{20,28},{24,0},{28,4},{32,40},... | collective-permute-start | bytes 884744 | tf_op jit(solution)/shard_map/ppermute | solution.py:105
  163.8 8.9 %collective-permute-start.40 = (bf16[2,24,3072]{2,1,0:T(8,128)(2,1)S(1)}, bf16[2,24,3072]{2,1,0:T(8,128)(2,1)S(1)}, u32[]{:S(2)}, u32[]{:S(2)}) collective-permute-start(bf16[2,24,3072]{2,1,0:T(8,128)(2,1)S(1)} %slice.363), channel_id=1, source_target_pairs={{0,96},{4,100},{8,104},{12,108},{16,112},{20,116},{24,120},{28,124... | collective-permute-start | bytes 884744 | tf_op jit(solution)/shard_map/ppermute | solution.py:105
  165.7 7.2 %collective-permute-start.41 = (bf16[2,24,3072]{2,1,0:T(8,128)(2,1)S(1)}, bf16[2,24,3072]{2,1,0:T(8,128)(2,1)S(1)}, u32[]{:S(2)}, u32[]{:S(2)}) collective-permute-start(bf16[2,24,3072]{2,1,0:T(8,128)(2,1)S(1)} %slice.364), channel_id=1, source_target_pairs={{0,24},{4,28},{8,0},{12,4},{16,8},{20,12},{24,16},{28,20},{32,56},... | collective-permute-start | bytes 884744 | tf_op jit(solution)/shard_map/ppermute | solution.py:105
  172.8 4.1 %collective-permute-start.46 = (bf16[2,24,3072]{2,1,0:T(8,128)(2,1)S(1)}, bf16[2,24,3072]{2,1,0:T(8,128)(2,1)S(1)}, u32[]{:S(2)}, u32[]{:S(2)}) collective-permute-start(bf16[2,24,3072]{2,1,0:T(8,128)(2,1)S(1)} %collective-permute-done.38), channel_id=1, source_target_pairs={{0,4},{4,0},{8,12},{12,8},{16,20},{20,16},{24,28},{28,24},{32,36},... | collective-permute-start | bytes 884744 | tf_op jit(solution)/shard_map/ppermute | solution.py:105
  176.4 2.6 %collective-permute-start.48 = (bf16[2,24,3072]{2,1,0:T(8,128)(2,1)S(1)}, bf16[2,24,3072]{2,1,0:T(8,128)(2,1)S(1)}, u32[]{:S(2)}, u32[]{:S(2)}) collective-permute-start(bf16[2,24,3072]{2,1,0:T(8,128)(2,1)S(1)} %collective-permute-done.40), channel_id=1, source_target_pairs={{0,4},{4,0},{8,12},{12,8},{16,20},{20,16},{24,28},{28,24},{32,36},... | collective-permute-start | bytes 884744 | tf_op jit(solution)/shard_map/ppermute | solution.py:105
  176.9 3.1 %collective-permute-start.49 = (bf16[2,24,3072]{2,1,0:T(8,128)(2,1)S(1)}, bf16[2,24,3072]{2,1,0:T(8,128)(2,1)S(1)}, u32[]{:S(2)}, u32[]{:S(2)}) collective-permute-start(bf16[2,24,3072]{2,1,0:T(8,128)(2,1)S(1)} %collective-permute-done.41), channel_id=1, source_target_pairs={{0,4},{4,0},{8,12},{12,8},{16,20},{20,16},{24,28},{28,24},{32,36},... | collective-permute-start | bytes 884744 | tf_op jit(solution)/shard_map/ppermute | solution.py:105
  (13 other events, 71.0 us)

commit v6 on v5

--- a/solution.py
+++ b/solution.py
@@ -123,7 +123,8 @@
             array = array + shift(array, dc=1)
         else:
             move = {"x": along_x, "z": along_z, "y": shift_y}[way]
-            array = array + move(array, 1) + move(array, 2) + move(array, 3)
+            parts = lax.optimization_barrier([move(array, d) for d in (2, 1, 3)])
+            array = array + parts[0] + parts[1] + parts[2]
     return array
 
 
@@ -181,7 +182,7 @@
 
 
 def gather_line(own, me, move):
-    got = [own] + [move(own, d) for d in (1, 2, 3)]
+    got = [own, *lax.optimization_barrier([move(own, d) for d in (1, 2, 3)])]
     turned = jnp.stack([got[3], got[2], got[1], got[0], got[3], got[2], got[1]])
     return lax.dynamic_slice_in_dim(turned, 3 - me, 4, axis=0)
 

time: 182 us -> 180 us (0.989)
  waiting for transfers between devices: 54.5 us -> 48.4 us
  starting transfers between devices: 63.4 us -> 68.1 us
    ppermute x47, waiting for transfers between devices: 53.1 us -> 47.4 us  [shift(): return lax.ppermute(array, 'dp', pairs)]
    ppermute x47, starting transfers between devices: 58.4 us -> 62.5 us  [shift(): return lax.ppermute(array, 'dp', pairs)]
  transfers between devices with their start and end apart: 50 -> 50, of which waited for: 20 -> 15; matrix products, arithmetic and copies ran while one was open for 19% -> 19% of each run, Pallas kernels for 9% -> 9%
where the time goes in v6:
time: 180 us
  starting transfers between devices  68.1 us (38%)
  waiting for transfers between devices  48.4 us (27%)
  other arithmetic  34 us (19%)
  Pallas kernels  16 us (9%)
  local copies, waits for them, and re-layouts  10.4 us (6%)
  between operations  2.86 us (2%)
    ppermute x47, starting transfers between devices, shift(): return lax.ppermute(array, 'dp', pairs)  62.5 us
    ppermute x47, waiting for transfers between devices, shift(): return lax.ppermute(array, 'dp', pairs)  47.4 us
    pallas_call x2, Pallas kernels, chip_product(): pl.pallas_call(functools.partial(product_kernel, x_first), grid_spec=pltp...  16 us
    dynamic_update_slice x10, other arithmetic, put(): return lax.dynamic_update_slice(full, piece, at)  12.3 us
    dynamic_slice x2, local copies, waits for them, and re-layouts, columns(): return lax.dynamic_slice(array, (0, start), (tokens, sizes[which]))  7.61 us
    add x4, other arithmetic, coded_sum(): total, bias = (total + value, bias + line)  5.7 us
    ppermute x3, starting transfers between devices, shift_y(): return lax.ppermute(array, 'mp', [(y, (y + dy) % Y) for y in range(Y)])  5.66 us
  transfers between devices with their start and end apart: 50, of which 15 were waited for; matrix products, arithmetic and copies ran while one was open for 19% of the time, Pallas kernels for 9%

profile of v6, /device:TPU:1, one launch (start us, length us, event | category | flops | bytes accessed | tf_op | source)
XLA Modules:
  0.0 179.8 jit_solution(16738609338192512257)
XLA Ops:
  0.7 3.7 %constant_dynamic-slice_fusion.13 = bf16[1024,1536]{1,0:T(8,128)(2,1)} fusion(bf16[1024,6144]{1,0:T(8,128)(2,1)} %own_cols.3, s32[]{:T(128)S(6)} %select_n.316), kind=kLoop, calls=%fused_computation.150 | loop fusion | bytes 6291460 | tf_op jit(solution)/shard_map/dynamic_slice | solution.py:271
  4.4 1.4 collective-permute-start.1
  5.8 3.9 %constant_dynamic-slice_fusion.12 = bf16[1024,1536]{1,0:T(8,128)(2,1)} fusion(bf16[1024,6144]{1,0:T(8,128)(2,1)} %own_cols.3, s32[]{:T(128)S(6)} %select_n.320), kind=kLoop, calls=%fused_computation.149 | loop fusion | bytes 6291460 | tf_op jit(solution)/shard_map/dynamic_slice | solution.py:271
  10.4 5.2 %collective-permute-done.other = bf16[1024,768]{1,0:T(8,128)(2,1)S(1)} collective-permute-done((bf16[1024,768]{1,0:T(8,128)(2,1)S(1)}, bf16[1024,768]{1,0:T(8,128)(2,1)S(1)}, u32[]{:S(2)}, u32[]{:S(2)}) %collective-permute-start) | collective-permute-done | bytes 1572896 | tf_op jit(solution)/shard_map/ppermute | solution.py:105
  15.6 8.0 %shard_map.177 = f32[4,200,1536]{2,1,0:T(8,128)S(1)} custom-call(s32[1]{0:T(128)} %bitcast.side, bf16[1024,768]{1,0:T(8,128)(2,1)S(1)} %copy-done.2, bf16[1024,768]{1,0:T(8,128)(2,1)S(1)} %collective-permute-done.other, bf16[1024,6144]{1,0:T(8,128)(2,1)} %own_cols.3, bf16[1024,1536]{1,0:T(8,128)(2,1)} %collective-permute-done.1.other_cols, ...), custom_call_target="tpu_custom_call" | custom-call | flops 1 | bytes 1 | tf_op jit(solution)/shard_map/pallas_call | solution.py:72
  23.6 2.0 %dynamic-slice_bitcast_fusion = (f32[200,1536]{1,0:T(8,128)}, f16[200,1536]{1,0:T(8,128)(2,1)}, f16[200,1536]{1,0:T(8,128)(2,1)}, f16[200,1536]{1,0:T(8,128)(2,1)}) fusion(f32[4,200,1536]{2,1,0:T(8,128)S(1)} %shard_map.177, s32[]{:T(128)S(6)} %select_n.319, s32[]{:T(128)S(6)} %select_n.326, s32[]{:T(128)S(6)} %select_n.324, s32[]{:T(128)S(6)} %select_n.322), kind=kLoop, calls=%fused_computation.22 | loop fusion | flops 921600 | bytes 7987216 | tf_op jit(solution)/shard_map/jit(dynamic_index_in_dim)/squeeze | solution.py:132
  26.8 1.3 collective-permute-start.4
  28.1 1.4 collective-permute-start.5
  29.5 1.6 collective-permute-start.3
  31.1 8.0 %shard_map.178 = f32[4,200,1536]{2,1,0:T(8,128)S(1)} custom-call(s32[1]{0:T(128)} %bitcast.17.side, bf16[1024,768]{1,0:T(8,128)(2,1)S(1)} %copy-done.2, bf16[1024,768]{1,0:T(8,128)(2,1)S(1)} %collective-permute-done.other, bf16[1024,6144]{1,0:T(8,128)(2,1)} %own_cols.3, bf16[1024,1536]{1,0:T(8,128)(2,1)} %collective-permute-done.2.other_cols, ...), custom_call_target="tpu_custom_call" | custom-call | flops 1 | bytes 1 | tf_op jit(solution)/shard_map/pallas_call | solution.py:72
  39.1 1.5 fusion.11
  40.6 3.6 %collective-permute-start.9 = (f16[200,1536]{1,0:T(8,128)(2,1)}, f16[200,1536]{1,0:T(8,128)(2,1)S(1)}, u32[]{:S(2)}, u32[]{:S(2)}) collective-permute-start(f16[200,1536]{1,0:T(8,128)(2,1)} %get-tuple-element.117), channel_id=1, source_target_pairs={{0,16},{4,20},{8,24},{12,28},{16,0},{20,4},{24,8},{28,12},{32,48},... | collective-permute-start | bytes 1843208 | tf_op jit(solution)/shard_map/ppermute | solution.py:105
  46.6 2.0 %collective-permute-start.11 = (f16[200,1536]{1,0:T(8,128)(2,1)}, f16[200,1536]{1,0:T(8,128)(2,1)S(1)}, u32[]{:S(2)}, u32[]{:S(2)}) collective-permute-start(f16[200,1536]{1,0:T(8,128)(2,1)} %get-tuple-element.118), channel_id=1, source_target_pairs={{0,24},{4,28},{8,0},{12,4},{16,8},{20,12},{24,16},{28,20},{32,56},... | collective-permute-start | bytes 1843208 | tf_op jit(solution)/shard_map/ppermute | solution.py:105
  51.1 6.4 %collective-permute-done.3 = f16[200,1536]{1,0:T(8,128)(2,1)S(1)} collective-permute-done((f16[200,1536]{1,0:T(8,128)(2,1)}, f16[200,1536]{1,0:T(8,128)(2,1)S(1)}, u32[]{:S(2)}, u32[]{:S(2)}) %collective-permute-start.3) | collective-permute-done | bytes 614432 | tf_op jit(solution)/shard_map/ppermute | solution.py:105
  58.8 1.8 fusion.4
  63.1 3.6 %collective-permute-start.6 = (f32[56,1536]{1,0:T(8,128)}, f32[56,1536]{1,0:T(8,128)S(1)}, u32[]{:S(2)}, u32[]{:S(2)}) collective-permute-start(f32[56,1536]{1,0:T(8,128)} %get-tuple-element.129), channel_id=1, source_target_pairs={{0,16},{4,20},{8,24},{12,28},{16,0},{20,4},{24,8},{28,12},{32,48},... | collective-permute-start | bytes 1032200 | tf_op jit(solution)/shard_map/ppermute | solution.py:105
  67.4 5.8 %collective-permute-done.10 = f16[200,1536]{1,0:T(8,128)(2,1)S(1)} collective-permute-done((f16[200,1536]{1,0:T(8,128)(2,1)}, f16[200,1536]{1,0:T(8,128)(2,1)S(1)}, u32[]{:S(2)}, u32[]{:S(2)}) %collective-permute-start.10) | collective-permute-done | bytes 614432 | tf_op jit(solution)/shard_map/ppermute | solution.py:105
  74.8 1.8 fusion
  76.8 1.5 collective-permute-start.12
  78.3 2.7 %collective-permute-start.14 = (f32[56,1536]{1,0:T(8,128)S(1)}, f32[56,1536]{1,0:T(8,128)S(1)}, u32[]{:S(2)}, u32[]{:S(2)}) collective-permute-start(f32[56,1536]{1,0:T(8,128)S(1)} %get-tuple-element.124), channel_id=1, source_target_pairs={{0,96},{4,100},{8,104},{12,108},{16,112},{20,116},{24,120},{28,124... | collective-permute-start | bytes 1032200 | tf_op jit(solution)/shard_map/ppermute | solution.py:105
  81.1 5.6 %collective-permute-done.7 = f32[56,1536]{1,0:T(8,128)S(1)} collective-permute-done((f32[56,1536]{1,0:T(8,128)}, f32[56,1536]{1,0:T(8,128)S(1)}, u32[]{:S(2)}, u32[]{:S(2)}) %collective-permute-start.7) | collective-permute-done | bytes 344096 | tf_op jit(solution)/shard_map/ppermute | solution.py:105
  86.8 8.9 %collective-permute-done.13 = f32[56,1536]{1,0:T(8,128)S(1)} collective-permute-done((f32[56,1536]{1,0:T(8,128)S(1)}, f32[56,1536]{1,0:T(8,128)S(1)}, u32[]{:S(2)}, u32[]{:S(2)}) %collective-permute-start.13) | collective-permute-done | bytes 344096 | tf_op jit(solution)/shard_map/ppermute | solution.py:105
  97.4 1.4 collective-permute-start.16
  98.8 2.7 %collective-permute-start.18 = (f32[8,128]{1,0:T(8,128)S(1)}, f32[8,128]{1,0:T(8,128)S(1)}, u32[]{:S(2)}, u32[]{:S(2)}) collective-permute-start(f32[8,128]{1,0:T(8,128)S(1)} %add.531), channel_id=1, source_target_pairs={{0,96},{4,100},{8,104},{12,108},{16,112},{20,116},{24,120},{28,124... | collective-permute-start | bytes 12296 | tf_op jit(solution)/shard_map/ppermute | solution.py:105
  103.0 1.4 collective-permute-start.19
  104.4 2.5 %collective-permute-start.20 = (f32[8,128]{1,0:T(8,128)S(1)}, f32[8,128]{1,0:T(8,128)S(1)}, u32[]{:S(2)}, u32[]{:S(2)}) collective-permute-start(f32[8,128]{1,0:T(8,128)S(1)} %add_add_fusion.1), channel_id=1, source_target_pairs={{0,8},{4,12},{8,16},{12,20},{16,24},{20,28},{24,0},{28,4},{32,40},... | collective-permute-start | bytes 12296 | tf_op jit(solution)/shard_map/ppermute | solution.py:105
  111.1 3.0 %collective-permute-start.23 = (f32[8,128]{1,0:T(8,128)S(1)}, f32[8,128]{1,0:T(8,128)S(1)}, u32[]{:S(2)}, u32[]{:S(2)}) collective-permute-start(f32[8,128]{1,0:T(8,128)S(1)} %add_add_fusion), channel_id=1, source_target_pairs={{0,2},{1,3},{2,0},{3,1},{4,6},{5,7},{6,4},{7,5},{8,10},{9,11},{10,... | collective-permute-start | bytes 12296 | tf_op jit(solution)/shard_map/ppermute | solution.py:109
  114.5 2.3 %collective-permute-start.25 = (f32[8,128]{1,0:T(8,128)S(1)}, f32[8,128]{1,0:T(8,128)S(1)}, u32[]{:S(2)}, u32[]{:S(2)}) collective-permute-start(f32[8,128]{1,0:T(8,128)S(1)} %add_add_fusion), channel_id=1, source_target_pairs={{0,3},{1,0},{2,1},{3,2},{4,7},{5,4},{6,5},{7,6},{8,11},{9,8},{10,9... | collective-permute-start | bytes 12296 | tf_op jit(solution)/shard_map/ppermute | solution.py:109
  119.8 1.7 fusion.104
  121.6 2.6 %collective-permute-start.27 = (bf16[24,3072]{1,0:T(8,128)(2,1)S(1)}, bf16[24,3072]{1,0:T(8,128)(2,1)S(1)}, u32[]{:S(2)}, u32[]{:S(2)}) collective-permute-start(bf16[24,3072]{1,0:T(8,128)(2,1)S(1)} %get-tuple-element.150), channel_id=1, source_target_pairs={{0,16},{4,20},{8,24},{12,28},{16,0},{20,4},{24,8},{28,12},{32,48},... | collective-permute-start | bytes 442376 | tf_op jit(solution)/shard_map/ppermute | solution.py:105
  124.8 3.5 %collective-permute-start.30 = (bf16[24,3072]{1,0:T(8,128)(2,1)S(1)}, bf16[24,3072]{1,0:T(8,128)(2,1)S(1)}, u32[]{:S(2)}, u32[]{:S(2)}) collective-permute-start(bf16[24,3072]{1,0:T(8,128)(2,1)S(1)} %get-tuple-element.149), channel_id=1, source_target_pairs={{0,64},{4,68},{8,72},{12,76},{16,80},{20,84},{24,88},{28,92},{32,9... | collective-permute-start | bytes 442376 | tf_op jit(solution)/shard_map/ppermute | solution.py:105
  128.4 2.3 %collective-permute-start.31 = (bf16[24,3072]{1,0:T(8,128)(2,1)S(1)}, bf16[24,3072]{1,0:T(8,128)(2,1)S(1)}, u32[]{:S(2)}, u32[]{:S(2)}) collective-permute-start(bf16[24,3072]{1,0:T(8,128)(2,1)S(1)} %get-tuple-element.149), channel_id=1, source_target_pairs={{0,96},{4,100},{8,104},{12,108},{16,112},{20,116},{24,120},{28,124... | collective-permute-start | bytes 442376 | tf_op jit(solution)/shard_map/ppermute | solution.py:105
  130.7 2.0 %collective-permute-done.30 = bf16[24,3072]{1,0:T(8,128)(2,1)S(1)} collective-permute-done((bf16[24,3072]{1,0:T(8,128)(2,1)S(1)}, bf16[24,3072]{1,0:T(8,128)(2,1)S(1)}, u32[]{:S(2)}, u32[]{:S(2)}) %collective-permute-start.30) | collective-permute-done | bytes 147488 | tf_op jit(solution)/shard_map/ppermute | solution.py:105
  133.2 7.1 %collective-permute-start.36 = (bf16[4,24,3072]{2,1,0:T(8,128)(2,1)S(1)}, bf16[4,24,3072]{2,1,0:T(8,128)(2,1)S(1)}, u32[]{:S(2)}, u32[]{:S(2)}) collective-permute-start(bf16[4,24,3072]{2,1,0:T(8,128)(2,1)S(1)} %constant_dynamic-slice_fusion.6), channel_id=1, source_target_pairs={{0,4},{4,0},{8,12},{12,8},{16,20},{20,16},{24,28},{28,24},{32,36},... | collective-permute-start | bytes 1769480 | tf_op jit(solution)/shard_map/ppermute | solution.py:105
  141.4 2.8 %collective-permute-start.34 = (bf16[4,24,3072]{2,1,0:T(8,128)(2,1)S(1)}, bf16[4,24,3072]{2,1,0:T(8,128)(2,1)S(1)}, u32[]{:S(2)}, u32[]{:S(2)}) collective-permute-start(bf16[4,24,3072]{2,1,0:T(8,128)(2,1)S(1)} %constant_dynamic-slice_fusion.6), channel_id=1, source_target_pairs={{0,96},{4,100},{8,104},{12,108},{16,112},{20,116},{24,120},{28,124... | collective-permute-start | bytes 1769480 | tf_op jit(solution)/shard_map/ppermute | solution.py:105
  144.2 1.9 %collective-permute-start.35 = (bf16[4,24,3072]{2,1,0:T(8,128)(2,1)S(1)}, bf16[4,24,3072]{2,1,0:T(8,128)(2,1)S(1)}, u32[]{:S(2)}, u32[]{:S(2)}) collective-permute-start(bf16[4,24,3072]{2,1,0:T(8,128)(2,1)S(1)} %constant_dynamic-slice_fusion.5), channel_id=1, source_target_pairs={{0,24},{4,28},{8,0},{12,4},{16,8},{20,12},{24,16},{28,20},{32,56},... | collective-permute-start | bytes 1769480 | tf_op jit(solution)/shard_map/ppermute | solution.py:105
  146.1 1.4 select_dynamic-update-slice_fusion.5
  147.4 1.4 select_dynamic-update-slice_fusion.4
  148.8 7.4 %collective-permute-done.32 = bf16[4,24,3072]{2,1,0:T(8,128)(2,1)S(1)} collective-permute-done((bf16[4,24,3072]{2,1,0:T(8,128)(2,1)S(1)}, bf16[4,24,3072]{2,1,0:T(8,128)(2,1)S(1)}, u32[]{:S(2)}, u32[]{:S(2)}) %collective-permute-start.32) | collective-permute-done | bytes 589856 | tf_op jit(solution)/shard_map/ppermute | solution.py:105
  156.6 1.9 %collective-permute-done.35 = bf16[4,24,3072]{2,1,0:T(8,128)(2,1)S(1)} collective-permute-done((bf16[4,24,3072]{2,1,0:T(8,128)(2,1)S(1)}, bf16[4,24,3072]{2,1,0:T(8,128)(2,1)S(1)}, u32[]{:S(2)}, u32[]{:S(2)}) %collective-permute-start.35) | collective-permute-done | bytes 589856 | tf_op jit(solution)/shard_map/ppermute | solution.py:105
  158.4 1.5 collective-permute-start.42
  162.4 1.7 collective-permute-start.40
  164.1 2.5 %collective-permute-start.41 = (bf16[2,24,3072]{2,1,0:T(8,128)(2,1)S(1)}, bf16[2,24,3072]{2,1,0:T(8,128)(2,1)S(1)}, u32[]{:S(2)}, u32[]{:S(2)}) collective-permute-start(bf16[2,24,3072]{2,1,0:T(8,128)(2,1)S(1)} %slice.364), channel_id=1, source_target_pairs={{0,24},{4,28},{8,0},{12,4},{16,8},{20,12},{24,16},{28,20},{32,56},... | collective-permute-start | bytes 884744 | tf_op jit(solution)/shard_map/ppermute | solution.py:105
  166.6 1.4 select_dynamic-update-slice_fusion.3
  168.0 1.4 select_dynamic-update-slice_fusion.2
  169.3 1.4 select_dynamic-update-slice_fusion.1
  170.7 1.4 select_dynamic-update-slice_fusion
  172.1 1.7 collective-permute-start.46
  (196 shorter events, 33.1 us)
Async XLA Ops:
  4.4 11.2 %collective-permute-start.1 = (bf16[1024,1536]{1,0:T(8,128)(2,1)}, bf16[1024,1536]{1,0:T(8,128)(2,1)}, u32[]{:S(2)}, u32[]{:S(2)}) collective-permute-start(bf16[1024,1536]{1,0:T(8,128)(2,1)} %constant_dynamic-slice_fusion.13), channel_id=1, source_target_pairs={{0,4},{4,0},{8,12},{12,8},{16,20},{20,16},{24,28},{28,24},{32,36},... | collective-permute-start | bytes 9437192 | tf_op jit(solution)/shard_map/ppermute | solution.py:105
  9.7 17.1 %collective-permute-start.2 = (bf16[1024,1536]{1,0:T(8,128)(2,1)}, bf16[1024,1536]{1,0:T(8,128)(2,1)}, u32[]{:S(2)}, u32[]{:S(2)}) collective-permute-start(bf16[1024,1536]{1,0:T(8,128)(2,1)} %constant_dynamic-slice_fusion.12), channel_id=1, source_target_pairs={{0,4},{4,0},{8,12},{12,8},{16,20},{20,16},{24,28},{28,24},{32,36},... | collective-permute-start | bytes 9437192 | tf_op jit(solution)/shard_map/ppermute | solution.py:105
  9.7 5.9 %collective-permute-start = (bf16[1024,768]{1,0:T(8,128)(2,1)S(1)}, bf16[1024,768]{1,0:T(8,128)(2,1)S(1)}, u32[]{:S(2)}, u32[]{:S(2)}) collective-permute-start(bf16[1024,768]{1,0:T(8,128)(2,1)S(1)} %copy-done.2), channel_id=1, source_target_pairs={{0,4},{4,0},{8,12},{12,8},{16,20},{20,16},{24,28},{28,24},{32,36},... | collective-permute-start | bytes 4718600 | tf_op jit(solution)/shard_map/ppermute | solution.py:105
  26.8 19.8 %collective-permute-start.4 = (f16[200,1536]{1,0:T(8,128)(2,1)}, f16[200,1536]{1,0:T(8,128)(2,1)}, u32[]{:S(2)}, u32[]{:S(2)}) collective-permute-start(f16[200,1536]{1,0:T(8,128)(2,1)} %get-tuple-element.61), channel_id=1, source_target_pairs={{0,32},{4,36},{8,40},{12,44},{16,48},{20,52},{24,56},{28,60},{32,6... | collective-permute-start | bytes 1843208 | tf_op jit(solution)/shard_map/ppermute | solution.py:105
  28.1 21.7 %collective-permute-start.5 = (f16[200,1536]{1,0:T(8,128)(2,1)}, f16[200,1536]{1,0:T(8,128)(2,1)}, u32[]{:S(2)}, u32[]{:S(2)}) collective-permute-start(f16[200,1536]{1,0:T(8,128)(2,1)} %get-tuple-element.62), channel_id=1, source_target_pairs={{0,96},{4,100},{8,104},{12,108},{16,112},{20,116},{24,120},{28,124... | collective-permute-start | bytes 1843208 | tf_op jit(solution)/shard_map/ppermute | solution.py:105
  29.5 28.0 %collective-permute-start.3 = (f16[200,1536]{1,0:T(8,128)(2,1)}, f16[200,1536]{1,0:T(8,128)(2,1)S(1)}, u32[]{:S(2)}, u32[]{:S(2)}) collective-permute-start(f16[200,1536]{1,0:T(8,128)(2,1)} %get-tuple-element.60), channel_id=1, source_target_pairs={{0,64},{4,68},{8,72},{12,76},{16,80},{20,84},{24,88},{28,92},{32,9... | collective-permute-start | bytes 1843208 | tf_op jit(solution)/shard_map/ppermute | solution.py:105
  40.6 33.0 %collective-permute-start.9 = (f16[200,1536]{1,0:T(8,128)(2,1)}, f16[200,1536]{1,0:T(8,128)(2,1)S(1)}, u32[]{:S(2)}, u32[]{:S(2)}) collective-permute-start(f16[200,1536]{1,0:T(8,128)(2,1)} %get-tuple-element.117), channel_id=1, source_target_pairs={{0,16},{4,20},{8,24},{12,28},{16,0},{20,4},{24,8},{28,12},{32,48},... | collective-permute-start | bytes 1843208 | tf_op jit(solution)/shard_map/ppermute | solution.py:105
  44.2 29.0 %collective-permute-start.10 = (f16[200,1536]{1,0:T(8,128)(2,1)}, f16[200,1536]{1,0:T(8,128)(2,1)S(1)}, u32[]{:S(2)}, u32[]{:S(2)}) collective-permute-start(f16[200,1536]{1,0:T(8,128)(2,1)} %get-tuple-element.119), channel_id=1, source_target_pairs={{0,8},{4,12},{8,16},{12,20},{16,24},{20,28},{24,0},{28,4},{32,40},... | collective-permute-start | bytes 1843208 | tf_op jit(solution)/shard_map/ppermute | solution.py:105
  46.6 26.8 %collective-permute-start.11 = (f16[200,1536]{1,0:T(8,128)(2,1)}, f16[200,1536]{1,0:T(8,128)(2,1)S(1)}, u32[]{:S(2)}, u32[]{:S(2)}) collective-permute-start(f16[200,1536]{1,0:T(8,128)(2,1)} %get-tuple-element.118), channel_id=1, source_target_pairs={{0,24},{4,28},{8,0},{12,4},{16,8},{20,12},{24,16},{28,20},{32,56},... | collective-permute-start | bytes 1843208 | tf_op jit(solution)/shard_map/ppermute | solution.py:105
  63.1 15.3 %collective-permute-start.6 = (f32[56,1536]{1,0:T(8,128)}, f32[56,1536]{1,0:T(8,128)S(1)}, u32[]{:S(2)}, u32[]{:S(2)}) collective-permute-start(f32[56,1536]{1,0:T(8,128)} %get-tuple-element.129), channel_id=1, source_target_pairs={{0,16},{4,20},{8,24},{12,28},{16,0},{20,4},{24,8},{28,12},{32,48},... | collective-permute-start | bytes 1032200 | tf_op jit(solution)/shard_map/ppermute | solution.py:105
  66.7 19.9 %collective-permute-start.7 = (f32[56,1536]{1,0:T(8,128)}, f32[56,1536]{1,0:T(8,128)S(1)}, u32[]{:S(2)}, u32[]{:S(2)}) collective-permute-start(f32[56,1536]{1,0:T(8,128)} %get-tuple-element.130), channel_id=1, source_target_pairs={{0,8},{4,12},{8,16},{12,20},{16,24},{20,28},{24,0},{28,4},{32,40},... | collective-permute-start | bytes 1032200 | tf_op jit(solution)/shard_map/ppermute | solution.py:105
  73.2 13.4 %collective-permute-start.8 = (f32[56,1536]{1,0:T(8,128)}, f32[56,1536]{1,0:T(8,128)S(1)}, u32[]{:S(2)}, u32[]{:S(2)}) collective-permute-start(f32[56,1536]{1,0:T(8,128)} %get-tuple-element.127), channel_id=1, source_target_pairs={{0,24},{4,28},{8,0},{12,4},{16,8},{20,12},{24,16},{28,20},{32,56},... | collective-permute-start | bytes 1032200 | tf_op jit(solution)/shard_map/ppermute | solution.py:105
  76.8 10.0 %collective-permute-start.12 = (f32[56,1536]{1,0:T(8,128)S(1)}, f32[56,1536]{1,0:T(8,128)S(1)}, u32[]{:S(2)}, u32[]{:S(2)}) collective-permute-start(f32[56,1536]{1,0:T(8,128)S(1)} %get-tuple-element.126), channel_id=1, source_target_pairs={{0,64},{4,68},{8,72},{12,76},{16,80},{20,84},{24,88},{28,92},{32,9... | collective-permute-start | bytes 1032200 | tf_op jit(solution)/shard_map/ppermute | solution.py:105
  78.3 17.4 %collective-permute-start.13 = (f32[56,1536]{1,0:T(8,128)S(1)}, f32[56,1536]{1,0:T(8,128)S(1)}, u32[]{:S(2)}, u32[]{:S(2)}) collective-permute-start(f32[56,1536]{1,0:T(8,128)S(1)} %get-tuple-element.125), channel_id=1, source_target_pairs={{0,32},{4,36},{8,40},{12,44},{16,48},{20,52},{24,56},{28,60},{32,6... | collective-permute-start | bytes 1032200 | tf_op jit(solution)/shard_map/ppermute | solution.py:105
  78.3 17.4 %collective-permute-start.14 = (f32[56,1536]{1,0:T(8,128)S(1)}, f32[56,1536]{1,0:T(8,128)S(1)}, u32[]{:S(2)}, u32[]{:S(2)}) collective-permute-start(f32[56,1536]{1,0:T(8,128)S(1)} %get-tuple-element.124), channel_id=1, source_target_pairs={{0,96},{4,100},{8,104},{12,108},{16,112},{20,116},{24,120},{28,124... | collective-permute-start | bytes 1032200 | tf_op jit(solution)/shard_map/ppermute | solution.py:105
  97.4 5.6 %collective-permute-start.16 = (f32[8,128]{1,0:T(8,128)S(1)}, f32[8,128]{1,0:T(8,128)S(1)}, u32[]{:S(2)}, u32[]{:S(2)}) collective-permute-start(f32[8,128]{1,0:T(8,128)S(1)} %add.531), channel_id=1, source_target_pairs={{0,64},{4,68},{8,72},{12,76},{16,80},{20,84},{24,88},{28,92},{32,9... | collective-permute-start | bytes 12296 | tf_op jit(solution)/shard_map/ppermute | solution.py:105
  98.8 4.2 %collective-permute-start.17 = (f32[8,128]{1,0:T(8,128)S(1)}, f32[8,128]{1,0:T(8,128)S(1)}, u32[]{:S(2)}, u32[]{:S(2)}) collective-permute-start(f32[8,128]{1,0:T(8,128)S(1)} %add.531), channel_id=1, source_target_pairs={{0,32},{4,36},{8,40},{12,44},{16,48},{20,52},{24,56},{28,60},{32,6... | collective-permute-start | bytes 12296 | tf_op jit(solution)/shard_map/ppermute | solution.py:105
  98.8 4.2 %collective-permute-start.18 = (f32[8,128]{1,0:T(8,128)S(1)}, f32[8,128]{1,0:T(8,128)S(1)}, u32[]{:S(2)}, u32[]{:S(2)}) collective-permute-start(f32[8,128]{1,0:T(8,128)S(1)} %add.531), channel_id=1, source_target_pairs={{0,96},{4,100},{8,104},{12,108},{16,112},{20,116},{24,120},{28,124... | collective-permute-start | bytes 12296 | tf_op jit(solution)/shard_map/ppermute | solution.py:105
  101.8 7.6 %collective-permute-start.22 = (f32[32,3072]{1,0:T(8,128)S(1)}, f32[32,3072]{1,0:T(8,128)S(1)}, u32[]{:S(2)}, u32[]{:S(2)}) collective-permute-start(f32[32,3072]{1,0:T(8,128)S(1)} %select_maximum_fusion), channel_id=1, source_target_pairs={{0,4},{4,0},{8,12},{12,8},{16,20},{20,16},{24,28},{28,24},{32,36},... | collective-permute-start | bytes 1179656 | tf_op jit(solution)/shard_map/ppermute | solution.py:105
  103.0 4.2 %collective-permute-start.19 = (f32[8,128]{1,0:T(8,128)S(1)}, f32[8,128]{1,0:T(8,128)S(1)}, u32[]{:S(2)}, u32[]{:S(2)}) collective-permute-start(f32[8,128]{1,0:T(8,128)S(1)} %add_add_fusion.1), channel_id=1, source_target_pairs={{0,16},{4,20},{8,24},{12,28},{16,0},{20,4},{24,8},{28,12},{32,48},... | collective-permute-start | bytes 12296 | tf_op jit(solution)/shard_map/ppermute | solution.py:105
  104.4 3.7 %collective-permute-start.20 = (f32[8,128]{1,0:T(8,128)S(1)}, f32[8,128]{1,0:T(8,128)S(1)}, u32[]{:S(2)}, u32[]{:S(2)}) collective-permute-start(f32[8,128]{1,0:T(8,128)S(1)} %add_add_fusion.1), channel_id=1, source_target_pairs={{0,8},{4,12},{8,16},{12,20},{16,24},{20,28},{24,0},{28,4},{32,40},... | collective-permute-start | bytes 12296 | tf_op jit(solution)/shard_map/ppermute | solution.py:105
  106.9 2.5 %collective-permute-start.21 = (f32[8,128]{1,0:T(8,128)S(1)}, f32[8,128]{1,0:T(8,128)S(1)}, u32[]{:S(2)}, u32[]{:S(2)}) collective-permute-start(f32[8,128]{1,0:T(8,128)S(1)} %add_add_fusion.1), channel_id=1, source_target_pairs={{0,24},{4,28},{8,0},{12,4},{16,8},{20,12},{24,16},{28,20},{32,56},... | collective-permute-start | bytes 12296 | tf_op jit(solution)/shard_map/ppermute | solution.py:105
  111.1 5.7 %collective-permute-start.23 = (f32[8,128]{1,0:T(8,128)S(1)}, f32[8,128]{1,0:T(8,128)S(1)}, u32[]{:S(2)}, u32[]{:S(2)}) collective-permute-start(f32[8,128]{1,0:T(8,128)S(1)} %add_add_fusion), channel_id=1, source_target_pairs={{0,2},{1,3},{2,0},{3,1},{4,6},{5,7},{6,4},{7,5},{8,10},{9,11},{10,... | collective-permute-start | bytes 12296 | tf_op jit(solution)/shard_map/ppermute | solution.py:109
  114.1 3.7 %collective-permute-start.24 = (f32[8,128]{1,0:T(8,128)S(1)}, f32[8,128]{1,0:T(8,128)S(1)}, u32[]{:S(2)}, u32[]{:S(2)}) collective-permute-start(f32[8,128]{1,0:T(8,128)S(1)} %add_add_fusion), channel_id=1, source_target_pairs={{0,1},{1,2},{2,3},{3,0},{4,5},{5,6},{6,7},{7,4},{8,9},{9,10},{10,1... | collective-permute-start | bytes 12296 | tf_op jit(solution)/shard_map/ppermute | solution.py:109
  114.5 3.3 %collective-permute-start.25 = (f32[8,128]{1,0:T(8,128)S(1)}, f32[8,128]{1,0:T(8,128)S(1)}, u32[]{:S(2)}, u32[]{:S(2)}) collective-permute-start(f32[8,128]{1,0:T(8,128)S(1)} %add_add_fusion), channel_id=1, source_target_pairs={{0,3},{1,0},{2,1},{3,2},{4,7},{5,4},{6,5},{7,6},{8,11},{9,8},{10,9... | collective-permute-start | bytes 12296 | tf_op jit(solution)/shard_map/ppermute | solution.py:109
  121.5 6.9 %collective-permute-start.26 = (bf16[24,3072]{1,0:T(8,128)(2,1)S(1)}, bf16[24,3072]{1,0:T(8,128)(2,1)S(1)}, u32[]{:S(2)}, u32[]{:S(2)}) collective-permute-start(bf16[24,3072]{1,0:T(8,128)(2,1)S(1)} %get-tuple-element.150), channel_id=1, source_target_pairs={{0,8},{4,12},{8,16},{12,20},{16,24},{20,28},{24,0},{28,4},{32,40},... | collective-permute-start | bytes 442376 | tf_op jit(solution)/shard_map/ppermute | solution.py:105
  121.6 9.1 %collective-permute-start.27 = (bf16[24,3072]{1,0:T(8,128)(2,1)S(1)}, bf16[24,3072]{1,0:T(8,128)(2,1)S(1)}, u32[]{:S(2)}, u32[]{:S(2)}) collective-permute-start(bf16[24,3072]{1,0:T(8,128)(2,1)S(1)} %get-tuple-element.150), channel_id=1, source_target_pairs={{0,16},{4,20},{8,24},{12,28},{16,0},{20,4},{24,8},{28,12},{32,48},... | collective-permute-start | bytes 442376 | tf_op jit(solution)/shard_map/ppermute | solution.py:105
  124.1 6.6 %collective-permute-start.28 = (bf16[24,3072]{1,0:T(8,128)(2,1)S(1)}, bf16[24,3072]{1,0:T(8,128)(2,1)S(1)}, u32[]{:S(2)}, u32[]{:S(2)}) collective-permute-start(bf16[24,3072]{1,0:T(8,128)(2,1)S(1)} %get-tuple-element.150), channel_id=1, source_target_pairs={{0,24},{4,28},{8,0},{12,4},{16,8},{20,12},{24,16},{28,20},{32,56},... | collective-permute-start | bytes 442376 | tf_op jit(solution)/shard_map/ppermute | solution.py:105
  124.8 5.9 %collective-permute-start.29 = (bf16[24,3072]{1,0:T(8,128)(2,1)S(1)}, bf16[24,3072]{1,0:T(8,128)(2,1)S(1)}, u32[]{:S(2)}, u32[]{:S(2)}) collective-permute-start(bf16[24,3072]{1,0:T(8,128)(2,1)S(1)} %get-tuple-element.149), channel_id=1, source_target_pairs={{0,32},{4,36},{8,40},{12,44},{16,48},{20,52},{24,56},{28,60},{32,6... | collective-permute-start | bytes 442376 | tf_op jit(solution)/shard_map/ppermute | solution.py:105
  124.8 7.9 %collective-permute-start.30 = (bf16[24,3072]{1,0:T(8,128)(2,1)S(1)}, bf16[24,3072]{1,0:T(8,128)(2,1)S(1)}, u32[]{:S(2)}, u32[]{:S(2)}) collective-permute-start(bf16[24,3072]{1,0:T(8,128)(2,1)S(1)} %get-tuple-element.149), channel_id=1, source_target_pairs={{0,64},{4,68},{8,72},{12,76},{16,80},{20,84},{24,88},{28,92},{32,9... | collective-permute-start | bytes 442376 | tf_op jit(solution)/shard_map/ppermute | solution.py:105
  128.4 4.4 %collective-permute-start.31 = (bf16[24,3072]{1,0:T(8,128)(2,1)S(1)}, bf16[24,3072]{1,0:T(8,128)(2,1)S(1)}, u32[]{:S(2)}, u32[]{:S(2)}) collective-permute-start(bf16[24,3072]{1,0:T(8,128)(2,1)S(1)} %get-tuple-element.149), channel_id=1, source_target_pairs={{0,96},{4,100},{8,104},{12,108},{16,112},{20,116},{24,120},{28,124... | collective-permute-start | bytes 442376 | tf_op jit(solution)/shard_map/ppermute | solution.py:105
  133.2 11.0 %collective-permute-start.36 = (bf16[4,24,3072]{2,1,0:T(8,128)(2,1)S(1)}, bf16[4,24,3072]{2,1,0:T(8,128)(2,1)S(1)}, u32[]{:S(2)}, u32[]{:S(2)}) collective-permute-start(bf16[4,24,3072]{2,1,0:T(8,128)(2,1)S(1)} %constant_dynamic-slice_fusion.6), channel_id=1, source_target_pairs={{0,4},{4,0},{8,12},{12,8},{16,20},{20,16},{24,28},{28,24},{32,36},... | collective-permute-start | bytes 1769480 | tf_op jit(solution)/shard_map/ppermute | solution.py:105
  140.3 16.0 %collective-permute-start.32 = (bf16[4,24,3072]{2,1,0:T(8,128)(2,1)S(1)}, bf16[4,24,3072]{2,1,0:T(8,128)(2,1)S(1)}, u32[]{:S(2)}, u32[]{:S(2)}) collective-permute-start(bf16[4,24,3072]{2,1,0:T(8,128)(2,1)S(1)} %constant_dynamic-slice_fusion.6), channel_id=1, source_target_pairs={{0,32},{4,36},{8,40},{12,44},{16,48},{20,52},{24,56},{28,60},{32,6... | collective-permute-start | bytes 1769480 | tf_op jit(solution)/shard_map/ppermute | solution.py:105
  140.3 7.2 %collective-permute-start.37 = (bf16[4,24,3072]{2,1,0:T(8,128)(2,1)S(1)}, bf16[4,24,3072]{2,1,0:T(8,128)(2,1)S(1)}, u32[]{:S(2)}, u32[]{:S(2)}) collective-permute-start(bf16[4,24,3072]{2,1,0:T(8,128)(2,1)S(1)} %constant_dynamic-slice_fusion.5), channel_id=1, source_target_pairs={{0,4},{4,0},{8,12},{12,8},{16,20},{20,16},{24,28},{28,24},{32,36},... | collective-permute-start | bytes 1769480 | tf_op jit(solution)/shard_map/ppermute | solution.py:105
  140.6 15.9 %collective-permute-start.33 = (bf16[4,24,3072]{2,1,0:T(8,128)(2,1)S(1)}, bf16[4,24,3072]{2,1,0:T(8,128)(2,1)S(1)}, u32[]{:S(2)}, u32[]{:S(2)}) collective-permute-start(bf16[4,24,3072]{2,1,0:T(8,128)(2,1)S(1)} %constant_dynamic-slice_fusion.5), channel_id=1, source_target_pairs={{0,8},{4,12},{8,16},{12,20},{16,24},{20,28},{24,0},{28,4},{32,40},... | collective-permute-start | bytes 1769480 | tf_op jit(solution)/shard_map/ppermute | solution.py:105
  141.4 15.2 %collective-permute-start.34 = (bf16[4,24,3072]{2,1,0:T(8,128)(2,1)S(1)}, bf16[4,24,3072]{2,1,0:T(8,128)(2,1)S(1)}, u32[]{:S(2)}, u32[]{:S(2)}) collective-permute-start(bf16[4,24,3072]{2,1,0:T(8,128)(2,1)S(1)} %constant_dynamic-slice_fusion.6), channel_id=1, source_target_pairs={{0,96},{4,100},{8,104},{12,108},{16,112},{20,116},{24,120},{28,124... | collective-permute-start | bytes 1769480 | tf_op jit(solution)/shard_map/ppermute | solution.py:105
  144.2 14.3 %collective-permute-start.35 = (bf16[4,24,3072]{2,1,0:T(8,128)(2,1)S(1)}, bf16[4,24,3072]{2,1,0:T(8,128)(2,1)S(1)}, u32[]{:S(2)}, u32[]{:S(2)}) collective-permute-start(bf16[4,24,3072]{2,1,0:T(8,128)(2,1)S(1)} %constant_dynamic-slice_fusion.5), channel_id=1, source_target_pairs={{0,24},{4,28},{8,0},{12,4},{16,8},{20,12},{24,16},{28,20},{32,56},... | collective-permute-start | bytes 1769480 | tf_op jit(solution)/shard_map/ppermute | solution.py:105
  158.4 3.1 %collective-permute-start.42 = (bf16[4,24,3072]{2,1,0:T(8,128)(2,1)S(1)}, bf16[4,24,3072]{2,1,0:T(8,128)(2,1)S(1)}, u32[]{:S(2)}, u32[]{:S(2)}) collective-permute-start(bf16[4,24,3072]{2,1,0:T(8,128)(2,1)S(1)} %collective-permute-done.32), channel_id=1, source_target_pairs={{0,4},{4,0},{8,12},{12,8},{16,20},{20,16},{24,28},{28,24},{32,36},... | collective-permute-start | bytes 1769480 | tf_op jit(solution)/shard_map/ppermute | solution.py:105
  159.9 2.5 %collective-permute-start.43 = (bf16[4,24,3072]{2,1,0:T(8,128)(2,1)S(1)}, bf16[4,24,3072]{2,1,0:T(8,128)(2,1)S(1)}, u32[]{:S(2)}, u32[]{:S(2)}) collective-permute-start(bf16[4,24,3072]{2,1,0:T(8,128)(2,1)S(1)} %collective-permute-done.33), channel_id=1, source_target_pairs={{0,4},{4,0},{8,12},{12,8},{16,20},{20,16},{24,28},{28,24},{32,36},... | collective-permute-start | bytes 1769480 | tf_op jit(solution)/shard_map/ppermute | solution.py:105
  159.9 4.2 %collective-permute-start.44 = (bf16[4,24,3072]{2,1,0:T(8,128)(2,1)S(1)}, bf16[4,24,3072]{2,1,0:T(8,128)(2,1)S(1)}, u32[]{:S(2)}, u32[]{:S(2)}) collective-permute-start(bf16[4,24,3072]{2,1,0:T(8,128)(2,1)S(1)} %collective-permute-done.34), channel_id=1, source_target_pairs={{0,4},{4,0},{8,12},{12,8},{16,20},{20,16},{24,28},{28,24},{32,36},... | collective-permute-start | bytes 1769480 | tf_op jit(solution)/shard_map/ppermute | solution.py:105
  160.4 6.2 %collective-permute-start.45 = (bf16[4,24,3072]{2,1,0:T(8,128)(2,1)S(1)}, bf16[4,24,3072]{2,1,0:T(8,128)(2,1)S(1)}, u32[]{:S(2)}, u32[]{:S(2)}) collective-permute-start(bf16[4,24,3072]{2,1,0:T(8,128)(2,1)S(1)} %collective-permute-done.35), channel_id=1, source_target_pairs={{0,4},{4,0},{8,12},{12,8},{16,20},{20,16},{24,28},{28,24},{32,36},... | collective-permute-start | bytes 1769480 | tf_op jit(solution)/shard_map/ppermute | solution.py:105
  160.6 11.4 %collective-permute-start.38 = (bf16[2,24,3072]{2,1,0:T(8,128)(2,1)S(1)}, bf16[2,24,3072]{2,1,0:T(8,128)(2,1)S(1)}, u32[]{:S(2)}, u32[]{:S(2)}) collective-permute-start(bf16[2,24,3072]{2,1,0:T(8,128)(2,1)S(1)} %slice.361), channel_id=1, source_target_pairs={{0,32},{4,36},{8,40},{12,44},{16,48},{20,52},{24,56},{28,60},{32,6... | collective-permute-start | bytes 884744 | tf_op jit(solution)/shard_map/ppermute | solution.py:105
  161.5 10.5 %collective-permute-start.39 = (bf16[2,24,3072]{2,1,0:T(8,128)(2,1)S(1)}, bf16[2,24,3072]{2,1,0:T(8,128)(2,1)S(1)}, u32[]{:S(2)}, u32[]{:S(2)}) collective-permute-start(bf16[2,24,3072]{2,1,0:T(8,128)(2,1)S(1)} %slice.362), channel_id=1, source_target_pairs={{0,8},{4,12},{8,16},{12,20},{16,24},{20,28},{24,0},{28,4},{32,40},... | collective-permute-start | bytes 884744 | tf_op jit(solution)/shard_map/ppermute | solution.py:105
  162.4 9.7 %collective-permute-start.40 = (bf16[2,24,3072]{2,1,0:T(8,128)(2,1)S(1)}, bf16[2,24,3072]{2,1,0:T(8,128)(2,1)S(1)}, u32[]{:S(2)}, u32[]{:S(2)}) collective-permute-start(bf16[2,24,3072]{2,1,0:T(8,128)(2,1)S(1)} %slice.363), channel_id=1, source_target_pairs={{0,96},{4,100},{8,104},{12,108},{16,112},{20,116},{24,120},{28,124... | collective-permute-start | bytes 884744 | tf_op jit(solution)/shard_map/ppermute | solution.py:105
  164.1 8.0 %collective-permute-start.41 = (bf16[2,24,3072]{2,1,0:T(8,128)(2,1)S(1)}, bf16[2,24,3072]{2,1,0:T(8,128)(2,1)S(1)}, u32[]{:S(2)}, u32[]{:S(2)}) collective-permute-start(bf16[2,24,3072]{2,1,0:T(8,128)(2,1)S(1)} %slice.364), channel_id=1, source_target_pairs={{0,24},{4,28},{8,0},{12,4},{16,8},{20,12},{24,16},{28,20},{32,56},... | collective-permute-start | bytes 884744 | tf_op jit(solution)/shard_map/ppermute | solution.py:105
  172.1 3.5 %collective-permute-start.46 = (bf16[2,24,3072]{2,1,0:T(8,128)(2,1)S(1)}, bf16[2,24,3072]{2,1,0:T(8,128)(2,1)S(1)}, u32[]{:S(2)}, u32[]{:S(2)}) collective-permute-start(bf16[2,24,3072]{2,1,0:T(8,128)(2,1)S(1)} %collective-permute-done.38), channel_id=1, source_target_pairs={{0,4},{4,0},{8,12},{12,8},{16,20},{20,16},{24,28},{28,24},{32,36},... | collective-permute-start | bytes 884744 | tf_op jit(solution)/shard_map/ppermute | solution.py:105
  175.1 2.6 %collective-permute-start.48 = (bf16[2,24,3072]{2,1,0:T(8,128)(2,1)S(1)}, bf16[2,24,3072]{2,1,0:T(8,128)(2,1)S(1)}, u32[]{:S(2)}, u32[]{:S(2)}) collective-permute-start(bf16[2,24,3072]{2,1,0:T(8,128)(2,1)S(1)} %collective-permute-done.40), channel_id=1, source_target_pairs={{0,4},{4,0},{8,12},{12,8},{16,20},{20,16},{24,28},{28,24},{32,36},... | collective-permute-start | bytes 884744 | tf_op jit(solution)/shard_map/ppermute | solution.py:105
  175.6 3.1 %collective-permute-start.49 = (bf16[2,24,3072]{2,1,0:T(8,128)(2,1)S(1)}, bf16[2,24,3072]{2,1,0:T(8,128)(2,1)S(1)}, u32[]{:S(2)}, u32[]{:S(2)}) collective-permute-start(bf16[2,24,3072]{2,1,0:T(8,128)(2,1)S(1)} %collective-permute-done.41), channel_id=1, source_target_pairs={{0,4},{4,0},{8,12},{12,8},{16,20},{20,16},{24,28},{28,24},{32,36},... | collective-permute-start | bytes 884744 | tf_op jit(solution)/shard_map/ppermute | solution.py:105
  (13 other events, 71.9 us)
